TPU v7x, 32 devices: a whole 2x2x4 slice. The times are simulated.
32 devices in a mesh: groups: 2 (over y), rows: 4 (over z), cols: 2 (over x), section: 2 (over core).
Axes of the slice: x: 2, y: 2, z: 4, core: 2. Of those that a mesh axis runs over, the one named last changes fastest.
Arguments:
- state: float32 [2, 64, 512], P(None, ('groups', 'rows'), ('cols', 'section')), parts along dimension 1, may hold values from -6 to 6
- cotangent: float32 [2, 64, 512], P(None, ('groups', 'rows'), ('cols', 'section')), parts along dimension 1, may hold values from -6 to 6
- first_weight: bfloat16 [64, 18], replicated, may hold values from -1.5 to 1.5
- second_weight: bfloat16 [64, 64], replicated, may hold values from -0.75 to 0.75
- third_weight: bfloat16 [32, 64], replicated, may hold values from -0.75 to 0.75
Outputs:
- velocity: float32 [2, 64, 512], P(None, ('groups', 'rows'), ('cols', 'section')), parts along dimension 1
- grad_first: float32 [128, 18], P('groups'), parts along dimension 0
- grad_second: float32 [128, 64], P('groups'), parts along dimension 0
- grad_third: float32 [64, 64], P('groups'), parts along dimension 0
There are 2 independent parts, one for each index of `groups`. A program takes and returns all parts, laid end to end along the dimension named above; an argument that names none is the same for every part. Nothing has to cross between parts.
All inputs are finite; a program needn't handle non-finite values.
Results may differ from a plain program's by a relative error of at most 0.0045.
Values sent between devices are 32-bit elements; how exact they have to be, the bound alone decides.
No kernel may reach another device: no remote copies, remote signals or barrier semaphores. Data moves between devices by JAX's collectives and lax.ppermute only.
A program may use at most 64 MiB of HBM per device.

v0:
```python
import math

import jax
import jax.numpy as jnp
from jax import lax
from jax.sharding import PartitionSpec as P

STEPS = 4
SWEEPS = 3


time_step = 0.1
viscosity = 0.2
correction_gain = 0.25
gradient_gain = 10.0


def with_halo(block, sides, width):
    for axis, dim in sides:
        count = lax.axis_size(axis)
        forward = [(i, i + 1) for i in range(count - 1)]
        forward.append((count - 1, 0))
        backward = [(target, source) for source, target in forward]
        low = lax.ppermute(
            lax.slice_in_dim(block, block.shape[dim] - width, None, axis=dim), axis, forward
        )
        high = lax.ppermute(lax.slice_in_dim(block, 0, width, axis=dim), axis, backward)
        block = jnp.concatenate([low, block, high], axis=dim)
    return block


def base_table():
    return jnp.array(
        [
            [0.5 if tap_number in (5, 9) else 0.0 for tap_number in range(16)],
            [0.5 if tap_number in (5, 6) else 0.0 for tap_number in range(16)],
        ],
        jnp.float32,
    )


def patches(extended):
    height = extended.shape[1] - 3
    breadth = extended.shape[2] - 3
    pieces = [
        extended[:, offset_row : offset_row + height, offset_col : offset_col + breadth]
        for offset_row in range(3)
        for offset_col in range(3)
    ]
    return jnp.stack(pieces, 1).reshape(18, height * breadth)


def network(inputs, first_weight, second_weight, third_weight):
    rounded = inputs.astype(jnp.bfloat16)
    first_pre = jnp.dot(first_weight, rounded, preferred_element_type=jnp.float32)
    first_act = jax.nn.gelu(first_pre).astype(jnp.bfloat16)
    second_pre = jnp.dot(second_weight, first_act, preferred_element_type=jnp.float32)
    second_act = jax.nn.gelu(second_pre).astype(jnp.bfloat16)
    coefficients = jnp.dot(third_weight, second_act, preferred_element_type=jnp.float32)
    return (rounded, first_pre, first_act, second_pre, second_act, coefficients)


def physics(extended, coefficients):
    height = extended.shape[1] - 3
    breadth = extended.shape[2] - 3
    inner_rows = height - 1
    inner_cols = breadth - 1
    raw_output = coefficients.reshape(2, 16, height, breadth)
    weights = base_table()[:, :, None, None] + correction_gain * (
        raw_output - jnp.mean(raw_output, axis=1, keepdims=True)
    )
    stencil = jnp.stack(
        [
            extended[:, offset_row : offset_row + height, offset_col : offset_col + breadth]
            for offset_row in range(4)
            for offset_col in range(4)
        ],
        0,
    )
    face_rows = jnp.sum(weights[0][:, None] * stencil, axis=0)
    face_cols = jnp.sum(weights[1][:, None] * stencil, axis=0)
    speed_rows = 0.5 * (
        extended[0, 1 : 1 + height, 1 : 1 + breadth] + extended[0, 2 : 2 + height, 1 : 1 + breadth]
    )
    speed_cols = 0.5 * (
        extended[1, 1 : 1 + height, 1 : 1 + breadth] + extended[1, 1 : 1 + height, 2 : 2 + breadth]
    )
    flux_rows = speed_rows * face_rows
    flux_cols = speed_cols * face_cols
    transport = (
        flux_rows[:, 1:, 1:] - flux_rows[:, :-1, 1:] + flux_cols[:, 1:, 1:] - flux_cols[:, 1:, :-1]
    )
    centre = extended[:, 2 : 2 + inner_rows, 2 : 2 + inner_cols]
    laplace = (
        extended[:, 1 : 1 + inner_rows, 2 : 2 + inner_cols]
        + extended[:, 3 : 3 + inner_rows, 2 : 2 + inner_cols]
        + extended[:, 2 : 2 + inner_rows, 1 : 1 + inner_cols]
        + extended[:, 2 : 2 + inner_rows, 3 : 3 + inner_cols]
        - 4.0 * centre
    )
    return centre - time_step * transport + time_step * viscosity * laplace


def advance(extended, first_weight, second_weight, third_weight):
    outputs = network(patches(extended), first_weight, second_weight, third_weight)
    return physics(extended, outputs[5])


def gelu_back(preact, upstream):
    return jax.vjp(jax.nn.gelu, preact)[1](upstream)[0]


def advance_back(extended, first_weight, second_weight, third_weight, upstream):
    inputs, patch_back = jax.vjp(patches, extended)
    rounded, first_pre, first_act, second_pre, second_act, coefficients = network(
        inputs, first_weight, second_weight, third_weight
    )
    advanced, physics_back = jax.vjp(physics, extended, coefficients)
    extended_grad, coef_grad = physics_back(upstream)
    coef_round = coef_grad.astype(jnp.bfloat16)
    outer = (((1,), (1,)), ((), ()))
    inner = (((0,), (0,)), ((), ()))
    third_grad = lax.dot_general(coef_round, second_act, outer, preferred_element_type=jnp.float32)
    second_back = gelu_back(
        second_pre,
        lax.dot_general(third_weight, coef_round, inner, preferred_element_type=jnp.float32),
    ).astype(jnp.bfloat16)
    second_grad = lax.dot_general(second_back, first_act, outer, preferred_element_type=jnp.float32)
    first_back = gelu_back(
        first_pre,
        lax.dot_general(second_weight, second_back, inner, preferred_element_type=jnp.float32),
    ).astype(jnp.bfloat16)
    first_grad = lax.dot_general(first_back, rounded, outer, preferred_element_type=jnp.float32)
    input_grad = lax.dot_general(
        first_weight, first_back, inner, preferred_element_type=jnp.float32
    )
    extended_grad = extended_grad + patch_back(input_grad)[0]
    return (extended_grad, (first_grad, second_grad, third_grad))


def divergence(padded):
    return 0.5 * (
        padded[0, 2:, 1:-1] - padded[0, :-2, 1:-1] + (padded[1, 1:-1, 2:] - padded[1, 1:-1, :-2])
    )


def neighbours(padded):
    return padded[2:, 1:-1] + padded[:-2, 1:-1] + padded[1:-1, 2:] + padded[1:-1, :-2]


def pressure_gradient(padded):
    return jnp.stack(
        [0.5 * (padded[2:, 1:-1] - padded[:-2, 1:-1]), 0.5 * (padded[1:-1, 2:] - padded[1:-1, :-2])]
    )


def fold_rims(returned, margin):
    row_count = returned.shape[-2] - 4 * margin
    col_count = returned.shape[-1] - 4 * margin
    leading = [(0, 0)] * (returned.ndim - 1)
    middle = (
        returned[..., 2 * margin : 2 * margin + col_count]
        + jnp.pad(returned[..., :margin], leading + [(0, col_count - margin)])
        + jnp.pad(returned[..., -margin:], leading + [(col_count - margin, 0)])
    )
    leading_rows = [(0, 0)] * (returned.ndim - 2)
    return (
        middle[..., 2 * margin : 2 * margin + row_count, :]
        + jnp.pad(middle[..., :margin, :], leading_rows + [(0, row_count - margin), (0, 0)])
        + jnp.pad(middle[..., -margin:, :], leading_rows + [(row_count - margin, 0), (0, 0)])
    )


def shards(state, cotangent, first_weight, second_weight, third_weight):
    weights = (first_weight, second_weight, third_weight)
    current = state
    saved = []
    for step_number in range(STEPS):
        extended = with_halo(current, (("rows", 1), (("cols", "section"), 2)), 2)
        moved = advance(extended, *weights)
        velocity_pad = with_halo(moved, (("rows", 1), (("cols", "section"), 2)), 1)
        source = divergence(velocity_pad)
        pressure = -0.25 * source
        pressure_pads = []
        for sweep_number in range(SWEEPS):
            padded = with_halo(pressure, (("rows", 0), (("cols", "section"), 1)), 1)
            pressure_pads.append(padded)
            if sweep_number < SWEEPS - 1:
                pressure = 0.25 * (neighbours(padded) - source)
        saved.append((extended, velocity_pad, pressure_pads))
        current = moved - pressure_gradient(pressure_pads[-1])
    upstream = cotangent
    totals = (
        jnp.zeros(first_weight.shape, jnp.float32),
        jnp.zeros(second_weight.shape, jnp.float32),
        jnp.zeros(third_weight.shape, jnp.float32),
    )
    for step_number in reversed(range(STEPS)):
        record = saved[step_number]
        velocity_pad = record[1]
        pressure_pads = record[2]
        pad_grad = jax.vjp(pressure_gradient, pressure_pads[-1])[1](-upstream)[0]
        source_grad = jnp.zeros_like(upstream[0])
        for sweep_number in reversed(range(SWEEPS)):
            returned = with_halo(pad_grad, (("rows", 0), (("cols", "section"), 1)), 1)
            pressure_grad = fold_rims(returned, 1)
            source_grad = source_grad - 0.25 * pressure_grad
            if sweep_number > 0:
                pad_grad = jax.vjp(neighbours, pressure_pads[sweep_number - 1])[1](
                    0.25 * pressure_grad
                )[0]
        velocity_grad = jax.vjp(divergence, velocity_pad)[1](source_grad)[0]
        returned_velocity = with_halo(velocity_grad, (("rows", 1), (("cols", "section"), 2)), 1)
        moved_grad = upstream + fold_rims(returned_velocity, 1)
        extended_grad, grads = advance_back(
            record[0], first_weight, second_weight, third_weight, moved_grad
        )
        totals = (totals[0] + grads[0], totals[1] + grads[1], totals[2] + grads[2])
        if step_number > 0:
            returned_state = with_halo(extended_grad, (("rows", 1), (("cols", "section"), 2)), 2)
            upstream = fold_rims(returned_state, 2)
    totals = lax.psum((totals[0], totals[1], totals[2]), ("rows", "cols", "section"))
    cell_total = (
        state.shape[1] * state.shape[2] * lax.axis_size("rows") * lax.axis_size(("cols", "section"))
    )
    factor = gradient_gain / math.sqrt(cell_total)
    return (current, totals[0] * factor, totals[1] * factor, totals[2] * factor)


def solution(mesh):
    return jax.shard_map(
        shards,
        mesh=mesh,
        in_specs=(
            P(None, ("groups", "rows"), ("cols", "section")),
            P(None, ("groups", "rows"), ("cols", "section")),
            P(),
            P(),
            P(),
        ),
        out_specs=(
            P(None, ("groups", "rows"), ("cols", "section")),
            P("groups", None),
            P("groups", None),
            P("groups", None),
        ),
        check_vma=False,
    )
```

profile of v0, /device:TPU:0, one launch (start us, length us, event | category | flops | bytes accessed | tf_op | source)
XLA Modules:
  0.0 427.2 jit_solution(9308077185225650938)
XLA Ops:
  1.4 3.1 collective-permute-start.80
  4.5 2.1 collective-permute-start.81
  6.6 3.8 collective-permute-start.1
  23.4 3.8 collective-permute-start.4
  27.2 3.8 collective-permute-start.85
  35.0 3.8 collective-permute-start.8
  41.8 1.8 collective-permute-done.11
  43.7 3.9 collective-permute-start.12
  50.9 1.8 collective-permute-done.15
  53.5 3.1 collective-permute-start.16
  59.6 1.8 collective-permute-done.19
  62.5 3.0 collective-permute-start.21
  75.8 2.8 collective-permute-start.24
  78.6 3.8 collective-permute-start.89
  86.7 3.8 collective-permute-start.28
  93.5 1.8 collective-permute-done.31
  95.4 3.9 collective-permute-start.32
  102.6 1.8 collective-permute-done.35
  105.2 3.2 collective-permute-start.36
  111.4 1.8 collective-permute-done.39
  114.1 3.1 collective-permute-start.41
  128.1 3.0 collective-permute-start.44
  131.2 3.8 collective-permute-start.93
  137.4 1.9 collective-permute-done.47
  139.4 3.8 collective-permute-start.48
  148.1 3.9 collective-permute-start.52
  157.9 3.1 collective-permute-start.56
  166.9 2.9 collective-permute-start.61
  192.5 2.8 collective-permute-start.64
  203.0 3.8 collective-permute-start.68
  206.9 3.8 collective-permute-start.97
  216.5 3.9 collective-permute-start.101
  220.4 3.8 collective-permute-start.72
  228.4 3.8 collective-permute-start.105
  237.3 3.9 collective-permute-start.109
  247.3 2.8 collective-permute-start.113
  263.0 2.7 collective-permute-start.117
  270.3 2.6 collective-permute-start.76
  273.9 3.8 collective-permute-start.121
  282.7 3.9 collective-permute-start.125
  292.7 2.8 collective-permute-start.129
  301.8 2.7 collective-permute-start.133
  315.1 2.7 collective-permute-start.137
  324.2 2.7 collective-permute-start.141
  333.2 2.7 collective-permute-start.145
  342.1 2.7 collective-permute-start.149
  351.1 2.7 collective-permute-start.153
  362.8 62.7 %all-reduce.243 = (f32[64,18]{0,1:T(8,128)S(1)}, f32[64,64]{1,0:T(8,128)S(1)}, f32[32,64]{1,0:T(8,128)S(1)}) all-reduce(f32[64,18]{0,1:T(8,128)S(1)} %convolution_add_fusion.6, f32[64,64]{1,0:T(8,128)S(1)} %convolution_add_fusion, ...), channel_id=1, replica_groups=mesh['groups'=2,'rows'=4,'cols'=2,'section'=2] {'rows','cols','section'}, use_global_device_ids=true, to_apply=%region_36.37 | all-reduce | flops 7296 | bytes 58368 | tf_op jit(solution)/shard_map/psum | solution.py:222
  (871 shorter events, 217.4 us)
Async XLA Ops:
  1.4 9.0 %collective-permute-start.80 = (f32[1,130]{1,0:T(1,128)S(1)}, f32[1,130]{1,0:T(1,128)S(1)}, u32[]{:S(2)}, u32[]{:S(2)}) collective-permute-start(f32[1,130]{1,0:T(1,128)S(1)} %get-tuple-element.233), channel_id=1, source_target_pairs={{0,4},{4,8},{8,12},{12,0},{1,5},{5,9},{9,13},{13,1},{2,6},{6,10},{... | collective-permute-start | bytes 1568 | tf_op jit(solution)/shard_map/ppermute | solution.py:24
  4.5 5.9 %collective-permute-start.81 = (f32[1,130]{1,0:T(1,128)S(1)}, f32[1,130]{1,0:T(1,128)S(1)}, u32[]{:S(2)}, u32[]{:S(2)}) collective-permute-start(f32[1,130]{1,0:T(1,128)S(1)} %get-tuple-element.234), channel_id=1, source_target_pairs={{4,0},{8,4},{12,8},{0,12},{5,1},{9,5},{13,9},{1,13},{6,2},{10,6},{... | collective-permute-start | bytes 1568 | tf_op jit(solution)/shard_map/ppermute | solution.py:27
  6.6 7.8 %collective-permute-start = (f32[2,2,128]{2,1,0:T(2,128)S(1)}, f32[2,2,128]{2,1,0:T(2,128)S(1)}, u32[]{:S(2)}, u32[]{:S(2)}) collective-permute-start(f32[2,2,128]{2,1,0:T(2,128)S(1)} %get-tuple-element.320), channel_id=1, source_target_pairs={{0,4},{4,8},{8,12},{12,0},{1,5},{5,9},{9,13},{13,1},{2,6},{6,10},{... | collective-permute-start | bytes 6152 | tf_op jit(solution)/shard_map/ppermute | solution.py:24
  6.6 7.8 %collective-permute-start.1 = (f32[2,2,128]{2,1,0:T(2,128)S(1)}, f32[2,2,128]{2,1,0:T(2,128)S(1)}, u32[]{:S(2)}, u32[]{:S(2)}) collective-permute-start(f32[2,2,128]{2,1,0:T(2,128)S(1)} %get-tuple-element.321), channel_id=1, source_target_pairs={{4,0},{8,4},{12,8},{0,12},{5,1},{9,5},{13,9},{1,13},{6,2},{10,6},{... | collective-permute-start | bytes 6152 | tf_op jit(solution)/shard_map/ppermute | solution.py:27
  23.3 7.7 %collective-permute-start.5 = (f32[2,1,128]{2,1,0:T(1,128)S(1)}, f32[2,1,128]{2,1,0:T(1,128)S(1)}, u32[]{:S(2)}, u32[]{:S(2)}) collective-permute-start(f32[2,1,128]{2,1,0:T(1,128)S(1)} %get-tuple-element.318), channel_id=1, source_target_pairs={{0,4},{4,8},{8,12},{12,0},{1,5},{5,9},{9,13},{13,1},{2,6},{6,10},{... | collective-permute-start | bytes 3080 | tf_op jit(solution)/shard_map/ppermute | solution.py:24
  23.4 7.6 %collective-permute-start.4 = (f32[2,1,128]{2,1,0:T(1,128)S(1)}, f32[2,1,128]{2,1,0:T(1,128)S(1)}, u32[]{:S(2)}, u32[]{:S(2)}) collective-permute-start(f32[2,1,128]{2,1,0:T(1,128)S(1)} %get-tuple-element.319), channel_id=1, source_target_pairs={{4,0},{8,4},{12,8},{0,12},{5,1},{9,5},{13,9},{1,13},{6,2},{10,6},{... | collective-permute-start | bytes 3080 | tf_op jit(solution)/shard_map/ppermute | solution.py:27
  27.2 11.7 %collective-permute-start.84 = (f32[1,130]{1,0:T(1,128)S(1)}, f32[1,130]{1,0:T(1,128)S(1)}, u32[]{:S(2)}, u32[]{:S(2)}) collective-permute-start(f32[1,130]{1,0:T(1,128)S(1)} %get-tuple-element.229), channel_id=1, source_target_pairs={{0,4},{4,8},{8,12},{12,0},{1,5},{5,9},{9,13},{13,1},{2,6},{6,10},{... | collective-permute-start | bytes 1568 | tf_op jit(solution)/shard_map/ppermute | solution.py:24
  27.2 11.7 %collective-permute-start.85 = (f32[1,130]{1,0:T(1,128)S(1)}, f32[1,130]{1,0:T(1,128)S(1)}, u32[]{:S(2)}, u32[]{:S(2)}) collective-permute-start(f32[1,130]{1,0:T(1,128)S(1)} %get-tuple-element.230), channel_id=1, source_target_pairs={{4,0},{8,4},{12,8},{0,12},{5,1},{9,5},{13,9},{1,13},{6,2},{10,6},{... | collective-permute-start | bytes 1568 | tf_op jit(solution)/shard_map/ppermute | solution.py:27
  43.7 5.8 %collective-permute-start.13 = (f32[1,128]{1,0:T(1,128)S(1)}, f32[1,128]{1,0:T(1,128)S(1)}, u32[]{:S(2)}, u32[]{:S(2)}) collective-permute-start(f32[1,128]{1,0:T(1,128)S(1)} %get-tuple-element.350), channel_id=1, source_target_pairs={{0,4},{4,8},{8,12},{12,0},{1,5},{5,9},{9,13},{13,1},{2,6},{6,10},{... | collective-permute-start | bytes 1544 | tf_op jit(solution)/shard_map/ppermute | solution.py:24
  43.7 5.7 %collective-permute-start.12 = (f32[1,128]{1,0:T(1,128)S(1)}, f32[1,128]{1,0:T(1,128)S(1)}, u32[]{:S(2)}, u32[]{:S(2)}) collective-permute-start(f32[1,128]{1,0:T(1,128)S(1)} %get-tuple-element.351), channel_id=1, source_target_pairs={{4,0},{8,4},{12,8},{0,12},{5,1},{9,5},{13,9},{1,13},{6,2},{10,6},{... | collective-permute-start | bytes 1544 | tf_op jit(solution)/shard_map/ppermute | solution.py:27
  47.7 9.0 %collective-permute-start.86 = (f32[12,1]{1,0:T(8,128)S(1)}, f32[12,1]{1,0:T(8,128)S(1)}, u32[]{:S(2)}, u32[]{:S(2)}) collective-permute-start(f32[12,1]{1,0:T(8,128)S(1)} %get-tuple-element.227), channel_id=1, source_target_pairs={{0,1},{1,2},{2,3},{3,0},{4,5},{5,6},{6,7},{7,4},{8,9},{9,10},{10,1... | collective-permute-start | bytes 152 | tf_op jit(solution)/shard_map/ppermute | solution.py:24
  47.7 9.0 %collective-permute-start.87 = (f32[12,1]{1,0:T(8,128)S(1)}, f32[12,1]{1,0:T(8,128)S(1)}, u32[]{:S(2)}, u32[]{:S(2)}) collective-permute-start(f32[12,1]{1,0:T(8,128)S(1)} %get-tuple-element.228), channel_id=1, source_target_pairs={{1,0},{2,1},{3,2},{0,3},{5,4},{6,5},{7,6},{4,7},{9,8},{10,9},{11,1... | collective-permute-start | bytes 152 | tf_op jit(solution)/shard_map/ppermute | solution.py:27
  74.6 7.8 %collective-permute-start.25 = (f32[2,1,128]{2,1,0:T(1,128)S(1)}, f32[2,1,128]{2,1,0:T(1,128)S(1)}, u32[]{:S(2)}, u32[]{:S(2)}) collective-permute-start(f32[2,1,128]{2,1,0:T(1,128)S(1)} %get-tuple-element.308), channel_id=1, source_target_pairs={{0,4},{4,8},{8,12},{12,0},{1,5},{5,9},{9,13},{13,1},{2,6},{6,10},{... | collective-permute-start | bytes 3080 | tf_op jit(solution)/shard_map/ppermute | solution.py:24
  75.8 6.7 %collective-permute-start.24 = (f32[2,1,128]{2,1,0:T(1,128)S(1)}, f32[2,1,128]{2,1,0:T(1,128)S(1)}, u32[]{:S(2)}, u32[]{:S(2)}) collective-permute-start(f32[2,1,128]{2,1,0:T(1,128)S(1)} %get-tuple-element.309), channel_id=1, source_target_pairs={{4,0},{8,4},{12,8},{0,12},{5,1},{9,5},{13,9},{1,13},{6,2},{10,6},{... | collective-permute-start | bytes 3080 | tf_op jit(solution)/shard_map/ppermute | solution.py:27
  78.6 11.9 %collective-permute-start.88 = (f32[1,130]{1,0:T(1,128)S(1)}, f32[1,130]{1,0:T(1,128)S(1)}, u32[]{:S(2)}, u32[]{:S(2)}) collective-permute-start(f32[1,130]{1,0:T(1,128)S(1)} %get-tuple-element.225), channel_id=1, source_target_pairs={{0,4},{4,8},{8,12},{12,0},{1,5},{5,9},{9,13},{13,1},{2,6},{6,10},{... | collective-permute-start | bytes 1568 | tf_op jit(solution)/shard_map/ppermute | solution.py:24
  78.6 11.9 %collective-permute-start.89 = (f32[1,130]{1,0:T(1,128)S(1)}, f32[1,130]{1,0:T(1,128)S(1)}, u32[]{:S(2)}, u32[]{:S(2)}) collective-permute-start(f32[1,130]{1,0:T(1,128)S(1)} %get-tuple-element.226), channel_id=1, source_target_pairs={{4,0},{8,4},{12,8},{0,12},{5,1},{9,5},{13,9},{1,13},{6,2},{10,6},{... | collective-permute-start | bytes 1568 | tf_op jit(solution)/shard_map/ppermute | solution.py:27
  95.4 5.8 %collective-permute-start.33 = (f32[1,128]{1,0:T(1,128)S(1)}, f32[1,128]{1,0:T(1,128)S(1)}, u32[]{:S(2)}, u32[]{:S(2)}) collective-permute-start(f32[1,128]{1,0:T(1,128)S(1)} %get-tuple-element.344), channel_id=1, source_target_pairs={{0,4},{4,8},{8,12},{12,0},{1,5},{5,9},{9,13},{13,1},{2,6},{6,10},{... | collective-permute-start | bytes 1544 | tf_op jit(solution)/shard_map/ppermute | solution.py:24
  95.4 5.7 %collective-permute-start.32 = (f32[1,128]{1,0:T(1,128)S(1)}, f32[1,128]{1,0:T(1,128)S(1)}, u32[]{:S(2)}, u32[]{:S(2)}) collective-permute-start(f32[1,128]{1,0:T(1,128)S(1)} %get-tuple-element.345), channel_id=1, source_target_pairs={{4,0},{8,4},{12,8},{0,12},{5,1},{9,5},{13,9},{1,13},{6,2},{10,6},{... | collective-permute-start | bytes 1544 | tf_op jit(solution)/shard_map/ppermute | solution.py:27
  99.4 9.0 %collective-permute-start.90 = (f32[12,1]{1,0:T(8,128)S(1)}, f32[12,1]{1,0:T(8,128)S(1)}, u32[]{:S(2)}, u32[]{:S(2)}) collective-permute-start(f32[12,1]{1,0:T(8,128)S(1)} %get-tuple-element.223), channel_id=1, source_target_pairs={{0,1},{1,2},{2,3},{3,0},{4,5},{5,6},{6,7},{7,4},{8,9},{9,10},{10,1... | collective-permute-start | bytes 152 | tf_op jit(solution)/shard_map/ppermute | solution.py:24
  99.4 9.0 %collective-permute-start.91 = (f32[12,1]{1,0:T(8,128)S(1)}, f32[12,1]{1,0:T(8,128)S(1)}, u32[]{:S(2)}, u32[]{:S(2)}) collective-permute-start(f32[12,1]{1,0:T(8,128)S(1)} %get-tuple-element.224), channel_id=1, source_target_pairs={{1,0},{2,1},{3,2},{0,3},{5,4},{6,5},{7,6},{4,7},{9,8},{10,9},{11,1... | collective-permute-start | bytes 152 | tf_op jit(solution)/shard_map/ppermute | solution.py:27
  127.0 8.0 %collective-permute-start.45 = (f32[2,1,128]{2,1,0:T(1,128)S(1)}, f32[2,1,128]{2,1,0:T(1,128)S(1)}, u32[]{:S(2)}, u32[]{:S(2)}) collective-permute-start(f32[2,1,128]{2,1,0:T(1,128)S(1)} %get-tuple-element.298), channel_id=1, source_target_pairs={{0,4},{4,8},{8,12},{12,0},{1,5},{5,9},{9,13},{13,1},{2,6},{6,10},{... | collective-permute-start | bytes 3080 | tf_op jit(solution)/shard_map/ppermute | solution.py:24
  128.1 6.8 %collective-permute-start.44 = (f32[2,1,128]{2,1,0:T(1,128)S(1)}, f32[2,1,128]{2,1,0:T(1,128)S(1)}, u32[]{:S(2)}, u32[]{:S(2)}) collective-permute-start(f32[2,1,128]{2,1,0:T(1,128)S(1)} %get-tuple-element.299), channel_id=1, source_target_pairs={{4,0},{8,4},{12,8},{0,12},{5,1},{9,5},{13,9},{1,13},{6,2},{10,6},{... | collective-permute-start | bytes 3080 | tf_op jit(solution)/shard_map/ppermute | solution.py:27
  131.1 12.1 %collective-permute-start.92 = (f32[2,1,130]{2,1,0:T(1,128)S(1)}, f32[2,1,130]{2,1,0:T(1,128)S(1)}, u32[]{:S(2)}, u32[]{:S(2)}) collective-permute-start(f32[2,1,130]{2,1,0:T(1,128)S(1)} %get-tuple-element.169), channel_id=1, source_target_pairs={{0,4},{4,8},{8,12},{12,0},{1,5},{5,9},{9,13},{13,1},{2,6},{6,10},{... | collective-permute-start | bytes 3128 | tf_op jit(solution)/shard_map/ppermute | solution.py:24
  131.2 12.1 %collective-permute-start.93 = (f32[2,1,130]{2,1,0:T(1,128)S(1)}, f32[2,1,130]{2,1,0:T(1,128)S(1)}, u32[]{:S(2)}, u32[]{:S(2)}) collective-permute-start(f32[2,1,130]{2,1,0:T(1,128)S(1)} %get-tuple-element.170), channel_id=1, source_target_pairs={{4,0},{8,4},{12,8},{0,12},{5,1},{9,5},{13,9},{1,13},{6,2},{10,6},{... | collective-permute-start | bytes 3128 | tf_op jit(solution)/shard_map/ppermute | solution.py:27
  148.1 5.8 %collective-permute-start.53 = (f32[1,128]{1,0:T(1,128)S(1)}, f32[1,128]{1,0:T(1,128)S(1)}, u32[]{:S(2)}, u32[]{:S(2)}) collective-permute-start(f32[1,128]{1,0:T(1,128)S(1)} %get-tuple-element.338), channel_id=1, source_target_pairs={{0,4},{4,8},{8,12},{12,0},{1,5},{5,9},{9,13},{13,1},{2,6},{6,10},{... | collective-permute-start | bytes 1544 | tf_op jit(solution)/shard_map/ppermute | solution.py:24
  148.1 5.7 %collective-permute-start.52 = (f32[1,128]{1,0:T(1,128)S(1)}, f32[1,128]{1,0:T(1,128)S(1)}, u32[]{:S(2)}, u32[]{:S(2)}) collective-permute-start(f32[1,128]{1,0:T(1,128)S(1)} %get-tuple-element.339), channel_id=1, source_target_pairs={{4,0},{8,4},{12,8},{0,12},{5,1},{9,5},{13,9},{1,13},{6,2},{10,6},{... | collective-permute-start | bytes 1544 | tf_op jit(solution)/shard_map/ppermute | solution.py:27
  152.1 8.9 %collective-permute-start.94 = (f32[2,12,1]{2,1,0:T(8,128)S(1)}, f32[2,12,1]{2,1,0:T(8,128)S(1)}, u32[]{:S(2)}, u32[]{:S(2)}) collective-permute-start(f32[2,12,1]{2,1,0:T(8,128)S(1)} %get-tuple-element.167), channel_id=1, source_target_pairs={{0,1},{1,2},{2,3},{3,0},{4,5},{5,6},{6,7},{7,4},{8,9},{9,10},{10,1... | collective-permute-start | bytes 296 | tf_op jit(solution)/shard_map/ppermute | solution.py:24
  152.1 8.9 %collective-permute-start.95 = (f32[2,12,1]{2,1,0:T(8,128)S(1)}, f32[2,12,1]{2,1,0:T(8,128)S(1)}, u32[]{:S(2)}, u32[]{:S(2)}) collective-permute-start(f32[2,12,1]{2,1,0:T(8,128)S(1)} %get-tuple-element.168), channel_id=1, source_target_pairs={{1,0},{2,1},{3,2},{0,3},{5,4},{6,5},{7,6},{4,7},{9,8},{10,9},{11,1... | collective-permute-start | bytes 296 | tf_op jit(solution)/shard_map/ppermute | solution.py:27
  191.4 6.8 %collective-permute-start.65 = (f32[2,1,128]{2,1,0:T(1,128)}, f32[2,1,128]{2,1,0:T(1,128)S(1)}, u32[]{:S(2)}, u32[]{:S(2)}) collective-permute-start(f32[2,1,128]{2,1,0:T(1,128)} %get-tuple-element.284), channel_id=1, source_target_pairs={{0,4},{4,8},{8,12},{12,0},{1,5},{5,9},{9,13},{13,1},{2,6},{6,10},{... | collective-permute-start | bytes 3080 | tf_op jit(solution)/shard_map/ppermute | solution.py:24
  192.5 5.7 %collective-permute-start.64 = (f32[2,1,128]{2,1,0:T(1,128)}, f32[2,1,128]{2,1,0:T(1,128)S(1)}, u32[]{:S(2)}, u32[]{:S(2)}) collective-permute-start(f32[2,1,128]{2,1,0:T(1,128)} %get-tuple-element.285), channel_id=1, source_target_pairs={{4,0},{8,4},{12,8},{0,12},{5,1},{9,5},{13,9},{1,13},{6,2},{10,6},{... | collective-permute-start | bytes 3080 | tf_op jit(solution)/shard_map/ppermute | solution.py:27
  203.0 7.7 %collective-permute-start.69 = (f32[1,128]{1,0:T(1,128)S(1)}, f32[1,128]{1,0:T(1,128)S(1)}, u32[]{:S(2)}, u32[]{:S(2)}) collective-permute-start(f32[1,128]{1,0:T(1,128)S(1)} %get-tuple-element.334), channel_id=1, source_target_pairs={{0,4},{4,8},{8,12},{12,0},{1,5},{5,9},{9,13},{13,1},{2,6},{6,10},{... | collective-permute-start | bytes 1544 | tf_op jit(solution)/shard_map/ppermute | solution.py:24
  203.0 7.6 %collective-permute-start.68 = (f32[1,128]{1,0:T(1,128)S(1)}, f32[1,128]{1,0:T(1,128)S(1)}, u32[]{:S(2)}, u32[]{:S(2)}) collective-permute-start(f32[1,128]{1,0:T(1,128)S(1)} %get-tuple-element.335), channel_id=1, source_target_pairs={{4,0},{8,4},{12,8},{0,12},{5,1},{9,5},{13,9},{1,13},{6,2},{10,6},{... | collective-permute-start | bytes 1544 | tf_op jit(solution)/shard_map/ppermute | solution.py:27
  216.5 7.8 %collective-permute-start.100 = (f32[1,130]{1,0:T(1,128)S(1)}, f32[1,130]{1,0:T(1,128)S(1)}, u32[]{:S(2)}, u32[]{:S(2)}) collective-permute-start(f32[1,130]{1,0:T(1,128)S(1)} %get-tuple-element.217), channel_id=1, source_target_pairs={{0,4},{4,8},{8,12},{12,0},{1,5},{5,9},{9,13},{13,1},{2,6},{6,10},{... | collective-permute-start | bytes 1568 | tf_op jit(solution)/shard_map/ppermute | solution.py:24
  216.5 7.7 %collective-permute-start.101 = (f32[1,130]{1,0:T(1,128)S(1)}, f32[1,130]{1,0:T(1,128)S(1)}, u32[]{:S(2)}, u32[]{:S(2)}) collective-permute-start(f32[1,130]{1,0:T(1,128)S(1)} %get-tuple-element.218), channel_id=1, source_target_pairs={{4,0},{8,4},{12,8},{0,12},{5,1},{9,5},{13,9},{1,13},{6,2},{10,6},{... | collective-permute-start | bytes 1568 | tf_op jit(solution)/shard_map/ppermute | solution.py:27
  220.4 11.8 %collective-permute-start.73 = (f32[1,128]{1,0:T(1,128)S(1)}, f32[1,128]{1,0:T(1,128)S(1)}, u32[]{:S(2)}, u32[]{:S(2)}) collective-permute-start(f32[1,128]{1,0:T(1,128)S(1)} %get-tuple-element.332), channel_id=1, source_target_pairs={{0,4},{4,8},{8,12},{12,0},{1,5},{5,9},{9,13},{13,1},{2,6},{6,10},{... | collective-permute-start | bytes 1544 | tf_op jit(solution)/shard_map/ppermute | solution.py:24
  220.4 11.8 %collective-permute-start.72 = (f32[1,128]{1,0:T(1,128)S(1)}, f32[1,128]{1,0:T(1,128)S(1)}, u32[]{:S(2)}, u32[]{:S(2)}) collective-permute-start(f32[1,128]{1,0:T(1,128)S(1)} %get-tuple-element.333), channel_id=1, source_target_pairs={{4,0},{8,4},{12,8},{0,12},{5,1},{9,5},{13,9},{1,13},{6,2},{10,6},{... | collective-permute-start | bytes 1544 | tf_op jit(solution)/shard_map/ppermute | solution.py:27
  241.2 8.9 %collective-permute-start.74 = (f32[10,1]{1,0:T(8,128)S(1)}, f32[10,1]{1,0:T(8,128)S(1)}, u32[]{:S(2)}, u32[]{:S(2)}) collective-permute-start(f32[10,1]{1,0:T(8,128)S(1)} %get-tuple-element.280), channel_id=1, source_target_pairs={{1,0},{2,1},{3,2},{0,3},{5,4},{6,5},{7,6},{4,7},{9,8},{10,9},{11,1... | collective-permute-start | bytes 128 | tf_op jit(solution)/shard_map/ppermute | solution.py:27
  242.6 7.4 %collective-permute-start.75 = (f32[10,1]{1,0:T(8,128)S(1)}, f32[10,1]{1,0:T(8,128)S(1)}, u32[]{:S(2)}, u32[]{:S(2)}) collective-permute-start(f32[10,1]{1,0:T(8,128)S(1)} %get-tuple-element.281), channel_id=1, source_target_pairs={{0,1},{1,2},{2,3},{3,0},{4,5},{5,6},{6,7},{7,4},{8,9},{9,10},{10,1... | collective-permute-start | bytes 128 | tf_op jit(solution)/shard_map/ppermute | solution.py:24
  261.7 5.5 %collective-permute-start.116 = (f32[2,2,132]{2,1,0:T(2,128)S(1)}, f32[2,2,132]{2,1,0:T(2,128)S(1)}, u32[]{:S(2)}, u32[]{:S(2)}) collective-permute-start(f32[2,2,132]{2,1,0:T(2,128)S(1)} %get-tuple-element.153), channel_id=1, source_target_pairs={{0,4},{4,8},{8,12},{12,0},{1,5},{5,9},{9,13},{13,1},{2,6},{6,10},{... | collective-permute-start | bytes 6344 | tf_op jit(solution)/shard_map/ppermute | solution.py:24
  267.3 5.6 %collective-permute-start.118 = (f32[2,16,2]{2,1,0:T(8,128)S(1)}, f32[2,16,2]{2,1,0:T(8,128)S(1)}, u32[]{:S(2)}, u32[]{:S(2)}) collective-permute-start(f32[2,16,2]{2,1,0:T(8,128)S(1)} %get-tuple-element.151), channel_id=1, source_target_pairs={{0,1},{1,2},{2,3},{3,0},{4,5},{5,6},{6,7},{7,4},{8,9},{9,10},{10,1... | collective-permute-start | bytes 776 | tf_op jit(solution)/shard_map/ppermute | solution.py:24
  269.0 8.7 %collective-permute-start.77 = (f32[1,128]{1,0:T(1,128)S(1)}, f32[1,128]{1,0:T(1,128)S(1)}, u32[]{:S(2)}, u32[]{:S(2)}) collective-permute-start(f32[1,128]{1,0:T(1,128)S(1)} %get-tuple-element.330), channel_id=1, source_target_pairs={{0,4},{4,8},{8,12},{12,0},{1,5},{5,9},{9,13},{13,1},{2,6},{6,10},{... | collective-permute-start | bytes 1544 | tf_op jit(solution)/shard_map/ppermute | solution.py:24
  270.3 7.4 %collective-permute-start.76 = (f32[1,128]{1,0:T(1,128)S(1)}, f32[1,128]{1,0:T(1,128)S(1)}, u32[]{:S(2)}, u32[]{:S(2)}) collective-permute-start(f32[1,128]{1,0:T(1,128)S(1)} %get-tuple-element.331), channel_id=1, source_target_pairs={{4,0},{8,4},{12,8},{0,12},{5,1},{9,5},{13,9},{1,13},{6,2},{10,6},{... | collective-permute-start | bytes 1544 | tf_op jit(solution)/shard_map/ppermute | solution.py:27
  286.7 8.9 %collective-permute-start.78 = (f32[10,1]{1,0:T(8,128)S(1)}, f32[10,1]{1,0:T(8,128)S(1)}, u32[]{:S(2)}, u32[]{:S(2)}) collective-permute-start(f32[10,1]{1,0:T(8,128)S(1)} %get-tuple-element.278), channel_id=1, source_target_pairs={{1,0},{2,1},{3,2},{0,3},{5,4},{6,5},{7,6},{4,7},{9,8},{10,9},{11,1... | collective-permute-start | bytes 128 | tf_op jit(solution)/shard_map/ppermute | solution.py:27
  288.1 7.4 %collective-permute-start.79 = (f32[10,1]{1,0:T(8,128)S(1)}, f32[10,1]{1,0:T(8,128)S(1)}, u32[]{:S(2)}, u32[]{:S(2)}) collective-permute-start(f32[10,1]{1,0:T(8,128)S(1)} %get-tuple-element.279), channel_id=1, source_target_pairs={{0,1},{1,2},{2,3},{3,0},{4,5},{5,6},{6,7},{7,4},{8,9},{9,10},{10,1... | collective-permute-start | bytes 128 | tf_op jit(solution)/shard_map/ppermute | solution.py:24
  313.8 5.5 %collective-permute-start.136 = (f32[2,2,132]{2,1,0:T(2,128)S(1)}, f32[2,2,132]{2,1,0:T(2,128)S(1)}, u32[]{:S(2)}, u32[]{:S(2)}) collective-permute-start(f32[2,2,132]{2,1,0:T(2,128)S(1)} %get-tuple-element.145), channel_id=1, source_target_pairs={{0,4},{4,8},{8,12},{12,0},{1,5},{5,9},{9,13},{13,1},{2,6},{6,10},{... | collective-permute-start | bytes 6344 | tf_op jit(solution)/shard_map/ppermute | solution.py:24
  322.9 5.5 %collective-permute-start.140 = (f32[1,130]{1,0:T(1,128)S(1)}, f32[1,130]{1,0:T(1,128)S(1)}, u32[]{:S(2)}, u32[]{:S(2)}) collective-permute-start(f32[1,130]{1,0:T(1,128)S(1)} %get-tuple-element.189), channel_id=1, source_target_pairs={{0,4},{4,8},{8,12},{12,0},{1,5},{5,9},{9,13},{13,1},{2,6},{6,10},{... | collective-permute-start | bytes 1568 | tf_op jit(solution)/shard_map/ppermute | solution.py:24
  331.8 5.5 %collective-permute-start.144 = (f32[1,130]{1,0:T(1,128)S(1)}, f32[1,130]{1,0:T(1,128)S(1)}, u32[]{:S(2)}, u32[]{:S(2)}) collective-permute-start(f32[1,130]{1,0:T(1,128)S(1)} %get-tuple-element.185), channel_id=1, source_target_pairs={{0,4},{4,8},{8,12},{12,0},{1,5},{5,9},{9,13},{13,1},{2,6},{6,10},{... | collective-permute-start | bytes 1568 | tf_op jit(solution)/shard_map/ppermute | solution.py:24
  349.7 5.5 %collective-permute-start.152 = (f32[2,1,130]{2,1,0:T(1,128)S(1)}, f32[2,1,130]{2,1,0:T(1,128)S(1)}, u32[]{:S(2)}, u32[]{:S(2)}) collective-permute-start(f32[2,1,130]{2,1,0:T(1,128)S(1)} %get-tuple-element.141), channel_id=1, source_target_pairs={{0,4},{4,8},{8,12},{12,0},{1,5},{5,9},{9,13},{13,1},{2,6},{6,10},{... | collective-permute-start | bytes 3128 | tf_op jit(solution)/shard_map/ppermute | solution.py:24
  (184 other events, 536.8 us)
where the time goes:
time: 429 us; the launch traced here: 427 us
  starting transfers between devices  206 us (48%)
  waiting for transfers between devices  90.3 us (21%)
  blocking collectives  62.7 us (15%)
  local copies, waits for them, and re-layouts  33.4 us (8%)
  other arithmetic  19.4 us (5%)
  matrix products  12.7 us (3%)
    ppermute x78, starting transfers between devices, with_halo(): lax.ppermute(lax.slice_in_dim(block, 0, width, axis=dim), axis, backward)  166 us
    ppermute x78, waiting for transfers between devices, with_halo(): lax.ppermute(lax.slice_in_dim(block, block.shape[dim] - width, None, axis...  76 us
    psum x1, blocking collectives, shards(): lax.psum((totals[0], totals[1], totals[2]), ('rows', 'cols', 'section'))  62.7 us
    ppermute x78, starting transfers between devices, with_halo(): lax.ppermute(lax.slice_in_dim(block, block.shape[dim] - width, None, axis...  39.9 us
    unnamed x244, local copies, waits for them, and re-layouts  24.2 us
    ppermute x78, waiting for transfers between devices, with_halo(): lax.ppermute(lax.slice_in_dim(block, 0, width, axis=dim), axis, backward)  14.3 us
  transfers between devices with their start and end apart: 156, of which 68 were waited for; matrix products, arithmetic and copies ran while one was open for 2% of the time, Pallas kernels for 0%

commit v1 on v0

--- a/solution.py
+++ b/solution.py
@@ -1,18 +1,368 @@
+import functools
 import math
 
 import jax
 import jax.numpy as jnp
 from jax import lax
+from jax.experimental import pallas as pl
+from jax.experimental.pallas import tpu as pltpu
 from jax.sharding import PartitionSpec as P
 
 STEPS = 4
 SWEEPS = 3
-
+CHANNELS = 64
+TAPS = 18
+COEFS = 32
+LANES = 128
+HALO = 48
 
 time_step = 0.1
 viscosity = 0.2
 correction_gain = 0.25
 gradient_gain = 10.0
+
+GELU_SCALE = math.sqrt(2.0 / math.pi)
+GELU_CUBE = 0.044715
+
+RANGE = (-1, 0, 1, 2)
+
+
+def shift(plane, row, col):
+    if row:
+        plane = pltpu.roll(plane, (-row) % plane.shape[0], 0)
+    if col:
+        plane = pltpu.roll(plane, (-col) % plane.shape[1], 1)
+    return plane
+
+
+def gelu_pair(x):
+    square = x * x
+    t = jnp.tanh(x * (GELU_SCALE + (GELU_SCALE * GELU_CUBE) * square))
+    half = 0.5 * x
+    slope = (0.5 + 0.5 * t) + (half * (1.0 - t * t)) * (
+        GELU_SCALE + (3.0 * GELU_SCALE * GELU_CUBE) * square
+    )
+    return half + half * t, slope
+
+
+def neighbours(p):
+    return (shift(p, 1, 0) + shift(p, -1, 0)) + (shift(p, 0, 1) + shift(p, 0, -1))
+
+
+def dot(a, b):
+    return jnp.dot(a, b, preferred_element_type=jnp.float32)
+
+
+def dot_cells(a, b):
+    return lax.dot_general(a, b, (((1,), (1,)), ((), ())), preferred_element_type=jnp.float32)
+
+
+def kernel(
+    core,
+    chunk_rows,
+    gathered,
+    w1,
+    w2,
+    w3,
+    w1t,
+    w2t,
+    w3t,
+    velocity,
+    grads,
+    s_all,
+    up,
+    st,
+    wt,
+    qs,
+    xs,
+    co,
+    x_all,
+    a1_all,
+    a2_all,
+    g1_all,
+    g2_all,
+    g_first,
+    g_second,
+    g_third,
+):
+    height = s_all.shape[2]
+    chunks = height // chunk_rows
+    cells = chunk_rows * LANES
+    z = lax.axis_index("rows")
+
+    lane = lax.broadcasted_iota(jnp.int32, (8, LANES), 1) + (core * z - HALO)
+    own = (lane >= 0) & (lane < LANES)
+    amount = lax.rem(HALO - core * z + 4 * LANES, LANES)
+    for i, k in enumerate((0, 2, 1, 3)):
+        row = pl.multiple_of(8 * (z ^ k), 8)
+        for c in range(4):
+            mine = pltpu.roll(gathered[i, 0, c], amount, 1)
+            other = pltpu.roll(gathered[i, 1, c], amount, 1)
+            tile = jnp.where(own, mine, other)
+            if c < 2:
+                s_all[0, c, pl.ds(row, 8), :] = tile
+            else:
+                up[c - 2, pl.ds(row, 8), :] = tile
+
+    xs[...] = jnp.zeros_like(xs)
+    g_first[...] = jnp.zeros_like(g_first)
+    g_second[...] = jnp.zeros_like(g_second)
+    g_third[...] = jnp.zeros_like(g_third)
+
+    def forward(step, carry):
+        s = [s_all[step, c] for c in range(2)]
+        for c in range(2):
+            for a in RANGE:
+                line = shift(s[c], a, 0)
+                for b in RANGE:
+                    plane = shift(line, 0, b)
+                    st[step, c * 16 + (a + 1) * 4 + (b + 1)] = plane
+                    if a < 2 and b < 2:
+                        xs[pl.ds(c * 9 + (a + 1) * 3 + (b + 1), height, stride=32), :] = plane
+
+        def chunk(index, carry):
+            base = index * (chunk_rows * 32)
+            x = jnp.concatenate(
+                [xs[pl.ds(base + 32 * r, 32), :] for r in range(chunk_rows)], axis=1
+            ).astype(jnp.bfloat16)
+            at = pl.ds(pl.multiple_of(index * cells, cells), cells)
+            x_all[step, :, at] = x
+            act, slope = gelu_pair(dot(w1[...], x))
+            act = act.astype(jnp.bfloat16)
+            a1_all[step, :, at] = act
+            g1_all[step, :, at] = slope
+            act, slope = gelu_pair(dot(w2[...], act))
+            act = act.astype(jnp.bfloat16)
+            a2_all[step, :, at] = act
+            g2_all[step, :, at] = slope
+            out = dot(w3[...], act)
+            for r in range(chunk_rows):
+                co[pl.ds(base + 32 * r, 32), :] = out[:, r * LANES : (r + 1) * LANES]
+            return carry
+
+        lax.fori_loop(0, chunks, chunk, 0)
+
+        q = [[None, None], [None, None]]
+        for f in range(2):
+            total = None
+            for t in range(16):
+                raw = co[pl.ds(f * 16 + t, height, stride=32), :]
+                total = raw if total is None else total + raw
+            mean = (correction_gain / 16.0) * total
+            for t in range(16):
+                raw = co[pl.ds(f * 16 + t, height, stride=32), :]
+                weight = correction_gain * raw - mean
+                if t in ((5, 9), (5, 6))[f]:
+                    weight = weight + 0.5
+                wt[step, f * 16 + t] = weight
+                for c in range(2):
+                    term = weight * st[step, c * 16 + t]
+                    q[f][c] = term if q[f][c] is None else q[f][c] + term
+        speed = [0.5 * (s[0] + shift(s[0], 1, 0)), 0.5 * (s[1] + shift(s[1], 0, 1))]
+        moved = []
+        for c in range(2):
+            for f in range(2):
+                qs[step, f * 2 + c] = q[f][c]
+            rows, cols = speed[0] * q[0][c], speed[1] * q[1][c]
+            transport = (rows - shift(rows, -1, 0)) + (cols - shift(cols, 0, -1))
+            moved.append(
+                s[c]
+                - time_step * transport
+                + time_step * viscosity * (neighbours(s[c]) - 4.0 * s[c])
+            )
+        source = 0.5 * (
+            (shift(moved[0], 1, 0) - shift(moved[0], -1, 0))
+            + (shift(moved[1], 0, 1) - shift(moved[1], 0, -1))
+        )
+        pressure = -0.25 * source
+        for _ in range(SWEEPS - 1):
+            pressure = 0.25 * (neighbours(pressure) - source)
+        s_all[step + 1, 0] = moved[0] - 0.5 * (shift(pressure, 1, 0) - shift(pressure, -1, 0))
+        s_all[step + 1, 1] = moved[1] - 0.5 * (shift(pressure, 0, 1) - shift(pressure, 0, -1))
+        return carry
+
+    lax.fori_loop(0, STEPS, forward, 0)
+    velocity[...] = s_all[STEPS]
+
+    column = lax.broadcasted_iota(jnp.int32, (1, cells), 1) % LANES
+    inside = (column >= HALO) & (column < HALO + core)
+
+    def backward(count, carry):
+        step = STEPS - 1 - count
+        u = [up[c] for c in range(2)]
+        s = [s_all[step, c] for c in range(2)]
+        p_bar = 0.5 * (
+            (shift(u[0], 1, 0) - shift(u[0], -1, 0)) + (shift(u[1], 0, 1) - shift(u[1], 0, -1))
+        )
+        source_bar = -0.25 * p_bar
+        for _ in range(SWEEPS - 1):
+            p_bar = 0.25 * neighbours(p_bar)
+            source_bar = source_bar - 0.25 * p_bar
+        half = 0.5 * source_bar
+        m_bar = [
+            u[0] + (shift(half, -1, 0) - shift(half, 1, 0)),
+            u[1] + (shift(half, 0, -1) - shift(half, 0, 1)),
+        ]
+        speed = [0.5 * (s[0] + shift(s[0], 1, 0)), 0.5 * (s[1] + shift(s[1], 0, 1))]
+        speed_bar = [None, None]
+        q_bar = [[None, None], [None, None]]
+        for c in range(2):
+            flux_bar = [
+                time_step * (shift(m_bar[c], 1, 0) - m_bar[c]),
+                time_step * (shift(m_bar[c], 0, 1) - m_bar[c]),
+            ]
+            for f in range(2):
+                q_bar[f][c] = speed[f] * flux_bar[f]
+                term = qs[step, f * 2 + c] * flux_bar[f]
+                speed_bar[f] = term if c == 0 else speed_bar[f] + term
+            up[c] = m_bar[c] + time_step * viscosity * (neighbours(m_bar[c]) - 4.0 * m_bar[c])
+        up[0] = up[0] + 0.5 * (speed_bar[0] + shift(speed_bar[0], -1, 0))
+        up[1] = up[1] + 0.5 * (speed_bar[1] + shift(speed_bar[1], 0, -1))
+
+        for f in range(2):
+            total = None
+            for t in range(16):
+                w_bar = q_bar[f][0] * st[step, t] + q_bar[f][1] * st[step, 16 + t]
+                total = w_bar if total is None else total + w_bar
+            mean = (1.0 / 16.0) * total
+            for t in range(16):
+                w_bar = q_bar[f][0] * st[step, t] + q_bar[f][1] * st[step, 16 + t]
+                co[pl.ds(f * 16 + t, height, stride=32), :] = correction_gain * (w_bar - mean)
+
+        def chunk(index, carry):
+            base = index * (chunk_rows * 32)
+            at = pl.ds(pl.multiple_of(index * cells, cells), cells)
+            third = jnp.concatenate(
+                [co[pl.ds(base + 32 * r, 32), :] for r in range(chunk_rows)], axis=1
+            )
+            zero = jnp.zeros((), jnp.float32)
+            back = third.astype(jnp.bfloat16)
+            kept = jnp.where(inside, third, zero).astype(jnp.bfloat16)
+            g_third[...] += dot_cells(kept, a2_all[step, :, at])
+            second = dot(w3t[...], back) * g2_all[step, :, at]
+            back = second.astype(jnp.bfloat16)
+            kept = jnp.where(inside, second, zero).astype(jnp.bfloat16)
+            g_second[...] += dot_cells(kept, a1_all[step, :, at])
+            first = dot(w2t[...], back) * g1_all[step, :, at]
+            back = first.astype(jnp.bfloat16)
+            kept = jnp.where(inside, first, zero).astype(jnp.bfloat16)
+            g_first[...] += dot_cells(kept, x_all[step, :, at])
+            out = dot(w1t[...], back)
+            for r in range(chunk_rows):
+                xs[pl.ds(base + 32 * r, 32), :] = out[:, r * LANES : (r + 1) * LANES]
+            return carry
+
+        lax.fori_loop(0, chunks, chunk, 0)
+
+        for c in range(2):
+            s_bar = up[c]
+            for b in RANGE:
+                column_sum = None
+                for a in RANGE:
+                    t = (a + 1) * 4 + (b + 1)
+                    y = wt[step, t] * q_bar[0][c] + wt[step, 16 + t] * q_bar[1][c]
+                    if a < 2 and b < 2:
+                        y = y + xs[pl.ds(c * 9 + (a + 1) * 3 + (b + 1), height, stride=32), :]
+                    y = shift(y, -a, 0)
+                    column_sum = y if column_sum is None else column_sum + y
+                s_bar = s_bar + shift(column_sum, 0, -b)
+            up[c] = s_bar
+        return carry
+
+    lax.fori_loop(0, STEPS, backward, 0)
+    grads[:, 0:64] = g_second[...]
+    grads[:, 64:96] = g_first[...]
+    grads[0:32, 96:128] = g_third[:, 0:32]
+    grads[32:64, 96:128] = g_third[:, 32:64]
+
+
+def strip_call(height, core, chunk_rows, gathered, weights):
+    cells = height * LANES
+    f32, bf16 = jnp.float32, jnp.bfloat16
+    vmem = pl.BlockSpec(memory_space=pltpu.VMEM)
+    return pl.pallas_call(
+        functools.partial(kernel, core, chunk_rows),
+        out_shape=(
+            jax.ShapeDtypeStruct((2, height, LANES), f32),
+            jax.ShapeDtypeStruct((CHANNELS, LANES), f32),
+        ),
+        in_specs=[vmem] * 7,
+        out_specs=(vmem, vmem),
+        scratch_shapes=[
+            pltpu.VMEM((STEPS + 1, 2, height, LANES), f32),
+            pltpu.VMEM((2, height, LANES), f32),
+            pltpu.VMEM((STEPS, 32, height, LANES), f32),
+            pltpu.VMEM((STEPS, 32, height, LANES), f32),
+            pltpu.VMEM((STEPS, 4, height, LANES), f32),
+            pltpu.VMEM((height * 32, LANES), f32),
+            pltpu.VMEM((height * 32, LANES), f32),
+            pltpu.VMEM((STEPS, 32, cells), bf16),
+            pltpu.VMEM((STEPS, CHANNELS, cells), bf16),
+            pltpu.VMEM((STEPS, CHANNELS, cells), bf16),
+            pltpu.VMEM((STEPS, CHANNELS, cells), f32),
+            pltpu.VMEM((STEPS, CHANNELS, cells), f32),
+            pltpu.VMEM((CHANNELS, 32), f32),
+            pltpu.VMEM((CHANNELS, CHANNELS), f32),
+            pltpu.VMEM((COEFS, CHANNELS), f32),
+        ],
+        compiler_params=pltpu.CompilerParams(vmem_limit_bytes=48 * 1024 * 1024),
+    )(gathered, *weights)
+
+
+def swap(x, axis, bit):
+    return lax.ppermute(x, axis, [(i, i ^ bit) for i in range(lax.axis_size(axis))])
+
+
+def strips(state, cotangent, first_weight, second_weight, third_weight):
+    row_count = lax.axis_size("rows")
+    block_count = lax.axis_size(("cols", "section"))
+    height = row_count * state.shape[1]
+    core = LANES // row_count
+    z = lax.axis_index("rows")
+
+    tile = jnp.concatenate([state, cotangent], 0)
+    pairs = []
+    for row in range(row_count):
+        step = 1 if row < row_count // 2 else block_count - 1
+        for block in range(block_count):
+            pairs.append((row * block_count + block, row * block_count + (block + step) % block_count))
+    held = jnp.stack([tile, swap(tile, "rows", 2)])
+    other = lax.ppermute(held, ("rows", "cols", "section"), pairs)
+    held = jnp.stack([held, other], 1)
+    held = jnp.concatenate([held, swap(held, "rows", 1)], 0)
+
+    first = jnp.pad(first_weight, ((0, 0), (0, 32 - TAPS)))
+    velocity, grads = strip_call(
+        height,
+        core,
+        4,
+        held,
+        (first, second_weight, third_weight, first.T, second_weight.T, third_weight.T),
+    )
+
+    grads = grads + swap(grads, "section", 1)
+    grads = grads + swap(grads, "cols", 1)
+    strip = velocity[:, :, HALO : HALO + core].reshape(4, 16, core)
+    strip = strip.transpose(1, 0, 2).reshape(16, LANES)
+    sent = jnp.concatenate([grads, strip], 0)
+    got = swap(sent, "rows", 1)
+    sent = jnp.concatenate([sent[:64] + got[:64], sent[64:], got[64:]], 0)
+    got = swap(sent, "rows", 2)
+    grads = sent[:64] + got[:64]
+    parts = jnp.concatenate([sent[64:], got[64:]], 0).reshape(4, 16, 4, core)
+    parts = parts.transpose(0, 2, 1, 3).reshape(4, 2, 4, 8, core)
+    mine = lax.dynamic_index_in_dim(parts, z, 2, keepdims=False)
+    tile_out = jnp.concatenate(
+        [lax.dynamic_index_in_dim(mine, z ^ k, 0, keepdims=False) for k in range(4)], -1
+    )
+    factor = gradient_gain / math.sqrt(height * LANES * block_count)
+    grads = grads * factor
+    return (
+        tile_out,
+        grads[:, 64 : 64 + TAPS],
+        grads[:, 0:64],
+        jnp.concatenate([grads[:32, 96:], grads[32:, 96:]], 1),
+    )
 
 
 def with_halo(block, sides, width):
@@ -144,7 +494,7 @@
     )
 
 
-def neighbours(padded):
+def padded_neighbours(padded):
     return padded[2:, 1:-1] + padded[:-2, 1:-1] + padded[1:-1, 2:] + padded[1:-1, :-2]
 
 
@@ -171,7 +521,7 @@
     )
 
 
-def shards(state, cotangent, first_weight, second_weight, third_weight):
+def tiles(state, cotangent, first_weight, second_weight, third_weight):
     weights = (first_weight, second_weight, third_weight)
     current = state
     saved = []
@@ -186,7 +536,7 @@
             padded = with_halo(pressure, (("rows", 0), (("cols", "section"), 1)), 1)
             pressure_pads.append(padded)
             if sweep_number < SWEEPS - 1:
-                pressure = 0.25 * (neighbours(padded) - source)
+                pressure = 0.25 * (padded_neighbours(padded) - source)
         saved.append((extended, velocity_pad, pressure_pads))
         current = moved - pressure_gradient(pressure_pads[-1])
     upstream = cotangent
@@ -206,7 +556,7 @@
             pressure_grad = fold_rims(returned, 1)
             source_grad = source_grad - 0.25 * pressure_grad
             if sweep_number > 0:
-                pad_grad = jax.vjp(neighbours, pressure_pads[sweep_number - 1])[1](
+                pad_grad = jax.vjp(padded_neighbours, pressure_pads[sweep_number - 1])[1](
                     0.25 * pressure_grad
                 )[0]
         velocity_grad = jax.vjp(divergence, velocity_pad)[1](source_grad)[0]
@@ -228,8 +578,19 @@
 
 
 def solution(mesh):
+    def program(state, *rest):
+        fits = (
+            lax.axis_size("rows") == 4
+            and state.shape[1] == 8
+            and state.shape[2] == LANES
+            and lax.axis_size(("cols", "section")) >= 2
+            and lax.axis_size("section") == 2
+            and lax.axis_size("cols") == 2
+        )
+        return (strips if fits else tiles)(state, *rest)
+
     return jax.shard_map(
-        shards,
+        program,
         mesh=mesh,
         in_specs=(
             P(None, ("groups", "rows"), ("cols", "section")),

time: 429 us -> 73 us (0.17)
  starting transfers between devices: 206 us -> 11.4 us
  waiting for transfers between devices: 90.3 us -> 14.6 us
  blocking collectives: 62.7 us -> 0 us
  Pallas kernels: 0 us -> 40.6 us
  local copies, waits for them, and re-layouts: 33.4 us -> 3.82 us
  other arithmetic: 19.4 us -> 1.42 us
  matrix products: 12.7 us -> 0 us
    ppermute x156 -> x7, starting transfers between devices: 206 us -> 11.4 us  [the longest x6 11.3 us: swap(): lax.ppermute(x, axis, [(i, i ^ bit) for i in range(lax.axis_size(axis))])]
    ppermute x156 -> x7, waiting for transfers between devices: 90.3 us -> 14.6 us  [the longest x6 12.8 us: swap(): lax.ppermute(x, axis, [(i, i ^ bit) for i in range(lax.axis_size(axis))])]
    psum x1 -> x0, blocking collectives: 62.7 us -> none  [shards(): lax.psum((totals[0], totals[1], totals[2]), ('rows', 'cols', 'section'))]
    pallas_call x0 -> x1, Pallas kernels: none -> 40.6 us  [strip_call(): pl.pallas_call(functools.partial(kernel, core, chunk_rows), out_shape=(ja...]
    unnamed x244 -> x15, local copies, waits for them, and re-layouts: 24.2 us -> 3.35 us
    dot_general x34 -> x0, matrix products: 12.7 us -> none  [the longest x4 2.43 us: advance_back(): lax.dot_general(third_weight, coef_round, inner, preferred_element_type=j...]
    mul x51 -> x1, other arithmetic: 7.8 us -> 0.01 us  [strips(): grads = grads * factor]
  transfers between devices with their start and end apart: 156 -> 7, of which waited for: 68 -> 7; matrix products, arithmetic and copies ran while one was open for 2% -> 1% of each run, Pallas kernels for 0% -> 0%
where the time goes in v1:
time: 73 us; the launch traced here: 72.6 us
  Pallas kernels  40.6 us (56%)
  waiting for transfers between devices  14.6 us (20%)
  starting transfers between devices  11.4 us (16%)
  local copies, waits for them, and re-layouts  3.82 us (5%)
  other arithmetic  1.42 us (2%)
  between operations  0.74 us (1%)
    pallas_call x1, Pallas kernels, strip_call(): pl.pallas_call(functools.partial(kernel, core, chunk_rows), out_shape=(ja...  40.6 us
    ppermute x6, waiting for transfers between devices, swap(): lax.ppermute(x, axis, [(i, i ^ bit) for i in range(lax.axis_size(axis))])  12.8 us
    ppermute x6, starting transfers between devices, swap(): lax.ppermute(x, axis, [(i, i ^ bit) for i in range(lax.axis_size(axis))])  11.3 us
    unnamed x15, local copies, waits for them, and re-layouts  3.35 us
    ppermute x1, waiting for transfers between devices, strips(): other = lax.ppermute(held, ('rows', 'cols', 'section'), pairs)  1.8 us
  transfers between devices with their start and end apart: 7, of which 7 were waited for; matrix products, arithmetic and copies ran while one was open for 1% of the time, Pallas kernels for 0%

profile of v1, /device:TPU:0, one launch (start us, length us, event | category | flops | bytes accessed | tf_op | source)
XLA Modules:
  0.0 72.6 jit_solution(6041881808646740861)
XLA Ops:
  0.6 0.0 copy-start.4
  0.6 0.7 constant_dynamic-update-slice_fusion.1
  1.3 0.0 copy-done.4
  1.3 4.0 %collective-permute-start = (f32[4,8,128]{2,1,0:T(8,128)S(1)}, f32[4,8,128]{2,1,0:T(8,128)S(1)}, u32[]{:S(2)}, u32[]{:S(2)}) collective-permute-start(f32[4,8,128]{2,1,0:T(8,128)S(1)} %constant_dynamic-update-slice_fusion), channel_id=1, source_target_pairs={{0,8},{4,12},{8,0},{12,4},{1,9},{5,13},{9,1},{13,5},{2,10},{6,14},... | collective-permute-start | bytes 49160 | tf_op jit(solution)/shard_map/ppermute | solution.py:313
  5.4 1.7 %collective-permute-done = f32[4,8,128]{2,1,0:T(8,128)S(1)} collective-permute-done((f32[4,8,128]{2,1,0:T(8,128)S(1)}, f32[4,8,128]{2,1,0:T(8,128)S(1)}, u32[]{:S(2)}, u32[]{:S(2)}) %collective-permute-start) | collective-permute-done | bytes 16416 | tf_op jit(solution)/shard_map/ppermute | solution.py:313
  7.1 0.0 copy-start.3
  7.1 0.0 copy-start
  7.1 0.1 collective-permute-start.1
  7.2 0.6 copy-done.3
  7.8 0.1 copy.23
  7.9 0.0 copy-done
  7.9 0.0 copy-start.1
  7.9 0.1 copy.16
  8.0 0.6 copy-done.1
  8.6 0.1 copy.17
  8.7 1.8 %collective-permute-done.1 = f32[2,4,8,128]{3,2,1,0:T(8,128)S(1)} collective-permute-done((f32[2,4,8,128]{3,2,1,0:T(8,128)S(1)}, f32[2,4,8,128]{3,2,1,0:T(8,128)S(1)}, u32[]{:S(2)}, u32[]{:S(2)}) %collective-permute-start.1) | collective-permute-done | bytes 32800 | tf_op jit(solution)/shard_map/ppermute | solution.py:330
  10.5 1.9 %collective-permute-start.2 = (f32[2,2,4,8,128]{4,3,2,1,0:T(8,128)S(1)}, f32[2,2,4,8,128]{4,3,2,1,0:T(8,128)S(1)}, u32[]{:S(2)}, u32[]{:S(2)}) collective-permute-start(f32[2,2,4,8,128]{4,3,2,1,0:T(8,128)S(1)} %pad_maximum_fusion.1), channel_id=1, source_target_pairs={{0,4},{4,0},{8,12},{12,8},{1,5},{5,1},{9,13},{13,9},{2,6},{6,2},{1... | collective-permute-start | bytes 196616 | tf_op jit(solution)/shard_map/ppermute | solution.py:313
  12.4 2.3 %collective-permute-done.2 = f32[2,2,4,8,128]{4,3,2,1,0:T(8,128)S(1)} collective-permute-done((f32[2,2,4,8,128]{4,3,2,1,0:T(8,128)S(1)}, f32[2,2,4,8,128]{4,3,2,1,0:T(8,128)S(1)}, u32[]{:S(2)}, u32[]{:S(2)}) %collective-permute-start.2) | collective-permute-done | bytes 65568 | tf_op jit(solution)/shard_map/ppermute | solution.py:313
  14.8 40.6 %shard_map.84 = (f32[2,32,128]{2,1,0:T(8,128)S(1)}, f32[64,128]{1,0:T(8,128)S(1)}) custom-call(f32[4,2,4,8,128]{4,3,2,1,0:T(8,128)S(1)} %pad_maximum_fusion.gathered, bf16[64,32]{1,0:T(8,128)(2,1)S(1)} %pad.4.clone.w1, bf16[64,64]{1,0:T(8,128)(2,1)S(1)} %copy-done, bf16[32,64]{1,0:T(8,128)(2,1)S(1)} %copy-done.1, bf16[32,64]{1,0:T(8,128)(2,1)S(1)} %pad_bitcast_fusion.w1t, ...), custom_call_target="tpu_custom_call" | custom-call | tf_op jit(solution)/shard_map/pallas_call | solution.py:283
  55.4 0.1 collective-permute-start.3
  55.5 1.2 %collective-permute-done.3 = f32[64,128]{1,0:T(8,128)S(1)} collective-permute-done((f32[64,128]{1,0:T(8,128)S(1)}, f32[64,128]{1,0:T(8,128)S(1)}, u32[]{:S(2)}, u32[]{:S(2)}) %collective-permute-start.3) | collective-permute-done | bytes 32800 | tf_op jit(solution)/shard_map/ppermute | solution.py:313
  56.7 1.9 %collective-permute-start.4 = (f32[64,128]{1,0:T(8,128)S(1)}, f32[64,128]{1,0:T(8,128)S(1)}, u32[]{:S(2)}, u32[]{:S(2)}) collective-permute-start(f32[64,128]{1,0:T(8,128)S(1)} %add.49), channel_id=1, source_target_pairs={{0,2},{2,0},{1,3},{3,1},{4,6},{6,4},{5,7},{7,5},{8,10},{10,8},{9,1... | collective-permute-start | bytes 98312 | tf_op jit(solution)/shard_map/ppermute | solution.py:313
  58.5 0.1 slice.29
  58.6 0.1 reshape.29
  58.7 1.9 %collective-permute-done.4 = f32[64,128]{1,0:T(8,128)S(1)} collective-permute-done((f32[64,128]{1,0:T(8,128)S(1)}, f32[64,128]{1,0:T(8,128)S(1)}, u32[]{:S(2)}, u32[]{:S(2)}) %collective-permute-start.4) | collective-permute-done | bytes 32800 | tf_op jit(solution)/shard_map/ppermute | solution.py:313
  60.6 2.0 %collective-permute-start.5 = (f32[80,128]{1,0:T(8,128)S(1)}, f32[80,128]{1,0:T(8,128)S(1)}, u32[]{:S(2)}, u32[]{:S(2)}) collective-permute-start(f32[80,128]{1,0:T(8,128)S(1)} %pad_maximum_fusion.3), channel_id=1, source_target_pairs={{0,4},{4,0},{8,12},{12,8},{1,5},{5,1},{9,13},{13,9},{2,6},{6,2},{1... | collective-permute-start | bytes 122888 | tf_op jit(solution)/shard_map/ppermute | solution.py:313
  62.6 2.1 %collective-permute-done.5 = f32[80,128]{1,0:T(8,128)S(1)} collective-permute-done((f32[80,128]{1,0:T(8,128)S(1)}, f32[80,128]{1,0:T(8,128)S(1)}, u32[]{:S(2)}, u32[]{:S(2)}) %collective-permute-start.5) | collective-permute-done | bytes 40992 | tf_op jit(solution)/shard_map/ppermute | solution.py:313
  64.7 1.5 %collective-permute-start.6 = (f32[96,128]{1,0:T(8,128)S(1)}, f32[96,128]{1,0:T(8,128)S(1)}, u32[]{:S(2)}, u32[]{:S(2)}) collective-permute-start(f32[96,128]{1,0:T(8,128)S(1)} %pad_maximum_fusion.2), channel_id=1, source_target_pairs={{0,8},{4,12},{8,0},{12,4},{1,9},{5,13},{9,1},{13,5},{2,10},{6,14},... | collective-permute-start | bytes 147464 | tf_op jit(solution)/shard_map/ppermute | solution.py:313
  66.1 3.6 %collective-permute-done.6 = f32[96,128]{1,0:T(8,128)S(1)} collective-permute-done((f32[96,128]{1,0:T(8,128)S(1)}, f32[96,128]{1,0:T(8,128)S(1)}, u32[]{:S(2)}, u32[]{:S(2)}) %collective-permute-start.6) | collective-permute-done | bytes 49184 | tf_op jit(solution)/shard_map/ppermute | solution.py:313
  69.7 0.0 copy-start.2
  69.7 0.1 fusion.2
  69.8 0.1 slice.42
  69.9 0.5 copy-done.2
  70.4 0.7 copy.21
  71.0 0.1 reshape.30
  71.2 0.7 pad_maximum_fusion.6
  71.9 0.7 pad_maximum_fusion.7
  (18 shorter events, 0.1 us)
Async XLA Ops:
  0.6 0.7 copy-start.4
  1.3 5.8 %collective-permute-start = (f32[4,8,128]{2,1,0:T(8,128)S(1)}, f32[4,8,128]{2,1,0:T(8,128)S(1)}, u32[]{:S(2)}, u32[]{:S(2)}) collective-permute-start(f32[4,8,128]{2,1,0:T(8,128)S(1)} %constant_dynamic-update-slice_fusion), channel_id=1, source_target_pairs={{0,8},{4,12},{8,0},{12,4},{1,9},{5,13},{9,1},{13,5},{2,10},{6,14},... | collective-permute-start | bytes 49160 | tf_op jit(solution)/shard_map/ppermute | solution.py:313
  7.1 0.7 copy-start.3
  7.1 0.8 %copy-start = (bf16[64,64]{1,0:T(8,128)(2,1)S(1)}, bf16[64,64]{1,0:T(8,128)(2,1)}, u32[]{:S(2)}) copy-start(bf16[64,64]{1,0:T(8,128)(2,1)} %w2.1) | copy-start | bytes 24580
  7.1 3.4 %collective-permute-start.1 = (f32[2,4,8,128]{3,2,1,0:T(8,128)S(1)}, f32[2,4,8,128]{3,2,1,0:T(8,128)S(1)}, u32[]{:S(2)}, u32[]{:S(2)}) collective-permute-start(f32[2,4,8,128]{3,2,1,0:T(8,128)S(1)} %get-tuple-element.23), channel_id=1, source_target_pairs={{0,1},{1,2},{2,3},{3,0},{4,5},{5,6},{6,7},{7,4},{8,11},{9,8},{10,9... | collective-permute-start | bytes 98312 | tf_op jit(solution)/shard_map/ppermute | solution.py:330
  7.9 0.7 copy-start.1
  10.5 4.3 %collective-permute-start.2 = (f32[2,2,4,8,128]{4,3,2,1,0:T(8,128)S(1)}, f32[2,2,4,8,128]{4,3,2,1,0:T(8,128)S(1)}, u32[]{:S(2)}, u32[]{:S(2)}) collective-permute-start(f32[2,2,4,8,128]{4,3,2,1,0:T(8,128)S(1)} %pad_maximum_fusion.1), channel_id=1, source_target_pairs={{0,4},{4,0},{8,12},{12,8},{1,5},{5,1},{9,13},{13,9},{2,6},{6,2},{1... | collective-permute-start | bytes 196616 | tf_op jit(solution)/shard_map/ppermute | solution.py:313
  55.4 1.3 %collective-permute-start.3 = (f32[64,128]{1,0:T(8,128)S(1)}, f32[64,128]{1,0:T(8,128)S(1)}, u32[]{:S(2)}, u32[]{:S(2)}) collective-permute-start(f32[64,128]{1,0:T(8,128)S(1)} %get-tuple-element.7), channel_id=1, source_target_pairs={{0,1},{1,0},{2,3},{3,2},{4,5},{5,4},{6,7},{7,6},{8,9},{9,8},{10,11... | collective-permute-start | bytes 98312 | tf_op jit(solution)/shard_map/ppermute | solution.py:313
  56.7 3.9 %collective-permute-start.4 = (f32[64,128]{1,0:T(8,128)S(1)}, f32[64,128]{1,0:T(8,128)S(1)}, u32[]{:S(2)}, u32[]{:S(2)}) collective-permute-start(f32[64,128]{1,0:T(8,128)S(1)} %add.49), channel_id=1, source_target_pairs={{0,2},{2,0},{1,3},{3,1},{4,6},{6,4},{5,7},{7,5},{8,10},{10,8},{9,1... | collective-permute-start | bytes 98312 | tf_op jit(solution)/shard_map/ppermute | solution.py:313
  60.6 4.1 %collective-permute-start.5 = (f32[80,128]{1,0:T(8,128)S(1)}, f32[80,128]{1,0:T(8,128)S(1)}, u32[]{:S(2)}, u32[]{:S(2)}) collective-permute-start(f32[80,128]{1,0:T(8,128)S(1)} %pad_maximum_fusion.3), channel_id=1, source_target_pairs={{0,4},{4,0},{8,12},{12,8},{1,5},{5,1},{9,13},{13,9},{2,6},{6,2},{1... | collective-permute-start | bytes 122888 | tf_op jit(solution)/shard_map/ppermute | solution.py:313
  64.7 5.1 %collective-permute-start.6 = (f32[96,128]{1,0:T(8,128)S(1)}, f32[96,128]{1,0:T(8,128)S(1)}, u32[]{:S(2)}, u32[]{:S(2)}) collective-permute-start(f32[96,128]{1,0:T(8,128)S(1)} %pad_maximum_fusion.2), channel_id=1, source_target_pairs={{0,8},{4,12},{8,0},{12,4},{1,9},{5,13},{9,1},{13,5},{2,10},{6,14},... | collective-permute-start | bytes 147464 | tf_op jit(solution)/shard_map/ppermute | solution.py:313
  69.7 0.6 copy-start.2

commit v2 on v0

--- a/solution.py
+++ b/solution.py
@@ -1,18 +1,496 @@
+import functools
 import math
 
 import jax
 import jax.numpy as jnp
 from jax import lax
+from jax.experimental import pallas as pl
+from jax.experimental.pallas import tpu as pltpu
 from jax.sharding import PartitionSpec as P
 
 STEPS = 4
 SWEEPS = 3
-
+CHANNELS = 64
+TAPS = 18
+COEFS = 32
+LANES = 128
+HALF = LANES // 2
+MARGIN = 16
+PACKED = 16
 
 time_step = 0.1
 viscosity = 0.2
 correction_gain = 0.25
 gradient_gain = 10.0
+
+GELU_SCALE = math.sqrt(2.0 / math.pi)
+GELU_CUBE = 0.044715
+
+
+def shift(plane, row, col):
+    if row:
+        plane = pltpu.roll(plane, (-row) % plane.shape[0], 0)
+    if col:
+        plane = pltpu.roll(plane, (-col) % plane.shape[1], 1)
+    return plane
+
+
+def swap_halves(x):
+    return pltpu.roll(x, HALF, 1)
+
+
+def neighbours(p):
+    return (shift(p, 1, 0) + shift(p, -1, 0)) + (shift(p, 0, 1) + shift(p, 0, -1))
+
+
+def dot(a, b):
+    return jnp.dot(a, b, preferred_element_type=jnp.float32)
+
+
+def dot_cells(a, b):
+    return lax.dot_general(a, b, (((1,), (1,)), ((), ())), preferred_element_type=jnp.float32)
+
+
+def gelu_half(h, with_slope):
+    a, b = 2.0 * GELU_SCALE, 8.0 * GELU_SCALE * GELU_CUBE
+    square = h * h
+    t = jnp.tanh(h * (a + b * square))
+    e = 1.0 + t
+    act = h * e
+    if not with_slope:
+        return act, None
+    return act, e * (1.0 + (h * (1.0 - t)) * (a + (3.0 * b) * square))
+
+
+def pick_taps(shape, place_dim):
+    place = lax.broadcasted_iota(jnp.int32, shape, place_dim)
+    tap = lax.broadcasted_iota(jnp.int32, shape, 1 - place_dim)
+    row, col = (tap // 4) % 4, tap % 4
+    wanted = (tap // 16) * 9 + row * 3 + col
+    return jnp.where((place == wanted) & (row < 3) & (col < 3), 1.0, 0.0)
+
+
+def kernel(
+    core,
+    factor,
+    gathered,
+    w1_in,
+    w2_in,
+    w3_in,
+    velocity,
+    grads,
+    s_all,
+    up,
+    qs,
+    uu,
+    ub,
+    qp,
+    bq,
+    x_all,
+    a1_all,
+    a2_all,
+    g1_all,
+    g2_all,
+    cf,
+    w1,
+    w1t,
+    w2,
+    w2t,
+    w3,
+    w3t,
+    g_first,
+    g_second,
+    g_third,
+):
+    f32, bf16 = jnp.float32, jnp.bfloat16
+    height = 2 * PACKED
+    z = lax.axis_index("rows")
+    left = lax.broadcasted_iota(jnp.int32, (PACKED, LANES), 1) < HALF
+
+    lane = lax.broadcasted_iota(jnp.int32, (8, LANES), 1)
+    column = jnp.where(lane < LANES - 32, lane, lane - LANES) + (core * z - MARGIN)
+    own = (column >= 0) & (column < LANES)
+    amount = lax.rem(MARGIN - core * z + 4 * LANES, LANES)
+    for i, k in enumerate((0, 2, 1, 3)):
+        row = pl.multiple_of(8 * (z ^ k), 8)
+        for c in range(4):
+            mine = pltpu.roll(gathered[i, 0, c], amount, 1)
+            other = pltpu.roll(gathered[i, 1, c], amount, 1)
+            tile = jnp.where(own, mine, other)
+            if c < 2:
+                s_all[0, c, pl.ds(row, 8), :] = tile
+            else:
+                up[c - 2, pl.ds(row, 8), :] = tile
+
+    spread = dot(pick_taps((32, TAPS), 1).astype(bf16), w1_in[...])
+    w1[...] = (0.5 * spread.T).astype(bf16)
+    w1t[...] = spread.astype(bf16)
+    wide = w2_in[...].astype(f32)
+    w2[...] = (0.5 * wide).astype(bf16)
+    w2t[...] = (0.5 * wide.T).astype(bf16)
+    wide = w3_in[...].astype(f32)
+    w3t[...] = ((0.5 * correction_gain) * wide.T).astype(bf16)
+    for f in range(2):
+        rows = wide[16 * f : 16 * f + 16]
+        rows = correction_gain * (rows - jnp.mean(rows, axis=0, keepdims=True))
+        high = rows.astype(bf16)
+        w3[16 * f : 16 * f + 16, 0:64] = high
+        w3[16 * f : 16 * f + 16, 64:128] = (rows - high.astype(f32)).astype(bf16)
+
+    g_first[...] = jnp.zeros_like(g_first)
+    g_second[...] = jnp.zeros_like(g_second)
+    g_third[...] = jnp.zeros_like(g_third)
+
+    def pack(plane, part):
+        turned = swap_halves(plane)
+        if part == 0:
+            return jnp.where(left, plane[:PACKED], turned[PACKED:])
+        return jnp.where(left, turned[:PACKED], plane[PACKED:])
+
+    def unpack(inner, outer):
+        if outer is None:
+            return jnp.concatenate([inner, swap_halves(inner)], 0)
+        return jnp.concatenate(
+            [
+                jnp.where(left, inner, swap_halves(outer)),
+                jnp.where(left, swap_halves(inner), outer),
+            ],
+            0,
+        )
+
+    def stencil(step, part, c, ah, r):
+        at = 8 * (r + 2 * ah)
+        return uu[step, part, c, at : at + 8, :]
+
+    def forward(step, last):
+        s = [s_all[step, c] for c in range(2)]
+        for c in range(2):
+            for al in range(2):
+                line = shift(s[c], al, 0)
+                for b in range(4):
+                    plane = shift(line, 0, b - 1)
+                    for part in range(2):
+                        uu[step, part, c, pl.ds(8 + 4 * al + b, PACKED, stride=8), :] = pack(
+                            plane, part
+                        )
+            for part in range(2):
+                uu[step, part, c, 0:8, :] = swap_halves(uu[step, part, c, 128:136, :])
+                uu[step, part, c, 136:144, :] = swap_halves(uu[step, part, c, 8:16, :])
+
+        for part in range(2):
+            keep = part == 0 or last
+            slot = step if part == 0 else STEPS
+            x = jnp.concatenate(
+                [
+                    jnp.concatenate(
+                        [stencil(step, part, c, ah, r) for c in range(2) for ah in range(2)], 0
+                    ).astype(bf16)
+                    for r in range(PACKED)
+                ],
+                1,
+            )
+            act, slope = gelu_half(dot(w1[...], x), keep)
+            act = act.astype(bf16)
+            if part == 0:
+                x_all[slot] = x
+                a1_all[slot] = act
+            if keep:
+                g1_all[slot] = slope
+            act, slope = gelu_half(dot(w2[...], act), keep)
+            act = act.astype(bf16)
+            if part == 0:
+                a2_all[slot] = act
+            if keep:
+                g2_all[slot] = slope
+            out = dot(w3[...], jnp.concatenate([act, act], 0))
+            if keep:
+                cf[slot] = out
+            for r in range(PACKED):
+                weight = out[:, r * LANES : (r + 1) * LANES]
+                for c in range(2):
+                    lower = stencil(step, part, c, 0, r)
+                    upper = stencil(step, part, c, 1, r)
+                    for f in range(2):
+                        qp[part, 2 * f + c, 8 * r : 8 * r + 8, :] = (
+                            weight[16 * f : 16 * f + 8] * lower
+                            + weight[16 * f + 8 : 16 * f + 16] * upper
+                        )
+
+        def reduced(part, which):
+            terms = [qp[part, which, pl.ds(j, PACKED, stride=8), :] for j in range(8)]
+            while len(terms) > 1:
+                terms = [a + b for a, b in zip(terms[::2], terms[1::2])]
+            return terms[0]
+
+        moved = []
+        near = [s[0] + shift(s[0], 1, 0), s[1] + shift(s[1], 0, 1)]
+        for c in range(2):
+            flux = []
+            for f in range(2):
+                mean = 0.5 * (s[c] + (shift(s[c], 1, 0) if f == 0 else shift(s[c], 0, 1)))
+                q = mean + unpack(reduced(0, 2 * f + c), reduced(1, 2 * f + c))
+                qs[step, 2 * f + c] = q
+                flux.append((0.5 * near[f]) * q)
+            transport = (flux[0] - shift(flux[0], -1, 0)) + (flux[1] - shift(flux[1], 0, -1))
+            moved.append(
+                s[c]
+                - time_step * transport
+                + time_step * viscosity * (neighbours(s[c]) - 4.0 * s[c])
+            )
+        source = 0.5 * (
+            (shift(moved[0], 1, 0) - shift(moved[0], -1, 0))
+            + (shift(moved[1], 0, 1) - shift(moved[1], 0, -1))
+        )
+        pressure = -0.25 * source
+        for _ in range(SWEEPS - 1):
+            pressure = 0.25 * (neighbours(pressure) - source)
+        s_all[step + 1, 0] = moved[0] - 0.5 * (shift(pressure, 1, 0) - shift(pressure, -1, 0))
+        s_all[step + 1, 1] = moved[1] - 0.5 * (shift(pressure, 0, 1) - shift(pressure, 0, -1))
+
+    def backward(step, full):
+        u = [up[c] for c in range(2)]
+        s = [s_all[step, c] for c in range(2)]
+        p_bar = 0.5 * (
+            (shift(u[0], 1, 0) - shift(u[0], -1, 0)) + (shift(u[1], 0, 1) - shift(u[1], 0, -1))
+        )
+        source_bar = -0.25 * p_bar
+        for _ in range(SWEEPS - 1):
+            p_bar = 0.25 * neighbours(p_bar)
+            source_bar = source_bar - 0.25 * p_bar
+        half = 0.5 * source_bar
+        m_bar = [
+            u[0] + (shift(half, -1, 0) - shift(half, 1, 0)),
+            u[1] + (shift(half, 0, -1) - shift(half, 0, 1)),
+        ]
+        speed = [0.5 * (s[0] + shift(s[0], 1, 0)), 0.5 * (s[1] + shift(s[1], 0, 1))]
+        box = []
+        for c in range(2):
+            pair = s[c] + shift(s[c], 0, 1)
+            line = shift(pair, 0, -1) + shift(pair, 0, 1)
+            pair = line + shift(line, 1, 0)
+            box.append((1.0 / 16.0) * (shift(pair, -1, 0) + shift(pair, 1, 0)))
+        speed_bar = [None, None]
+        s_bar = []
+        mean = [None, None]
+        parts = (0, 1) if full else (0,)
+        for c in range(2):
+            flux_bar = [
+                time_step * (shift(m_bar[c], 1, 0) - m_bar[c]),
+                time_step * (shift(m_bar[c], 0, 1) - m_bar[c]),
+            ]
+            total = m_bar[c] + time_step * viscosity * (neighbours(m_bar[c]) - 4.0 * m_bar[c])
+            for f in range(2):
+                q_bar = speed[f] * flux_bar[f]
+                for part in parts:
+                    bq[part, 2 * f + c] = pack(q_bar, part)
+                term = q_bar * box[c]
+                mean[f] = term if c == 0 else mean[f] + term
+                term = qs[step, 2 * f + c] * flux_bar[f]
+                speed_bar[f] = term if c == 0 else speed_bar[f] + term
+                half = 0.5 * q_bar
+                total = total + (half + (shift(half, -1, 0) if f == 0 else shift(half, 0, -1)))
+            s_bar.append(total)
+        half = 0.5 * speed_bar[0]
+        s_bar[0] = s_bar[0] + (half + shift(half, -1, 0))
+        half = 0.5 * speed_bar[1]
+        s_bar[1] = s_bar[1] + (half + shift(half, 0, -1))
+        for f in range(2):
+            for part in parts:
+                bq[part, 4 + f] = pack(mean[f], part)
+
+        for part in parts:
+            slot = step if part == 0 else STEPS
+
+            def spread_row(which, r):
+                return jnp.broadcast_to(bq[part, which, r : r + 1, :], (8, LANES))
+
+            third = []
+            for r in range(PACKED):
+                pieces = []
+                for f in range(2):
+                    q0, q1, m = (spread_row(w, r) for w in (2 * f, 2 * f + 1, 4 + f))
+                    for ah in range(2):
+                        pieces.append(
+                            (q0 * stencil(step, part, 0, ah, r) + q1 * stencil(step, part, 1, ah, r))
+                            - m
+                        )
+                third.append(jnp.concatenate(pieces, 0).astype(bf16))
+            third = jnp.concatenate(third, 1)
+            second = (dot(w3t[...], third) * g2_all[slot]).astype(bf16)
+            first = (dot(w2t[...], second) * g1_all[slot]).astype(bf16)
+            if part == 0:
+                cells = lax.broadcasted_iota(jnp.int32, (1, PACKED * LANES), 1) % HALF
+                inside = (cells >= MARGIN) & (cells < MARGIN + core)
+                zero = jnp.zeros((), bf16)
+                g_third[...] += dot_cells(jnp.where(inside, third, zero), a2_all[slot])
+                g_second[...] += dot_cells(jnp.where(inside, second, zero), a1_all[slot])
+                g_first[...] += dot_cells(jnp.where(inside, first, zero), x_all[slot])
+            out = dot(w1t[...], first)
+
+            y = {}
+            for r in range(PACKED):
+                lanes = slice(r * LANES, (r + 1) * LANES)
+                for c in range(2):
+                    q0, q1 = spread_row(c, r), spread_row(2 + c, r)
+                    for ah in range(2):
+                        y[c, ah, r] = (
+                            cf[slot, 8 * ah : 8 * ah + 8, lanes] * q0
+                            + cf[slot, 16 + 8 * ah : 24 + 8 * ah, lanes] * q1
+                        ) + out[16 * c + 8 * ah : 16 * c + 8 * ah + 8, lanes]
+            for c in range(2):
+                rows = []
+                for m in range(PACKED):
+                    value = y[c, 0, m + 1] if m + 1 < PACKED else swap_halves(y[c, 0, 0])
+                    other = y[c, 1, m - 1] if m > 0 else swap_halves(y[c, 1, PACKED - 1])
+                    rows.append(value + other)
+                ub[part, c, 0:8, :] = swap_halves(rows[PACKED - 1])
+                for m in range(PACKED):
+                    ub[part, c, 8 + 8 * m : 16 + 8 * m, :] = rows[m]
+
+        for c in range(2):
+            total = s_bar[c]
+            for b in range(4):
+                planes = [
+                    ub[part, c, pl.ds(8 + b, PACKED, stride=8), :]
+                    + ub[part, c, pl.ds(4 + b, PACKED, stride=8), :]
+                    for part in parts
+                ]
+                plane = unpack(planes[0], planes[1] if full else None)
+                total = total + shift(plane, 0, 1 - b)
+            up[c] = total
+
+    for step in range(STEPS):
+        forward(step, step == STEPS - 1)
+    group = lax.broadcasted_iota(jnp.int32, (8, LANES), 1) // core
+    for c in range(2):
+        strip = jnp.zeros((8, LANES), f32)
+        for k in range(LANES // core):
+            rows = s_all[STEPS, c, 8 * k : 8 * k + 8, :]
+            strip = jnp.where(group == k, pltpu.roll(rows, (core * k - MARGIN) % LANES, 1), strip)
+        velocity[8 * c : 8 * c + 8, :] = strip
+    for step in reversed(range(STEPS)):
+        backward(step, step == STEPS - 1)
+    grads[:, 0:64] = factor * g_second[...]
+    first = lax.dot_general(
+        pick_taps((TAPS, 32), 0),
+        factor * g_first[...],
+        (((1,), (1,)), ((), ())),
+        precision=lax.Precision.HIGHEST,
+        preferred_element_type=f32,
+    )
+    grads[0:TAPS, 64:128] = first
+    grads[TAPS:32, 64:128] = jnp.zeros((32 - TAPS, CHANNELS), f32)
+    grads[32:64, 64:128] = (factor * correction_gain) * g_third[...]
+
+
+def strip_call(core, factor, gathered, weights):
+    cells = PACKED * LANES
+    f32, bf16 = jnp.float32, jnp.bfloat16
+    vmem = pl.BlockSpec(memory_space=pltpu.VMEM)
+    return pl.pallas_call(
+        functools.partial(kernel, core, factor),
+        out_shape=(
+            jax.ShapeDtypeStruct((16, LANES), f32),
+            jax.ShapeDtypeStruct((CHANNELS, LANES), f32),
+        ),
+        in_specs=[vmem] * 4,
+        out_specs=(vmem, vmem),
+        scratch_shapes=[
+            pltpu.VMEM((STEPS + 1, 2, 2 * PACKED, LANES), f32),
+            pltpu.VMEM((2, 2 * PACKED, LANES), f32),
+            pltpu.VMEM((STEPS, 4, 2 * PACKED, LANES), f32),
+            pltpu.VMEM((STEPS, 2, 2, 8 * (PACKED + 2), LANES), f32),
+            pltpu.VMEM((2, 2, 8 * (PACKED + 1), LANES), f32),
+            pltpu.VMEM((2, 4, 8 * PACKED, LANES), f32),
+            pltpu.VMEM((2, 6, PACKED, LANES), f32),
+            pltpu.VMEM((STEPS, 32, cells), bf16),
+            pltpu.VMEM((STEPS, CHANNELS, cells), bf16),
+            pltpu.VMEM((STEPS, CHANNELS, cells), bf16),
+            pltpu.VMEM((STEPS + 1, CHANNELS, cells), f32),
+            pltpu.VMEM((STEPS + 1, CHANNELS, cells), f32),
+            pltpu.VMEM((STEPS + 1, COEFS, cells), f32),
+            pltpu.VMEM((CHANNELS, 32), bf16),
+            pltpu.VMEM((32, CHANNELS), bf16),
+            pltpu.VMEM((CHANNELS, CHANNELS), bf16),
+            pltpu.VMEM((CHANNELS, CHANNELS), bf16),
+            pltpu.VMEM((COEFS, 2 * CHANNELS), bf16),
+            pltpu.VMEM((CHANNELS, COEFS), bf16),
+            pltpu.VMEM((CHANNELS, 32), f32),
+            pltpu.VMEM((CHANNELS, CHANNELS), f32),
+            pltpu.VMEM((COEFS, CHANNELS), f32),
+        ],
+        compiler_params=pltpu.CompilerParams(vmem_limit_bytes=48 * 1024 * 1024),
+    )(gathered, *weights)
+
+
+def finish(core, sent, got, tile, first, second, third):
+    z = lax.axis_index("rows")
+    group = lax.broadcasted_iota(jnp.int32, (8, LANES), 1) // core
+    for c in range(2):
+        total = jnp.zeros((8, LANES), jnp.float32)
+        for k, (ref, at) in enumerate(((sent, 64), (sent, 80), (got, 64), (got, 80))):
+            strip = ref[at + 8 * c : at + 8 * c + 8, :]
+            owner = z ^ k
+            turned = pltpu.roll(strip, lax.rem(core * (owner - z) + LANES, LANES), 1)
+            total = jnp.where(group == owner, turned, total)
+        tile[c] = total
+    grads = sent[0:64, :] + got[0:64, :]
+    first[...] = grads[0:TAPS, 64:]
+    second[...] = grads[:, 0:64]
+    third[...] = grads[32:, 64:]
+
+
+def finish_call(core, sent, got):
+    vmem = pl.BlockSpec(memory_space=pltpu.VMEM)
+    f32 = jnp.float32
+    return pl.pallas_call(
+        functools.partial(finish, core),
+        out_shape=(
+            jax.ShapeDtypeStruct((2, 8, LANES), f32),
+            jax.ShapeDtypeStruct((TAPS, CHANNELS), f32),
+            jax.ShapeDtypeStruct((CHANNELS, CHANNELS), f32),
+            jax.ShapeDtypeStruct((COEFS, CHANNELS), f32),
+        ),
+        in_specs=[vmem] * 2,
+        out_specs=(vmem,) * 4,
+        compiler_params=pltpu.CompilerParams(vmem_limit_bytes=8 * 1024 * 1024),
+    )(sent, got)
+
+
+def swap(x, axis, bit):
+    return lax.ppermute(x, axis, [(i, i ^ bit) for i in range(lax.axis_size(axis))])
+
+
+def strips(state, cotangent, first_weight, second_weight, third_weight):
+    row_count = lax.axis_size("rows")
+    block_count = lax.axis_size(("cols", "section"))
+    height = row_count * state.shape[1]
+    core = LANES // row_count
+    z = lax.axis_index("rows")
+
+    tile = jnp.concatenate([state, cotangent], 0)
+    pairs = []
+    for row in range(row_count):
+        step = 1 if row < row_count // 2 else block_count - 1
+        for block in range(block_count):
+            pairs.append((row * block_count + block, row * block_count + (block + step) % block_count))
+    held = jnp.stack([tile, swap(tile, "rows", 2)])
+    other = lax.ppermute(held, ("rows", "cols", "section"), pairs)
+    held = jnp.stack([held, other], 1)
+    held = jnp.concatenate([held, swap(held, "rows", 1)], 0)
+
+    factor = gradient_gain / math.sqrt(height * LANES * block_count)
+    velocity, grads = strip_call(
+        core, factor, held, (first_weight.T, second_weight, third_weight)
+    )
+
+    grads = grads + swap(grads, "section", 1)
+    grads = grads + swap(grads, "cols", 1)
+    sent = jnp.concatenate([grads, velocity], 0)
+    got = swap(sent, "rows", 1)
+    sent = jnp.concatenate([sent[:64] + got[:64], sent[64:], got[64:]], 0)
+    tile, first, second, third = finish_call(core, sent, swap(sent, "rows", 2))
+    return tile, first.T, second, third
 
 
 def with_halo(block, sides, width):
@@ -144,7 +622,7 @@
     )
 
 
-def neighbours(padded):
+def padded_neighbours(padded):
     return padded[2:, 1:-1] + padded[:-2, 1:-1] + padded[1:-1, 2:] + padded[1:-1, :-2]
 
 
@@ -171,7 +649,7 @@
     )
 
 
-def shards(state, cotangent, first_weight, second_weight, third_weight):
+def tiles(state, cotangent, first_weight, second_weight, third_weight):
     weights = (first_weight, second_weight, third_weight)
     current = state
     saved = []
@@ -186,7 +664,7 @@
             padded = with_halo(pressure, (("rows", 0), (("cols", "section"), 1)), 1)
             pressure_pads.append(padded)
             if sweep_number < SWEEPS - 1:
-                pressure = 0.25 * (neighbours(padded) - source)
+                pressure = 0.25 * (padded_neighbours(padded) - source)
         saved.append((extended, velocity_pad, pressure_pads))
         current = moved - pressure_gradient(pressure_pads[-1])
     upstream = cotangent
@@ -206,7 +684,7 @@
             pressure_grad = fold_rims(returned, 1)
             source_grad = source_grad - 0.25 * pressure_grad
             if sweep_number > 0:
-                pad_grad = jax.vjp(neighbours, pressure_pads[sweep_number - 1])[1](
+                pad_grad = jax.vjp(padded_neighbours, pressure_pads[sweep_number - 1])[1](
                     0.25 * pressure_grad
                 )[0]
         velocity_grad = jax.vjp(divergence, velocity_pad)[1](source_grad)[0]
@@ -228,8 +706,19 @@
 
 
 def solution(mesh):
+    def program(state, *rest):
+        fits = (
+            lax.axis_size("rows") == 4
+            and state.shape[1] == 8
+            and state.shape[2] == LANES
+            and lax.axis_size(("cols", "section")) >= 2
+            and lax.axis_size("section") == 2
+            and lax.axis_size("cols") == 2
+        )
+        return (strips if fits else tiles)(state, *rest)
+
     return jax.shard_map(
-        shards,
+        program,
         mesh=mesh,
         in_specs=(
             P(None, ("groups", "rows"), ("cols", "section")),

time: 429 us -> 42.7 us (0.10)
  starting transfers between devices: 206 us -> 11.4 us
  waiting for transfers between devices: 90.3 us -> 16.4 us
  blocking collectives: 62.7 us -> 0 us
  local copies, waits for them, and re-layouts: 33.4 us -> 1.38 us
  other arithmetic: 19.4 us -> 0.05 us
  matrix products: 12.7 us -> 0 us
  Pallas kernels: 0 us -> 12.6 us
    ppermute x156 -> x7, starting transfers between devices: 206 us -> 11.4 us  [the longest x6 11.4 us: swap(): lax.ppermute(x, axis, [(i, i ^ bit) for i in range(lax.axis_size(axis))])]
    ppermute x156 -> x7, waiting for transfers between devices: 90.3 us -> 16.4 us  [the longest x6 13 us: swap(): lax.ppermute(x, axis, [(i, i ^ bit) for i in range(lax.axis_size(axis))])]
    psum x1 -> x0, blocking collectives: 62.7 us -> none  [shards(): lax.psum((totals[0], totals[1], totals[2]), ('rows', 'cols', 'section'))]
    unnamed x244 -> x9, local copies, waits for them, and re-layouts: 24.2 us -> 1.38 us
    dot_general x34 -> x0, matrix products: 12.7 us -> none  [the longest x4 2.43 us: advance_back(): lax.dot_general(third_weight, coef_round, inner, preferred_element_type=j...]
    pallas_call x0 -> x2, Pallas kernels: none -> 12.6 us  [the longest x1 11.9 us: strip_call(): pl.pallas_call(functools.partial(kernel, core, factor), out_shape=(jax.Sh...]
    mul x51 -> x0, other arithmetic: 7.8 us -> none  [the longest x3 1.83 us: shards(): return (current, totals[0] * factor, totals[1] * factor, totals[2] * factor)]
  transfers between devices with their start and end apart: 156 -> 7, of which waited for: 68 -> 7; matrix products, arithmetic and copies ran while one was open for 2% -> 0% of each run, Pallas kernels for 0% -> 0%
where the time goes in v2:
time: 42.7 us; the launch traced here: 42.4 us
  waiting for transfers between devices  16.4 us (38%)
  Pallas kernels  12.6 us (30%)
  starting transfers between devices  11.4 us (27%)
  local copies, waits for them, and re-layouts  1.38 us (3%)
  between operations  0.71 us (2%)
    ppermute x6, waiting for transfers between devices, swap(): lax.ppermute(x, axis, [(i, i ^ bit) for i in range(lax.axis_size(axis))])  13 us
    pallas_call x1, Pallas kernels, strip_call(): pl.pallas_call(functools.partial(kernel, core, factor), out_shape=(jax.Sh...  11.9 us
    ppermute x6, starting transfers between devices, swap(): lax.ppermute(x, axis, [(i, i ^ bit) for i in range(lax.axis_size(axis))])  11.4 us
    ppermute x1, waiting for transfers between devices, strips(): other = lax.ppermute(held, ('rows', 'cols', 'section'), pairs)  3.33 us
    unnamed x9, local copies, waits for them, and re-layouts  1.38 us
  transfers between devices with their start and end apart: 7, of which 7 were waited for; matrix products, arithmetic and copies ran while one was open for 0% of the time, Pallas kernels for 0%

profile of v2, /device:TPU:0, one launch (start us, length us, event | category | flops | bytes accessed | tf_op | source)
XLA Modules:
  0.0 42.4 jit_solution(17071956112985918343)
XLA Ops:
  0.6 0.0 copy-start.3
  0.6 0.7 %constant_dynamic-update-slice_fusion.1 = f32[4,8,128]{2,1,0:T(8,128)S(1)} fusion(f32[2,8,128]{2,1,0:T(8,128)} %param.5), kind=kLoop, calls=%fused_computation.7 | loop fusion | bytes 16384
  1.3 0.0 copy-done.3
  1.3 4.0 %collective-permute-start = (f32[4,8,128]{2,1,0:T(8,128)S(1)}, f32[4,8,128]{2,1,0:T(8,128)S(1)}, u32[]{:S(2)}, u32[]{:S(2)}) collective-permute-start(f32[4,8,128]{2,1,0:T(8,128)S(1)} %constant_dynamic-update-slice_fusion), channel_id=1, source_target_pairs={{0,8},{4,12},{8,0},{12,4},{1,9},{5,13},{9,1},{13,5},{2,10},{6,14},... | collective-permute-start | bytes 49160 | tf_op jit(solution)/shard_map/ppermute | solution.py:461
  5.4 1.7 %collective-permute-done = f32[4,8,128]{2,1,0:T(8,128)S(1)} collective-permute-done((f32[4,8,128]{2,1,0:T(8,128)S(1)}, f32[4,8,128]{2,1,0:T(8,128)S(1)}, u32[]{:S(2)}, u32[]{:S(2)}) %collective-permute-start) | collective-permute-done | bytes 16416 | tf_op jit(solution)/shard_map/ppermute | solution.py:461
  7.1 0.0 collective-permute-start.1
  7.1 3.3 %collective-permute-done.1 = f32[2,4,8,128]{3,2,1,0:T(8,128)S(1)} collective-permute-done((f32[2,4,8,128]{3,2,1,0:T(8,128)S(1)}, f32[2,4,8,128]{3,2,1,0:T(8,128)S(1)}, u32[]{:S(2)}, u32[]{:S(2)}) %collective-permute-start.1) | collective-permute-done | bytes 32800 | tf_op jit(solution)/shard_map/ppermute | solution.py:478
  10.5 0.0 copy-start
  10.5 0.0 copy-start.1
  10.5 2.0 %collective-permute-start.2 = (f32[2,2,4,8,128]{4,3,2,1,0:T(8,128)S(1)}, f32[2,2,4,8,128]{4,3,2,1,0:T(8,128)S(1)}, u32[]{:S(2)}, u32[]{:S(2)}) collective-permute-start(f32[2,2,4,8,128]{4,3,2,1,0:T(8,128)S(1)} %pad_maximum_fusion.1), channel_id=1, source_target_pairs={{0,4},{4,0},{8,12},{12,8},{1,5},{5,1},{9,13},{13,9},{2,6},{6,2},{1... | collective-permute-start | bytes 196616 | tf_op jit(solution)/shard_map/ppermute | solution.py:461
  12.4 2.4 %collective-permute-done.2 = f32[2,2,4,8,128]{4,3,2,1,0:T(8,128)S(1)} collective-permute-done((f32[2,2,4,8,128]{4,3,2,1,0:T(8,128)S(1)}, f32[2,2,4,8,128]{4,3,2,1,0:T(8,128)S(1)}, u32[]{:S(2)}, u32[]{:S(2)}) %collective-permute-start.2) | collective-permute-done | bytes 65568 | tf_op jit(solution)/shard_map/ppermute | solution.py:461
  14.8 0.0 copy-start.2
  14.8 0.0 copy-done
  14.8 0.0 copy-done.1
  14.8 0.7 %copy-done.2 = bf16[64,18]{0,1:T(8,128)(2,1)S(1)} copy-done((bf16[64,18]{0,1:T(8,128)(2,1)S(1)}, bf16[64,18]{0,1:T(8,128)(2,1)}, u32[]{:S(2)}) %copy-start.2) | copy-done | bytes 2328
  15.5 11.9 %shard_map.84 = (f32[16,128]{1,0:T(8,128)S(1)}, f32[64,128]{1,0:T(8,128)S(1)}) custom-call(f32[4,2,4,8,128]{4,3,2,1,0:T(8,128)S(1)} %pad_maximum_fusion.gathered, bf16[18,64]{1,0:T(8,128)(2,1)S(1)} %bitcast.9, bf16[64,64]{1,0:T(8,128)(2,1)S(1)} %copy-done, bf16[32,64]{1,0:T(8,128)(2,1)S(1)} %copy-done.1), custom_call_target="tpu_custom_call" | custom-call | tf_op jit(solution)/shard_map/pallas_call | solution.py:390
  27.4 0.1 collective-permute-start.3
  27.5 1.2 %collective-permute-done.3 = f32[64,128]{1,0:T(8,128)S(1)} collective-permute-done((f32[64,128]{1,0:T(8,128)S(1)}, f32[64,128]{1,0:T(8,128)S(1)}, u32[]{:S(2)}, u32[]{:S(2)}) %collective-permute-start.3) | collective-permute-done | bytes 32800 | tf_op jit(solution)/shard_map/ppermute | solution.py:461
  28.7 1.9 %collective-permute-start.4 = (f32[64,128]{1,0:T(8,128)S(1)}, f32[64,128]{1,0:T(8,128)S(1)}, u32[]{:S(2)}, u32[]{:S(2)}) collective-permute-start(f32[64,128]{1,0:T(8,128)S(1)} %add.9), channel_id=1, source_target_pairs={{0,2},{2,0},{1,3},{3,1},{4,6},{6,4},{5,7},{7,5},{8,10},{10,8},{9,1... | collective-permute-start | bytes 98312 | tf_op jit(solution)/shard_map/ppermute | solution.py:461
  30.5 2.0 %collective-permute-done.4 = f32[64,128]{1,0:T(8,128)S(1)} collective-permute-done((f32[64,128]{1,0:T(8,128)S(1)}, f32[64,128]{1,0:T(8,128)S(1)}, u32[]{:S(2)}, u32[]{:S(2)}) %collective-permute-start.4) | collective-permute-done | bytes 32800 | tf_op jit(solution)/shard_map/ppermute | solution.py:461
  32.6 2.0 %collective-permute-start.5 = (f32[80,128]{1,0:T(8,128)S(1)}, f32[80,128]{1,0:T(8,128)S(1)}, u32[]{:S(2)}, u32[]{:S(2)}) collective-permute-start(f32[80,128]{1,0:T(8,128)S(1)} %pad_maximum_fusion.3), channel_id=1, source_target_pairs={{0,4},{4,0},{8,12},{12,8},{1,5},{5,1},{9,13},{13,9},{2,6},{6,2},{1... | collective-permute-start | bytes 122888 | tf_op jit(solution)/shard_map/ppermute | solution.py:461
  34.6 2.1 %collective-permute-done.5 = f32[80,128]{1,0:T(8,128)S(1)} collective-permute-done((f32[80,128]{1,0:T(8,128)S(1)}, f32[80,128]{1,0:T(8,128)S(1)}, u32[]{:S(2)}, u32[]{:S(2)}) %collective-permute-start.5) | collective-permute-done | bytes 40992 | tf_op jit(solution)/shard_map/ppermute | solution.py:461
  36.7 1.4 %collective-permute-start.6 = (f32[96,128]{1,0:T(8,128)S(1)}, f32[96,128]{1,0:T(8,128)S(1)}, u32[]{:S(2)}, u32[]{:S(2)}) collective-permute-start(f32[96,128]{1,0:T(8,128)S(1)} %pad_maximum_fusion.2.sent), channel_id=1, source_target_pairs={{0,8},{4,12},{8,0},{12,4},{1,9},{5,13},{9,1},{13,5},{2,10},{6,14},... | collective-permute-start | bytes 147464 | tf_op jit(solution)/shard_map/ppermute | solution.py:461
  38.1 3.6 %collective-permute-done.6.got = f32[96,128]{1,0:T(8,128)S(1)} collective-permute-done((f32[96,128]{1,0:T(8,128)S(1)}, f32[96,128]{1,0:T(8,128)S(1)}, u32[]{:S(2)}, u32[]{:S(2)}) %collective-permute-start.6) | collective-permute-done | bytes 49184 | tf_op jit(solution)/shard_map/ppermute | solution.py:461
  41.7 0.7 %shard_map.85 = (f32[2,8,128]{2,1,0:T(8,128)}, f32[18,64]{1,0:T(8,128)}, f32[64,64]{1,0:T(8,128)}, f32[32,64]{1,0:T(8,128)}) custom-call(f32[96,128]{1,0:T(8,128)S(1)} %pad_maximum_fusion.2.sent, f32[96,128]{1,0:T(8,128)S(1)} %collective-permute-done.6.got), custom_call_target="tpu_custom_call" | custom-call | tf_op jit(solution)/shard_map/pallas_call | solution.py:446
  (10 shorter events, 0.1 us)
Async XLA Ops:
  0.6 0.7 %copy-start.3 = (f32[2,8,128]{2,1,0:T(8,128)S(1)}, f32[2,8,128]{2,1,0:T(8,128)}, u32[]{:S(2)}) copy-start(f32[2,8,128]{2,1,0:T(8,128)} %param.6) | copy-start | bytes 24580
  1.3 5.8 %collective-permute-start = (f32[4,8,128]{2,1,0:T(8,128)S(1)}, f32[4,8,128]{2,1,0:T(8,128)S(1)}, u32[]{:S(2)}, u32[]{:S(2)}) collective-permute-start(f32[4,8,128]{2,1,0:T(8,128)S(1)} %constant_dynamic-update-slice_fusion), channel_id=1, source_target_pairs={{0,8},{4,12},{8,0},{12,4},{1,9},{5,13},{9,1},{13,5},{2,10},{6,14},... | collective-permute-start | bytes 49160 | tf_op jit(solution)/shard_map/ppermute | solution.py:461
  7.1 3.3 %collective-permute-start.1 = (f32[2,4,8,128]{3,2,1,0:T(8,128)S(1)}, f32[2,4,8,128]{3,2,1,0:T(8,128)S(1)}, u32[]{:S(2)}, u32[]{:S(2)}) collective-permute-start(f32[2,4,8,128]{3,2,1,0:T(8,128)S(1)} %get-tuple-element.17), channel_id=1, source_target_pairs={{0,1},{1,2},{2,3},{3,0},{4,5},{5,6},{6,7},{7,4},{8,11},{9,8},{10,9... | collective-permute-start | bytes 98312 | tf_op jit(solution)/shard_map/ppermute | solution.py:478
  10.5 4.4 %copy-start = (bf16[64,64]{1,0:T(8,128)(2,1)S(1)}, bf16[64,64]{1,0:T(8,128)(2,1)}, u32[]{:S(2)}) copy-start(bf16[64,64]{1,0:T(8,128)(2,1)} %w2_in.1) | copy-start | bytes 24580
  10.5 4.4 %copy-start.1 = (bf16[32,64]{1,0:T(8,128)(2,1)S(1)}, bf16[32,64]{1,0:T(8,128)(2,1)}, u32[]{:S(2)}) copy-start(bf16[32,64]{1,0:T(8,128)(2,1)} %w3_in.1) | copy-start | bytes 12292
  10.5 4.3 %collective-permute-start.2 = (f32[2,2,4,8,128]{4,3,2,1,0:T(8,128)S(1)}, f32[2,2,4,8,128]{4,3,2,1,0:T(8,128)S(1)}, u32[]{:S(2)}, u32[]{:S(2)}) collective-permute-start(f32[2,2,4,8,128]{4,3,2,1,0:T(8,128)S(1)} %pad_maximum_fusion.1), channel_id=1, source_target_pairs={{0,4},{4,0},{8,12},{12,8},{1,5},{5,1},{9,13},{13,9},{2,6},{6,2},{1... | collective-permute-start | bytes 196616 | tf_op jit(solution)/shard_map/ppermute | solution.py:461
  14.8 0.7 %copy-start.2 = (bf16[64,18]{0,1:T(8,128)(2,1)S(1)}, bf16[64,18]{0,1:T(8,128)(2,1)}, u32[]{:S(2)}) copy-start(bf16[64,18]{0,1:T(8,128)(2,1)} %param.7) | copy-start | bytes 6916
  27.4 1.3 %collective-permute-start.3 = (f32[64,128]{1,0:T(8,128)S(1)}, f32[64,128]{1,0:T(8,128)S(1)}, u32[]{:S(2)}, u32[]{:S(2)}) collective-permute-start(f32[64,128]{1,0:T(8,128)S(1)} %get-tuple-element.10), channel_id=1, source_target_pairs={{0,1},{1,0},{2,3},{3,2},{4,5},{5,4},{6,7},{7,6},{8,9},{9,8},{10,11... | collective-permute-start | bytes 98312 | tf_op jit(solution)/shard_map/ppermute | solution.py:461
  28.7 3.9 %collective-permute-start.4 = (f32[64,128]{1,0:T(8,128)S(1)}, f32[64,128]{1,0:T(8,128)S(1)}, u32[]{:S(2)}, u32[]{:S(2)}) collective-permute-start(f32[64,128]{1,0:T(8,128)S(1)} %add.9), channel_id=1, source_target_pairs={{0,2},{2,0},{1,3},{3,1},{4,6},{6,4},{5,7},{7,5},{8,10},{10,8},{9,1... | collective-permute-start | bytes 98312 | tf_op jit(solution)/shard_map/ppermute | solution.py:461
  32.6 4.1 %collective-permute-start.5 = (f32[80,128]{1,0:T(8,128)S(1)}, f32[80,128]{1,0:T(8,128)S(1)}, u32[]{:S(2)}, u32[]{:S(2)}) collective-permute-start(f32[80,128]{1,0:T(8,128)S(1)} %pad_maximum_fusion.3), channel_id=1, source_target_pairs={{0,4},{4,0},{8,12},{12,8},{1,5},{5,1},{9,13},{13,9},{2,6},{6,2},{1... | collective-permute-start | bytes 122888 | tf_op jit(solution)/shard_map/ppermute | solution.py:461
  36.7 5.1 %collective-permute-start.6 = (f32[96,128]{1,0:T(8,128)S(1)}, f32[96,128]{1,0:T(8,128)S(1)}, u32[]{:S(2)}, u32[]{:S(2)}) collective-permute-start(f32[96,128]{1,0:T(8,128)S(1)} %pad_maximum_fusion.2.sent), channel_id=1, source_target_pairs={{0,8},{4,12},{8,0},{12,4},{1,9},{5,13},{9,1},{13,5},{2,10},{6,14},... | collective-permute-start | bytes 147464 | tf_op jit(solution)/shard_map/ppermute | solution.py:461

commit v3 on v2

--- a/solution.py
+++ b/solution.py
@@ -15,8 +15,8 @@
 COEFS = 32
 LANES = 128
 HALF = LANES // 2
-MARGIN = 16
 PACKED = 16
+SIDE = 32
 
 time_step = 0.1
 viscosity = 0.2
@@ -41,6 +41,14 @@
 
 def neighbours(p):
     return (shift(p, 1, 0) + shift(p, -1, 0)) + (shift(p, 0, 1) + shift(p, 0, -1))
+
+
+def pressure_of(source):
+    one = shift(source, 0, 1) + shift(source, 0, -1)
+    two = shift(source, 0, 2) + shift(source, 0, -2)
+    mixed = 4.0 * source + 2.0 * one
+    rows = (shift(mixed, 1, 0) + shift(mixed, -1, 0)) + (shift(source, 2, 0) + shift(source, -2, 0))
+    return (-1.0 / 64.0) * (((20.0 * source + 4.0 * one) + two) + rows)
 
 
 def dot(a, b):
@@ -70,58 +78,8 @@
     return jnp.where((place == wanted) & (row < 3) & (col < 3), 1.0, 0.0)
 
 
-def kernel(
-    core,
-    factor,
-    gathered,
-    w1_in,
-    w2_in,
-    w3_in,
-    velocity,
-    grads,
-    s_all,
-    up,
-    qs,
-    uu,
-    ub,
-    qp,
-    bq,
-    x_all,
-    a1_all,
-    a2_all,
-    g1_all,
-    g2_all,
-    cf,
-    w1,
-    w1t,
-    w2,
-    w2t,
-    w3,
-    w3t,
-    g_first,
-    g_second,
-    g_third,
-):
+def prepare(w1_in, w2_in, w3_in, w1, w1t, w2, w2t, w3, w3t):
     f32, bf16 = jnp.float32, jnp.bfloat16
-    height = 2 * PACKED
-    z = lax.axis_index("rows")
-    left = lax.broadcasted_iota(jnp.int32, (PACKED, LANES), 1) < HALF
-
-    lane = lax.broadcasted_iota(jnp.int32, (8, LANES), 1)
-    column = jnp.where(lane < LANES - 32, lane, lane - LANES) + (core * z - MARGIN)
-    own = (column >= 0) & (column < LANES)
-    amount = lax.rem(MARGIN - core * z + 4 * LANES, LANES)
-    for i, k in enumerate((0, 2, 1, 3)):
-        row = pl.multiple_of(8 * (z ^ k), 8)
-        for c in range(4):
-            mine = pltpu.roll(gathered[i, 0, c], amount, 1)
-            other = pltpu.roll(gathered[i, 1, c], amount, 1)
-            tile = jnp.where(own, mine, other)
-            if c < 2:
-                s_all[0, c, pl.ds(row, 8), :] = tile
-            else:
-                up[c - 2, pl.ds(row, 8), :] = tile
-
     spread = dot(pick_taps((32, TAPS), 1).astype(bf16), w1_in[...])
     w1[...] = (0.5 * spread.T).astype(bf16)
     w1t[...] = spread.astype(bf16)
@@ -137,49 +95,121 @@
         w3[16 * f : 16 * f + 16, 0:64] = high
         w3[16 * f : 16 * f + 16, 64:128] = (rows - high.astype(f32)).astype(bf16)
 
-    g_first[...] = jnp.zeros_like(g_first)
-    g_second[...] = jnp.zeros_like(g_second)
-    g_third[...] = jnp.zeros_like(g_third)
+
+def prepare_call(w1_in, w2_in, w3_in):
+    vmem = pl.BlockSpec(memory_space=pltpu.VMEM)
+    shapes = ((CHANNELS, 32), (32, CHANNELS), (CHANNELS, CHANNELS), (CHANNELS, CHANNELS))
+    shapes += ((COEFS, 2 * CHANNELS), (CHANNELS, COEFS))
+    return pl.pallas_call(
+        prepare,
+        out_shape=tuple(jax.ShapeDtypeStruct(shape, jnp.bfloat16) for shape in shapes),
+        in_specs=[vmem] * 3,
+        out_specs=(vmem,) * 6,
+        compiler_params=pltpu.CompilerParams(vmem_limit_bytes=8 * 1024 * 1024),
+        cost_estimate=pl.CostEstimate(flops=1 << 20, bytes_accessed=1 << 16, transcendentals=0),
+    )(w1_in, w2_in, w3_in)
+
+
+def kernel(
+    factor,
+    own_near,
+    own_far,
+    other_near,
+    other_far,
+    w1,
+    w1t,
+    w2,
+    w2t,
+    w3,
+    w3t,
+    mine,
+    theirs,
+    grads,
+    s_wide,
+    s_all,
+    up,
+    qs,
+    uu,
+    ub,
+    qp,
+    bq,
+    x_all,
+    a1_all,
+    a2_all,
+    g1_all,
+    g2_all,
+    cf,
+):
+    f32, bf16 = jnp.float32, jnp.bfloat16
+    z = lax.axis_index("rows")
+    left = lax.broadcasted_iota(jnp.int32, (PACKED, LANES), 1) < HALF
+
+    lane = lax.broadcasted_iota(jnp.int32, (8, LANES), 1)
+    odd = (lane * 0 + z) % 2 == 1
+    for k in range(4):
+        row = pl.multiple_of(8 * (z ^ k), 8)
+        own, other = ((own_near, other_near), (own_far, other_far))[k // 2]
+        for c in range(4):
+            here = own[k % 2, c]
+            there = other[k % 2, c]
+            turned = swap_halves(here)
+            upper = jnp.where(odd, jnp.where(lane < HALF, turned, swap_halves(there)), here)
+            lower = jnp.where(odd, turned, there)
+            narrow = jnp.where(lane < LANES - SIDE, upper, lower)
+            if c < 2:
+                s_wide[c, pl.ds(row, 8), 0:LANES] = upper
+                s_wide[c, pl.ds(row, 8), LANES : 2 * LANES] = lower
+                s_all[0, c, pl.ds(row, 8), :] = narrow
+            else:
+                up[c - 2, pl.ds(row, 8), :] = narrow
 
     def pack(plane, part):
+        plane = plane[:, LANES:] if part == 2 else plane[:, :LANES]
         turned = swap_halves(plane)
         if part == 0:
             return jnp.where(left, plane[:PACKED], turned[PACKED:])
         return jnp.where(left, turned[:PACKED], plane[PACKED:])
 
-    def unpack(inner, outer):
-        if outer is None:
-            return jnp.concatenate([inner, swap_halves(inner)], 0)
-        return jnp.concatenate(
+    def unpack(pieces):
+        inner, outer = pieces[0], pieces[1]
+        plane = jnp.concatenate(
             [
                 jnp.where(left, inner, swap_halves(outer)),
                 jnp.where(left, swap_halves(inner), outer),
             ],
             0,
         )
+        if len(pieces) == 2:
+            return plane
+        lower = jnp.concatenate([swap_halves(pieces[2]), pieces[2]], 0)
+        return jnp.concatenate([plane, lower], 1)
 
     def stencil(step, part, c, ah, r):
         at = 8 * (r + 2 * ah)
         return uu[step, part, c, at : at + 8, :]
 
-    def forward(step, last):
-        s = [s_all[step, c] for c in range(2)]
+    def slot_of(step, part):
+        return step if part == 0 else STEPS - 1 + step
+
+    def forward(step):
+        parts = range(3) if step == 0 else range(2)
+        s = [s_wide[c] if step == 0 else s_all[step, c] for c in range(2)]
         for c in range(2):
             for al in range(2):
                 line = shift(s[c], al, 0)
                 for b in range(4):
                     plane = shift(line, 0, b - 1)
-                    for part in range(2):
+                    for part in parts:
                         uu[step, part, c, pl.ds(8 + 4 * al + b, PACKED, stride=8), :] = pack(
                             plane, part
                         )
-            for part in range(2):
+            for part in parts:
                 uu[step, part, c, 0:8, :] = swap_halves(uu[step, part, c, 128:136, :])
                 uu[step, part, c, 136:144, :] = swap_halves(uu[step, part, c, 8:16, :])
 
-        for part in range(2):
-            keep = part == 0 or last
-            slot = step if part == 0 else STEPS
+        for part in parts:
+            keep = part == 0 or step > 0
+            slot = slot_of(step, part)
             x = jnp.concatenate(
                 [
                     jnp.concatenate(
@@ -203,7 +233,7 @@
             if keep:
                 g2_all[slot] = slope
             out = dot(w3[...], jnp.concatenate([act, act], 0))
-            if keep:
+            if keep and step > 0:
                 cf[slot] = out
             for r in range(PACKED):
                 weight = out[:, r * LANES : (r + 1) * LANES]
@@ -228,8 +258,9 @@
             flux = []
             for f in range(2):
                 mean = 0.5 * (s[c] + (shift(s[c], 1, 0) if f == 0 else shift(s[c], 0, 1)))
-                q = mean + unpack(reduced(0, 2 * f + c), reduced(1, 2 * f + c))
-                qs[step, 2 * f + c] = q
+                q = mean + unpack([reduced(part, 2 * f + c) for part in parts])
+                if step > 0:
+                    qs[step, 2 * f + c] = q
                 flux.append((0.5 * near[f]) * q)
             transport = (flux[0] - shift(flux[0], -1, 0)) + (flux[1] - shift(flux[1], 0, -1))
             moved.append(
@@ -241,23 +272,26 @@
             (shift(moved[0], 1, 0) - shift(moved[0], -1, 0))
             + (shift(moved[1], 0, 1) - shift(moved[1], 0, -1))
         )
-        pressure = -0.25 * source
-        for _ in range(SWEEPS - 1):
-            pressure = 0.25 * (neighbours(pressure) - source)
-        s_all[step + 1, 0] = moved[0] - 0.5 * (shift(pressure, 1, 0) - shift(pressure, -1, 0))
-        s_all[step + 1, 1] = moved[1] - 0.5 * (shift(pressure, 0, 1) - shift(pressure, 0, -1))
-
-    def backward(step, full):
+        pressure = pressure_of(source)
+        after = [
+            moved[0] - 0.5 * (shift(pressure, 1, 0) - shift(pressure, -1, 0)),
+            moved[1] - 0.5 * (shift(pressure, 0, 1) - shift(pressure, 0, -1)),
+        ]
+        for c in range(2):
+            if step == 0:
+                column = lax.broadcasted_iota(jnp.int32, (2 * PACKED, LANES), 1)
+                after[c] = jnp.where(
+                    column < LANES - SIDE, after[c][:, :LANES], after[c][:, LANES:]
+                )
+            s_all[step + 1, c] = after[c]
+
+    def backward(step, total):
         u = [up[c] for c in range(2)]
         s = [s_all[step, c] for c in range(2)]
         p_bar = 0.5 * (
             (shift(u[0], 1, 0) - shift(u[0], -1, 0)) + (shift(u[1], 0, 1) - shift(u[1], 0, -1))
         )
-        source_bar = -0.25 * p_bar
-        for _ in range(SWEEPS - 1):
-            p_bar = 0.25 * neighbours(p_bar)
-            source_bar = source_bar - 0.25 * p_bar
-        half = 0.5 * source_bar
+        half = 0.5 * pressure_of(p_bar)
         m_bar = [
             u[0] + (shift(half, -1, 0) - shift(half, 1, 0)),
             u[1] + (shift(half, 0, -1) - shift(half, 0, 1)),
@@ -272,34 +306,38 @@
         speed_bar = [None, None]
         s_bar = []
         mean = [None, None]
-        parts = (0, 1) if full else (0,)
+        parts = range(2) if step > 0 else range(1)
         for c in range(2):
             flux_bar = [
                 time_step * (shift(m_bar[c], 1, 0) - m_bar[c]),
                 time_step * (shift(m_bar[c], 0, 1) - m_bar[c]),
             ]
-            total = m_bar[c] + time_step * viscosity * (neighbours(m_bar[c]) - 4.0 * m_bar[c])
+            if step > 0:
+                kept = m_bar[c] + time_step * viscosity * (neighbours(m_bar[c]) - 4.0 * m_bar[c])
             for f in range(2):
                 q_bar = speed[f] * flux_bar[f]
                 for part in parts:
                     bq[part, 2 * f + c] = pack(q_bar, part)
                 term = q_bar * box[c]
                 mean[f] = term if c == 0 else mean[f] + term
-                term = qs[step, 2 * f + c] * flux_bar[f]
-                speed_bar[f] = term if c == 0 else speed_bar[f] + term
-                half = 0.5 * q_bar
-                total = total + (half + (shift(half, -1, 0) if f == 0 else shift(half, 0, -1)))
-            s_bar.append(total)
-        half = 0.5 * speed_bar[0]
-        s_bar[0] = s_bar[0] + (half + shift(half, -1, 0))
-        half = 0.5 * speed_bar[1]
-        s_bar[1] = s_bar[1] + (half + shift(half, 0, -1))
+                if step > 0:
+                    term = qs[step, 2 * f + c] * flux_bar[f]
+                    speed_bar[f] = term if c == 0 else speed_bar[f] + term
+                    half = 0.5 * q_bar
+                    kept = kept + (half + (shift(half, -1, 0) if f == 0 else shift(half, 0, -1)))
+            if step > 0:
+                s_bar.append(kept)
+        if step > 0:
+            half = 0.5 * speed_bar[0]
+            s_bar[0] = s_bar[0] + (half + shift(half, -1, 0))
+            half = 0.5 * speed_bar[1]
+            s_bar[1] = s_bar[1] + (half + shift(half, 0, -1))
         for f in range(2):
             for part in parts:
                 bq[part, 4 + f] = pack(mean[f], part)
 
         for part in parts:
-            slot = step if part == 0 else STEPS
+            slot = slot_of(step, part)
 
             def spread_row(which, r):
                 return jnp.broadcast_to(bq[part, which, r : r + 1, :], (8, LANES))
@@ -319,12 +357,14 @@
             second = (dot(w3t[...], third) * g2_all[slot]).astype(bf16)
             first = (dot(w2t[...], second) * g1_all[slot]).astype(bf16)
             if part == 0:
-                cells = lax.broadcasted_iota(jnp.int32, (1, PACKED * LANES), 1) % HALF
-                inside = (cells >= MARGIN) & (cells < MARGIN + core)
-                zero = jnp.zeros((), bf16)
-                g_third[...] += dot_cells(jnp.where(inside, third, zero), a2_all[slot])
-                g_second[...] += dot_cells(jnp.where(inside, second, zero), a1_all[slot])
-                g_first[...] += dot_cells(jnp.where(inside, first, zero), x_all[slot])
+                terms = (
+                    dot_cells(first, x_all[slot]),
+                    dot_cells(second, a1_all[slot]),
+                    dot_cells(third, a2_all[slot]),
+                )
+                total = terms if total is None else tuple(a + b for a, b in zip(total, terms))
+            if step == 0:
+                return total
             out = dot(w1t[...], first)
 
             y = {}
@@ -341,120 +381,112 @@
                 rows = []
                 for m in range(PACKED):
                     value = y[c, 0, m + 1] if m + 1 < PACKED else swap_halves(y[c, 0, 0])
-                    other = y[c, 1, m - 1] if m > 0 else swap_halves(y[c, 1, PACKED - 1])
-                    rows.append(value + other)
+                    before = y[c, 1, m - 1] if m > 0 else swap_halves(y[c, 1, PACKED - 1])
+                    rows.append(value + before)
                 ub[part, c, 0:8, :] = swap_halves(rows[PACKED - 1])
                 for m in range(PACKED):
                     ub[part, c, 8 + 8 * m : 16 + 8 * m, :] = rows[m]
 
         for c in range(2):
-            total = s_bar[c]
+            kept = s_bar[c]
             for b in range(4):
-                planes = [
-                    ub[part, c, pl.ds(8 + b, PACKED, stride=8), :]
-                    + ub[part, c, pl.ds(4 + b, PACKED, stride=8), :]
-                    for part in parts
-                ]
-                plane = unpack(planes[0], planes[1] if full else None)
-                total = total + shift(plane, 0, 1 - b)
-            up[c] = total
+                plane = unpack(
+                    [
+                        ub[part, c, pl.ds(8 + b, PACKED, stride=8), :]
+                        + ub[part, c, pl.ds(4 + b, PACKED, stride=8), :]
+                        for part in parts
+                    ]
+                )
+                kept = kept + shift(plane, 0, 1 - b)
+            up[c] = kept
+        return total
 
     for step in range(STEPS):
-        forward(step, step == STEPS - 1)
-    group = lax.broadcasted_iota(jnp.int32, (8, LANES), 1) // core
-    for c in range(2):
-        strip = jnp.zeros((8, LANES), f32)
-        for k in range(LANES // core):
-            rows = s_all[STEPS, c, 8 * k : 8 * k + 8, :]
-            strip = jnp.where(group == k, pltpu.roll(rows, (core * k - MARGIN) % LANES, 1), strip)
-        velocity[8 * c : 8 * c + 8, :] = strip
+        forward(step)
+    for ref, tile in ((mine, z), (theirs, z ^ 1)):
+        first, second = (s_all[STEPS, c, pl.ds(pl.multiple_of(8 * tile, 8), 8), :] for c in range(2))
+        ref[...] = jnp.where(lane < HALF, first, swap_halves(second))
+    total = None
     for step in reversed(range(STEPS)):
-        backward(step, step == STEPS - 1)
-    grads[:, 0:64] = factor * g_second[...]
+        total = backward(step, total)
+    grads[:, 0:64] = factor * total[1]
     first = lax.dot_general(
         pick_taps((TAPS, 32), 0),
-        factor * g_first[...],
+        factor * total[0],
         (((1,), (1,)), ((), ())),
         precision=lax.Precision.HIGHEST,
         preferred_element_type=f32,
     )
     grads[0:TAPS, 64:128] = first
     grads[TAPS:32, 64:128] = jnp.zeros((32 - TAPS, CHANNELS), f32)
-    grads[32:64, 64:128] = (factor * correction_gain) * g_third[...]
-
-
-def strip_call(core, factor, gathered, weights):
+    grads[32:64, 64:128] = (factor * correction_gain) * total[2]
+
+
+def strip_call(factor, pieces, weights):
     cells = PACKED * LANES
     f32, bf16 = jnp.float32, jnp.bfloat16
     vmem = pl.BlockSpec(memory_space=pltpu.VMEM)
+    slots = 2 * STEPS - 1
     return pl.pallas_call(
-        functools.partial(kernel, core, factor),
+        functools.partial(kernel, factor),
         out_shape=(
-            jax.ShapeDtypeStruct((16, LANES), f32),
+            jax.ShapeDtypeStruct((8, LANES), f32),
+            jax.ShapeDtypeStruct((8, LANES), f32),
             jax.ShapeDtypeStruct((CHANNELS, LANES), f32),
         ),
-        in_specs=[vmem] * 4,
-        out_specs=(vmem, vmem),
+        in_specs=[vmem] * 10,
+        out_specs=(vmem,) * 3,
         scratch_shapes=[
+            pltpu.VMEM((2, 2 * PACKED, 2 * LANES), f32),
             pltpu.VMEM((STEPS + 1, 2, 2 * PACKED, LANES), f32),
             pltpu.VMEM((2, 2 * PACKED, LANES), f32),
             pltpu.VMEM((STEPS, 4, 2 * PACKED, LANES), f32),
-            pltpu.VMEM((STEPS, 2, 2, 8 * (PACKED + 2), LANES), f32),
+            pltpu.VMEM((STEPS, 3, 2, 8 * (PACKED + 2), LANES), f32),
             pltpu.VMEM((2, 2, 8 * (PACKED + 1), LANES), f32),
-            pltpu.VMEM((2, 4, 8 * PACKED, LANES), f32),
+            pltpu.VMEM((3, 4, 8 * PACKED, LANES), f32),
             pltpu.VMEM((2, 6, PACKED, LANES), f32),
             pltpu.VMEM((STEPS, 32, cells), bf16),
             pltpu.VMEM((STEPS, CHANNELS, cells), bf16),
             pltpu.VMEM((STEPS, CHANNELS, cells), bf16),
-            pltpu.VMEM((STEPS + 1, CHANNELS, cells), f32),
-            pltpu.VMEM((STEPS + 1, CHANNELS, cells), f32),
-            pltpu.VMEM((STEPS + 1, COEFS, cells), f32),
-            pltpu.VMEM((CHANNELS, 32), bf16),
-            pltpu.VMEM((32, CHANNELS), bf16),
-            pltpu.VMEM((CHANNELS, CHANNELS), bf16),
-            pltpu.VMEM((CHANNELS, CHANNELS), bf16),
-            pltpu.VMEM((COEFS, 2 * CHANNELS), bf16),
-            pltpu.VMEM((CHANNELS, COEFS), bf16),
-            pltpu.VMEM((CHANNELS, 32), f32),
-            pltpu.VMEM((CHANNELS, CHANNELS), f32),
-            pltpu.VMEM((COEFS, CHANNELS), f32),
+            pltpu.VMEM((slots, CHANNELS, cells), f32),
+            pltpu.VMEM((slots, CHANNELS, cells), f32),
+            pltpu.VMEM((slots, COEFS, cells), f32),
         ],
         compiler_params=pltpu.CompilerParams(vmem_limit_bytes=48 * 1024 * 1024),
-    )(gathered, *weights)
-
-
-def finish(core, sent, got, tile, first, second, third):
+    )(*pieces, *weights)
+
+
+def finish(sent, got, mine, tile, first, second, third):
     z = lax.axis_index("rows")
-    group = lax.broadcasted_iota(jnp.int32, (8, LANES), 1) // core
+    lane = lax.broadcasted_iota(jnp.int32, (8, LANES), 1)
+    odd = (lane * 0 + z) % 2 == 1
+    near, far = mine[...], got[64:72, :]
     for c in range(2):
-        total = jnp.zeros((8, LANES), jnp.float32)
-        for k, (ref, at) in enumerate(((sent, 64), (sent, 80), (got, 64), (got, 80))):
-            strip = ref[at + 8 * c : at + 8 * c + 8, :]
-            owner = z ^ k
-            turned = pltpu.roll(strip, lax.rem(core * (owner - z) + LANES, LANES), 1)
-            total = jnp.where(group == owner, turned, total)
-        tile[c] = total
+        here, there = (x if c == 0 else swap_halves(x) for x in (near, far))
+        low = jnp.where(odd, there, here)
+        high = jnp.where(odd, here, there)
+        tile[c] = jnp.where(lane < HALF, low, swap_halves(high))
     grads = sent[0:64, :] + got[0:64, :]
     first[...] = grads[0:TAPS, 64:]
     second[...] = grads[:, 0:64]
     third[...] = grads[32:, 64:]
 
 
-def finish_call(core, sent, got):
+def finish_call(sent, got, mine):
     vmem = pl.BlockSpec(memory_space=pltpu.VMEM)
     f32 = jnp.float32
     return pl.pallas_call(
-        functools.partial(finish, core),
+        finish,
         out_shape=(
             jax.ShapeDtypeStruct((2, 8, LANES), f32),
             jax.ShapeDtypeStruct((TAPS, CHANNELS), f32),
             jax.ShapeDtypeStruct((CHANNELS, CHANNELS), f32),
             jax.ShapeDtypeStruct((COEFS, CHANNELS), f32),
         ),
-        in_specs=[vmem] * 2,
+        in_specs=[vmem] * 3,
         out_specs=(vmem,) * 4,
         compiler_params=pltpu.CompilerParams(vmem_limit_bytes=8 * 1024 * 1024),
-    )(sent, got)
+    )(sent, got, mine)
 
 
 def swap(x, axis, bit):
@@ -464,32 +496,31 @@
 def strips(state, cotangent, first_weight, second_weight, third_weight):
     row_count = lax.axis_size("rows")
     block_count = lax.axis_size(("cols", "section"))
-    height = row_count * state.shape[1]
-    core = LANES // row_count
-    z = lax.axis_index("rows")
+    weights = prepare_call(first_weight.T, second_weight, third_weight)
+
+    def beside(flip):
+        pairs = []
+        for row in range(row_count):
+            step = 1 if row % 2 == 0 else block_count - 1
+            for block in range(block_count):
+                target = (row ^ flip) * block_count + (block + step) % block_count
+                pairs.append((row * block_count + block, target))
+        return pairs
 
     tile = jnp.concatenate([state, cotangent], 0)
-    pairs = []
-    for row in range(row_count):
-        step = 1 if row < row_count // 2 else block_count - 1
-        for block in range(block_count):
-            pairs.append((row * block_count + block, row * block_count + (block + step) % block_count))
-    held = jnp.stack([tile, swap(tile, "rows", 2)])
-    other = lax.ppermute(held, ("rows", "cols", "section"), pairs)
-    held = jnp.stack([held, other], 1)
-    held = jnp.concatenate([held, swap(held, "rows", 1)], 0)
-
-    factor = gradient_gain / math.sqrt(height * LANES * block_count)
-    velocity, grads = strip_call(
-        core, factor, held, (first_weight.T, second_weight, third_weight)
-    )
+    near = jnp.stack([tile, swap(tile, "rows", 1)])
+    everyone = ("rows", "cols", "section")
+    other_near = lax.ppermute(near, everyone, beside(0))
+    other_far = lax.ppermute(near, everyone, beside(2))
+    far = swap(near, "rows", 2)
+
+    factor = gradient_gain / math.sqrt(row_count * state.shape[1] * LANES * block_count)
+    mine, theirs, grads = strip_call(factor, (near, far, other_near, other_far), weights)
 
     grads = grads + swap(grads, "section", 1)
     grads = grads + swap(grads, "cols", 1)
-    sent = jnp.concatenate([grads, velocity], 0)
-    got = swap(sent, "rows", 1)
-    sent = jnp.concatenate([sent[:64] + got[:64], sent[64:], got[64:]], 0)
-    tile, first, second, third = finish_call(core, sent, swap(sent, "rows", 2))
+    sent = jnp.concatenate([grads, theirs], 0)
+    tile, first, second, third = finish_call(sent, swap(sent, "rows", 1), mine)
     return tile, first.T, second, third
 
 

time: 42.7 us -> 38.3 us (0.90)
  waiting for transfers between devices: 16.4 us -> 12.4 us
  Pallas kernels: 12.6 us -> 14.1 us
  starting transfers between devices: 11.4 us -> 10.2 us
  local copies, waits for them, and re-layouts: 1.38 us -> 0.72 us
    ppermute x6 -> x5, starting transfers between devices: 11.4 us -> 6.09 us  [swap(): lax.ppermute(x, axis, [(i, i ^ bit) for i in range(lax.axis_size(axis))])]
    ppermute x1 -> x2, starting transfers between devices: 0.01 us -> 4.13 us  [the longest x1 2.75 us: strips(): other_near = lax.ppermute(near, everyone, beside(0))]
    ppermute x1 -> x2, waiting for transfers between devices: 3.33 us -> 1.16 us  [the longest x1 0.68 us: strips(): other_near = lax.ppermute(near, everyone, beside(0))]
    ppermute x6 -> x5, waiting for transfers between devices: 13 us -> 11.2 us  [swap(): lax.ppermute(x, axis, [(i, i ^ bit) for i in range(lax.axis_size(axis))])]
    pallas_call x2 -> x3, Pallas kernels: 12.6 us -> 14.1 us  [the longest x1 13.1 us: strip_call(): pl.pallas_call(functools.partial(kernel, factor), out_shape=(jax.ShapeDty...]
    unnamed x9, local copies, waits for them, and re-layouts: 1.38 us -> 0.72 us
  transfers between devices with their start and end apart: 7 -> 7, of which waited for: 7 -> 7; matrix products, arithmetic and copies ran while one was open for 0% -> 0% of each run, Pallas kernels for 0% -> 1%
where the time goes in v3:
time: 38.3 us; the launch traced here: 38.1 us
  Pallas kernels  14.1 us (37%)
  waiting for transfers between devices  12.4 us (32%)
  starting transfers between devices  10.2 us (27%)
  local copies, waits for them, and re-layouts  0.72 us (2%)
  between operations  0.67 us (2%)
    pallas_call x1, Pallas kernels, strip_call(): pl.pallas_call(functools.partial(kernel, factor), out_shape=(jax.ShapeDty...  13.1 us
    ppermute x5, waiting for transfers between devices, swap(): lax.ppermute(x, axis, [(i, i ^ bit) for i in range(lax.axis_size(axis))])  11.2 us
    ppermute x5, starting transfers between devices, swap(): lax.ppermute(x, axis, [(i, i ^ bit) for i in range(lax.axis_size(axis))])  6.09 us
    ppermute x1, starting transfers between devices, strips(): other_near = lax.ppermute(near, everyone, beside(0))  2.75 us
    ppermute x1, starting transfers between devices, strips(): other_far = lax.ppermute(near, everyone, beside(2))  1.38 us
  transfers between devices with their start and end apart: 7, of which 7 were waited for; matrix products, arithmetic and copies ran while one was open for 0% of the time, Pallas kernels for 1%

profile of v3, /device:TPU:0, one launch (start us, length us, event | category | flops | bytes accessed | tf_op | source)
XLA Modules:
  0.0 38.1 jit_solution(9281950793964108237)
XLA Ops:
  0.6 0.0 copy-start.3
  0.6 0.7 %constant_dynamic-update-slice_fusion.1 = f32[4,8,128]{2,1,0:T(8,128)S(1)} fusion(f32[2,8,128]{2,1,0:T(8,128)} %param.5), kind=kLoop, calls=%fused_computation.3 | loop fusion | bytes 16384
  1.3 0.0 copy-done.3
  1.3 3.0 %collective-permute-start = (f32[4,8,128]{2,1,0:T(8,128)S(1)}, f32[4,8,128]{2,1,0:T(8,128)S(1)}, u32[]{:S(2)}, u32[]{:S(2)}) collective-permute-start(f32[4,8,128]{2,1,0:T(8,128)S(1)} %constant_dynamic-update-slice_fusion), channel_id=1, source_target_pairs={{0,4},{4,0},{8,12},{12,8},{1,5},{5,1},{9,13},{13,9},{2,6},{6,2},{1... | collective-permute-start | bytes 49160 | tf_op jit(solution)/shard_map/ppermute | solution.py:493
  4.4 1.7 %collective-permute-done = f32[4,8,128]{2,1,0:T(8,128)S(1)} collective-permute-done((f32[4,8,128]{2,1,0:T(8,128)S(1)}, f32[4,8,128]{2,1,0:T(8,128)S(1)}, u32[]{:S(2)}, u32[]{:S(2)}) %collective-permute-start) | collective-permute-done | bytes 16416 | tf_op jit(solution)/shard_map/ppermute | solution.py:493
  6.1 0.0 copy-start
  6.1 0.0 copy-start.1
  6.1 0.0 copy-start.2
  6.1 1.4 %collective-permute-start.3 = (f32[2,4,8,128]{3,2,1,0:T(8,128)S(1)}, f32[2,4,8,128]{3,2,1,0:T(8,128)S(1)}, u32[]{:S(2)}, u32[]{:S(2)}) collective-permute-start(f32[2,4,8,128]{3,2,1,0:T(8,128)S(1)} %pad_maximum_fusion.1.own_near), channel_id=1, source_target_pairs={{0,9},{1,10},{2,11},{3,8},{4,15},{5,12},{6,13},{7,14},{8,1},{9,2},... | collective-permute-start | bytes 98312 | tf_op jit(solution)/shard_map/ppermute | solution.py:514
  7.5 2.8 %collective-permute-start.2 = (f32[2,4,8,128]{3,2,1,0:T(8,128)S(1)}, f32[2,4,8,128]{3,2,1,0:T(8,128)S(1)}, u32[]{:S(2)}, u32[]{:S(2)}) collective-permute-start(f32[2,4,8,128]{3,2,1,0:T(8,128)S(1)} %pad_maximum_fusion.1.own_near), channel_id=1, source_target_pairs={{0,1},{1,2},{2,3},{3,0},{4,7},{5,4},{6,5},{7,6},{8,9},{9,10},{10,1... | collective-permute-start | bytes 98312 | tf_op jit(solution)/shard_map/ppermute | solution.py:513
  10.2 0.3 collective-permute-start.1
  10.6 0.0 copy-done
  10.6 0.0 copy-done.1
  10.6 0.0 copy-done.2
  10.6 0.2 shard_map.84
  10.8 0.5 %collective-permute-done.3.other_far = f32[2,4,8,128]{3,2,1,0:T(8,128)S(1)} collective-permute-done((f32[2,4,8,128]{3,2,1,0:T(8,128)S(1)}, f32[2,4,8,128]{3,2,1,0:T(8,128)S(1)}, u32[]{:S(2)}, u32[]{:S(2)}) %collective-permute-start.3) | collective-permute-done | bytes 32800 | tf_op jit(solution)/shard_map/ppermute | solution.py:514
  11.3 0.7 %collective-permute-done.2.other_near = f32[2,4,8,128]{3,2,1,0:T(8,128)S(1)} collective-permute-done((f32[2,4,8,128]{3,2,1,0:T(8,128)S(1)}, f32[2,4,8,128]{3,2,1,0:T(8,128)S(1)}, u32[]{:S(2)}, u32[]{:S(2)}) %collective-permute-start.2) | collective-permute-done | bytes 32800 | tf_op jit(solution)/shard_map/ppermute | solution.py:513
  12.0 3.1 %collective-permute-done.1.own_far = f32[2,4,8,128]{3,2,1,0:T(8,128)S(1)} collective-permute-done((f32[2,4,8,128]{3,2,1,0:T(8,128)S(1)}, f32[2,4,8,128]{3,2,1,0:T(8,128)S(1)}, u32[]{:S(2)}, u32[]{:S(2)}) %collective-permute-start.1) | collective-permute-done | bytes 32800 | tf_op jit(solution)/shard_map/ppermute | solution.py:493
  15.0 13.1 %shard_map.85 = (f32[8,128]{1,0:T(8,128)S(1)}, f32[8,128]{1,0:T(8,128)S(1)}, f32[64,128]{1,0:T(8,128)S(1)}) custom-call(f32[2,4,8,128]{3,2,1,0:T(8,128)S(1)} %pad_maximum_fusion.1.own_near, f32[2,4,8,128]{3,2,1,0:T(8,128)S(1)} %collective-permute-done.1.own_far, f32[2,4,8,128]{3,2,1,0:T(8,128)S(1)} %collective-permute-done.2.other_near, ...), custom_call_target="tpu_custom_call" | custom-call | tf_op jit(solution)/shard_map/pallas_call | solution.py:430
  28.1 0.0 collective-permute-start.4
  28.2 1.2 %collective-permute-done.4 = f32[64,128]{1,0:T(8,128)S(1)} collective-permute-done((f32[64,128]{1,0:T(8,128)S(1)}, f32[64,128]{1,0:T(8,128)S(1)}, u32[]{:S(2)}, u32[]{:S(2)}) %collective-permute-start.4) | collective-permute-done | bytes 32800 | tf_op jit(solution)/shard_map/ppermute | solution.py:493
  29.4 0.9 %collective-permute-start.5 = (f32[64,128]{1,0:T(8,128)S(1)}, f32[64,128]{1,0:T(8,128)S(1)}, u32[]{:S(2)}, u32[]{:S(2)}) collective-permute-start(f32[64,128]{1,0:T(8,128)S(1)} %add.6), channel_id=1, source_target_pairs={{0,2},{2,0},{1,3},{3,1},{4,6},{6,4},{5,7},{7,5},{8,10},{10,8},{9,1... | collective-permute-start | bytes 98312 | tf_op jit(solution)/shard_map/ppermute | solution.py:493
  30.3 3.0 %collective-permute-done.5 = f32[64,128]{1,0:T(8,128)S(1)} collective-permute-done((f32[64,128]{1,0:T(8,128)S(1)}, f32[64,128]{1,0:T(8,128)S(1)}, u32[]{:S(2)}, u32[]{:S(2)}) %collective-permute-start.5) | collective-permute-done | bytes 32800 | tf_op jit(solution)/shard_map/ppermute | solution.py:493
  33.3 1.8 %collective-permute-start.6 = (f32[72,128]{1,0:T(8,128)S(1)}, f32[72,128]{1,0:T(8,128)S(1)}, u32[]{:S(2)}, u32[]{:S(2)}) collective-permute-start(f32[72,128]{1,0:T(8,128)S(1)} %pad_maximum_fusion.sent), channel_id=1, source_target_pairs={{0,4},{4,0},{8,12},{12,8},{1,5},{5,1},{9,13},{13,9},{2,6},{6,2},{1... | collective-permute-start | bytes 110600 | tf_op jit(solution)/shard_map/ppermute | solution.py:493
  35.1 2.2 %collective-permute-done.6.got = f32[72,128]{1,0:T(8,128)S(1)} collective-permute-done((f32[72,128]{1,0:T(8,128)S(1)}, f32[72,128]{1,0:T(8,128)S(1)}, u32[]{:S(2)}, u32[]{:S(2)}) %collective-permute-start.6) | collective-permute-done | bytes 36896 | tf_op jit(solution)/shard_map/ppermute | solution.py:493
  37.3 0.8 %shard_map.86 = (f32[2,8,128]{2,1,0:T(8,128)}, f32[18,64]{1,0:T(8,128)}, f32[64,64]{1,0:T(8,128)}, f32[32,64]{1,0:T(8,128)}) custom-call(f32[72,128]{1,0:T(8,128)S(1)} %pad_maximum_fusion.sent, f32[72,128]{1,0:T(8,128)S(1)} %collective-permute-done.6.got, f32[8,128]{1,0:T(8,128)S(1)} %get-tuple-element.25.mine), custom_call_target="tpu_custom_call" | custom-call | tf_op jit(solution)/shard_map/pallas_call | solution.py:478
  (5 shorter events, 0.0 us)
Async XLA Ops:
  0.6 0.7 %copy-start.3 = (f32[2,8,128]{2,1,0:T(8,128)S(1)}, f32[2,8,128]{2,1,0:T(8,128)}, u32[]{:S(2)}) copy-start(f32[2,8,128]{2,1,0:T(8,128)} %param.6) | copy-start | bytes 24580
  1.3 4.7 %collective-permute-start = (f32[4,8,128]{2,1,0:T(8,128)S(1)}, f32[4,8,128]{2,1,0:T(8,128)S(1)}, u32[]{:S(2)}, u32[]{:S(2)}) collective-permute-start(f32[4,8,128]{2,1,0:T(8,128)S(1)} %constant_dynamic-update-slice_fusion), channel_id=1, source_target_pairs={{0,4},{4,0},{8,12},{12,8},{1,5},{5,1},{9,13},{13,9},{2,6},{6,2},{1... | collective-permute-start | bytes 49160 | tf_op jit(solution)/shard_map/ppermute | solution.py:493
  6.1 4.5 %copy-start = (bf16[64,64]{1,0:T(8,128)(2,1)S(1)}, bf16[64,64]{1,0:T(8,128)(2,1)}, u32[]{:S(2)}) copy-start(bf16[64,64]{1,0:T(8,128)(2,1)} %w2_in.1) | copy-start | bytes 24580
  6.1 4.5 %copy-start.1 = (bf16[32,64]{1,0:T(8,128)(2,1)S(1)}, bf16[32,64]{1,0:T(8,128)(2,1)}, u32[]{:S(2)}) copy-start(bf16[32,64]{1,0:T(8,128)(2,1)} %w3_in.1) | copy-start | bytes 12292
  6.1 4.5 %copy-start.2 = (bf16[64,18]{0,1:T(8,128)(2,1)S(1)}, bf16[64,18]{0,1:T(8,128)(2,1)}, u32[]{:S(2)}) copy-start(bf16[64,18]{0,1:T(8,128)(2,1)} %param.7) | copy-start | bytes 6916
  6.1 5.2 %collective-permute-start.3 = (f32[2,4,8,128]{3,2,1,0:T(8,128)S(1)}, f32[2,4,8,128]{3,2,1,0:T(8,128)S(1)}, u32[]{:S(2)}, u32[]{:S(2)}) collective-permute-start(f32[2,4,8,128]{3,2,1,0:T(8,128)S(1)} %pad_maximum_fusion.1.own_near), channel_id=1, source_target_pairs={{0,9},{1,10},{2,11},{3,8},{4,15},{5,12},{6,13},{7,14},{8,1},{9,2},... | collective-permute-start | bytes 98312 | tf_op jit(solution)/shard_map/ppermute | solution.py:514
  7.5 4.5 %collective-permute-start.2 = (f32[2,4,8,128]{3,2,1,0:T(8,128)S(1)}, f32[2,4,8,128]{3,2,1,0:T(8,128)S(1)}, u32[]{:S(2)}, u32[]{:S(2)}) collective-permute-start(f32[2,4,8,128]{3,2,1,0:T(8,128)S(1)} %pad_maximum_fusion.1.own_near), channel_id=1, source_target_pairs={{0,1},{1,2},{2,3},{3,0},{4,7},{5,4},{6,5},{7,6},{8,9},{9,10},{10,1... | collective-permute-start | bytes 98312 | tf_op jit(solution)/shard_map/ppermute | solution.py:513
  10.2 4.8 %collective-permute-start.1 = (f32[2,4,8,128]{3,2,1,0:T(8,128)S(1)}, f32[2,4,8,128]{3,2,1,0:T(8,128)S(1)}, u32[]{:S(2)}, u32[]{:S(2)}) collective-permute-start(f32[2,4,8,128]{3,2,1,0:T(8,128)S(1)} %pad_maximum_fusion.1.own_near), channel_id=1, source_target_pairs={{0,8},{4,12},{8,0},{12,4},{1,9},{5,13},{9,1},{13,5},{2,10},{6,14},... | collective-permute-start | bytes 98312 | tf_op jit(solution)/shard_map/ppermute | solution.py:493
  28.1 1.2 %collective-permute-start.4 = (f32[64,128]{1,0:T(8,128)S(1)}, f32[64,128]{1,0:T(8,128)S(1)}, u32[]{:S(2)}, u32[]{:S(2)}) collective-permute-start(f32[64,128]{1,0:T(8,128)S(1)} %get-tuple-element.23), channel_id=1, source_target_pairs={{0,1},{1,0},{2,3},{3,2},{4,5},{5,4},{6,7},{7,6},{8,9},{9,8},{10,11... | collective-permute-start | bytes 98312 | tf_op jit(solution)/shard_map/ppermute | solution.py:493
  29.4 3.9 %collective-permute-start.5 = (f32[64,128]{1,0:T(8,128)S(1)}, f32[64,128]{1,0:T(8,128)S(1)}, u32[]{:S(2)}, u32[]{:S(2)}) collective-permute-start(f32[64,128]{1,0:T(8,128)S(1)} %add.6), channel_id=1, source_target_pairs={{0,2},{2,0},{1,3},{3,1},{4,6},{6,4},{5,7},{7,5},{8,10},{10,8},{9,1... | collective-permute-start | bytes 98312 | tf_op jit(solution)/shard_map/ppermute | solution.py:493
  33.3 4.0 %collective-permute-start.6 = (f32[72,128]{1,0:T(8,128)S(1)}, f32[72,128]{1,0:T(8,128)S(1)}, u32[]{:S(2)}, u32[]{:S(2)}) collective-permute-start(f32[72,128]{1,0:T(8,128)S(1)} %pad_maximum_fusion.sent), channel_id=1, source_target_pairs={{0,4},{4,0},{8,12},{12,8},{1,5},{5,1},{9,13},{13,9},{2,6},{6,2},{1... | collective-permute-start | bytes 110600 | tf_op jit(solution)/shard_map/ppermute | solution.py:493

commit v4 on v3

--- a/solution.py
+++ b/solution.py
@@ -43,12 +43,26 @@
     return (shift(p, 1, 0) + shift(p, -1, 0)) + (shift(p, 0, 1) + shift(p, 0, -1))
 
 
-def pressure_of(source):
-    one = shift(source, 0, 1) + shift(source, 0, -1)
-    two = shift(source, 0, 2) + shift(source, 0, -2)
+def project(first, second):
+    source = 0.5 * (
+        (shift(first, 1, 0) - shift(first, -1, 0)) + (shift(second, 0, 1) - shift(second, 0, -1))
+    )
+    up = {k: shift(source, 0, k) for k in (1, 2, 3)}
+    down = {k: shift(source, 0, -k) for k in (1, 2, 3)}
+
+    def rows(plane, reach):
+        return shift(plane, reach, 0) + shift(plane, -reach, 0)
+
+    one = up[1] + down[1]
     mixed = 4.0 * source + 2.0 * one
-    rows = (shift(mixed, 1, 0) + shift(mixed, -1, 0)) + (shift(source, 2, 0) + shift(source, -2, 0))
-    return (-1.0 / 64.0) * (((20.0 * source + 4.0 * one) + two) + rows)
+    pressure = ((20.0 * source + 4.0 * one) + (up[2] + down[2])) + (rows(mixed, 1) + rows(source, 2))
+    one, two = up[1] - down[1], up[2] - down[2]
+    mixed = 4.0 * one + 2.0 * two
+    slope = ((19.0 * one + 4.0 * two) + (up[3] - down[3])) + (rows(mixed, 1) + rows(one, 2))
+    return (
+        first + (1.0 / 128.0) * (shift(pressure, 1, 0) - shift(pressure, -1, 0)),
+        second + (1.0 / 128.0) * slope,
+    )
 
 
 def dot(a, b):
@@ -59,15 +73,16 @@
     return lax.dot_general(a, b, (((1,), (1,)), ((), ())), preferred_element_type=jnp.float32)
 
 
-def gelu_half(h, with_slope):
-    a, b = 2.0 * GELU_SCALE, 8.0 * GELU_SCALE * GELU_CUBE
-    square = h * h
-    t = jnp.tanh(h * (a + b * square))
-    e = 1.0 + t
-    act = h * e
-    if not with_slope:
-        return act, None
-    return act, e * (1.0 + (h * (1.0 - t)) * (a + (3.0 * b) * square))
+GELU_A, GELU_B = 2.0 * GELU_SCALE, 8.0 * GELU_SCALE * GELU_CUBE
+
+
+def gelu_half(h):
+    e = 1.0 + jnp.tanh(h * (GELU_A + GELU_B * (h * h)))
+    return h * e, e
+
+
+def gelu_half_slope(h, e):
+    return e * (1.0 + (2.0 - e) * (h * (GELU_A + ((3.0 * GELU_B) * h) * h)))
 
 
 def pick_taps(shape, place_dim):
@@ -136,8 +151,6 @@
     x_all,
     a1_all,
     a2_all,
-    g1_all,
-    g2_all,
     cf,
 ):
     f32, bf16 = jnp.float32, jnp.bfloat16
@@ -163,88 +176,87 @@
             else:
                 up[c - 2, pl.ds(row, 8), :] = narrow
 
-    def pack(plane, part):
-        plane = plane[:, LANES:] if part == 2 else plane[:, :LANES]
-        turned = swap_halves(plane)
+    def pack(plane, part, turned=None):
+        if turned is None:
+            plane = plane[:, LANES:] if part == 2 else plane[:, :LANES]
+            turned = swap_halves(plane)
+        low, high = plane[:PACKED], plane[PACKED:]
+        low_turned, high_turned = turned[:PACKED], turned[PACKED:]
         if part == 0:
-            return jnp.where(left, plane[:PACKED], turned[PACKED:])
-        return jnp.where(left, turned[:PACKED], plane[PACKED:])
-
-    def unpack(pieces):
+            return jnp.where(left, low, high_turned), jnp.where(left, high, low_turned)
+        return jnp.where(left, low_turned, high), jnp.where(left, high_turned, low)
+
+    def unpack(pieces, col=0):
         inner, outer = pieces[0], pieces[1]
-        plane = jnp.concatenate(
+        if len(pieces) == 3:
+            lower = jnp.concatenate([swap_halves(pieces[2]), pieces[2]], 0)
+            return shift(jnp.concatenate([unpack(pieces[:2]), lower], 1), 0, col)
+        lanes = lax.broadcasted_iota(jnp.int32, (PACKED, LANES), 1)
+        core = left if col == 0 else ((lanes + (col + LANES)) % LANES) < HALF
+        return jnp.concatenate(
             [
-                jnp.where(left, inner, swap_halves(outer)),
-                jnp.where(left, swap_halves(inner), outer),
+                jnp.where(core, shift(inner, 0, col), shift(outer, 0, col + HALF)),
+                jnp.where(core, shift(inner, 0, col + HALF), shift(outer, 0, col)),
             ],
             0,
         )
-        if len(pieces) == 2:
-            return plane
-        lower = jnp.concatenate([swap_halves(pieces[2]), pieces[2]], 0)
-        return jnp.concatenate([plane, lower], 1)
 
     def stencil(step, part, c, ah, r):
         at = 8 * (r + 2 * ah)
         return uu[step, part, c, at : at + 8, :]
 
-    def slot_of(step, part):
-        return step if part == 0 else STEPS - 1 + step
+    saved = {}
 
     def forward(step):
         parts = range(3) if step == 0 else range(2)
         s = [s_wide[c] if step == 0 else s_all[step, c] for c in range(2)]
         for c in range(2):
-            for al in range(2):
-                line = shift(s[c], al, 0)
-                for b in range(4):
-                    plane = shift(line, 0, b - 1)
-                    for part in parts:
-                        uu[step, part, c, pl.ds(8 + 4 * al + b, PACKED, stride=8), :] = pack(
-                            plane, part
-                        )
-            for part in parts:
-                uu[step, part, c, 0:8, :] = swap_halves(uu[step, part, c, 128:136, :])
-                uu[step, part, c, 136:144, :] = swap_halves(uu[step, part, c, 8:16, :])
-
-        for part in parts:
-            keep = part == 0 or step > 0
-            slot = slot_of(step, part)
-            x = jnp.concatenate(
-                [
-                    jnp.concatenate(
-                        [stencil(step, part, c, ah, r) for c in range(2) for ah in range(2)], 0
-                    ).astype(bf16)
-                    for r in range(PACKED)
-                ],
-                1,
-            )
-            act, slope = gelu_half(dot(w1[...], x), keep)
-            act = act.astype(bf16)
-            if part == 0:
-                x_all[slot] = x
-                a1_all[slot] = act
-            if keep:
-                g1_all[slot] = slope
-            act, slope = gelu_half(dot(w2[...], act), keep)
-            act = act.astype(bf16)
-            if part == 0:
-                a2_all[slot] = act
-            if keep:
-                g2_all[slot] = slope
-            out = dot(w3[...], jnp.concatenate([act, act], 0))
-            if keep and step > 0:
-                cf[slot] = out
-            for r in range(PACKED):
-                weight = out[:, r * LANES : (r + 1) * LANES]
-                for c in range(2):
-                    lower = stencil(step, part, c, 0, r)
-                    upper = stencil(step, part, c, 1, r)
-                    for f in range(2):
-                        qp[part, 2 * f + c, 8 * r : 8 * r + 8, :] = (
-                            weight[16 * f : 16 * f + 8] * lower
-                            + weight[16 * f + 8 : 16 * f + 16] * upper
-                        )
+            for b in range(4):
+                plane = shift(s[c], 0, b - 1)
+                turned = None if step == 0 else shift(s[c], 0, b - 1 + HALF)
+                for part in parts:
+                    packed, swapped = pack(plane, part, turned)
+                    ref = uu.at[step, part, c]
+                    ref[pl.ds(8 + b, PACKED, stride=8), :] = packed
+                    ref[pl.ds(4 + b, PACKED, stride=8), :] = packed
+                    for at, r in ((b, PACKED - 1), (132 + b, 0), (136 + b, 0), (140 + b, 1)):
+                        ref[at : at + 1, :] = swapped[r : r + 1]
+
+        cells = PACKED * LANES
+        rows = [(part, r) for part in parts for r in range(PACKED)]
+        kept = cells if step == 0 else 2 * cells
+        x = jnp.concatenate(
+            [
+                jnp.concatenate(
+                    [stencil(step, part, c, ah, r) for c in range(2) for ah in range(2)], 0
+                ).astype(bf16)
+                for part, r in rows
+            ],
+            1,
+        )
+        x_all[step] = x[:, :cells]
+        first = dot(w1[...], x)
+        act, first_up = gelu_half(first)
+        act = act.astype(bf16)
+        a1_all[step] = act[:, :cells]
+        second = dot(w2[...], act)
+        act, second_up = gelu_half(second)
+        act = act.astype(bf16)
+        a2_all[step] = act[:, :cells]
+        saved[step] = [value[:, :kept] for value in (first, first_up, second, second_up)]
+        out = dot(w3[...], jnp.concatenate([act, act], 0))
+        if step > 0:
+            cf[step] = out
+        for k, (part, r) in enumerate(rows):
+            weight = out[:, k * LANES : (k + 1) * LANES]
+            for c in range(2):
+                lower = stencil(step, part, c, 0, r)
+                upper = stencil(step, part, c, 1, r)
+                for f in range(2):
+                    qp[part, 2 * f + c, 8 * r : 8 * r + 8, :] = (
+                        weight[16 * f : 16 * f + 8] * lower
+                        + weight[16 * f + 8 : 16 * f + 16] * upper
+                    )
 
         def reduced(part, which):
             terms = [qp[part, which, pl.ds(j, PACKED, stride=8), :] for j in range(8)]
@@ -253,30 +265,24 @@
             return terms[0]
 
         moved = []
-        near = [s[0] + shift(s[0], 1, 0), s[1] + shift(s[1], 0, 1)]
+        speed = [0.5 * (s[0] + shift(s[0], 1, 0)), 0.5 * (s[1] + shift(s[1], 0, 1))]
+        speed_below = shift(speed[1], 0, -1)
         for c in range(2):
-            flux = []
-            for f in range(2):
-                mean = 0.5 * (s[c] + (shift(s[c], 1, 0) if f == 0 else shift(s[c], 0, 1)))
-                q = mean + unpack([reduced(part, 2 * f + c) for part in parts])
-                if step > 0:
-                    qs[step, 2 * f + c] = q
-                flux.append((0.5 * near[f]) * q)
-            transport = (flux[0] - shift(flux[0], -1, 0)) + (flux[1] - shift(flux[1], 0, -1))
+            pieces = [[reduced(part, 2 * f + c) for part in parts] for f in range(2)]
+            mean = [0.5 * (s[c] + shift(s[c], 1, 0)), 0.5 * (s[c] + shift(s[c], 0, 1))]
+            q = [mean[f] + unpack(pieces[f]) for f in range(2)]
+            if step > 0:
+                for f in range(2):
+                    qs[step, 2 * f + c] = q[f]
+            rows = speed[0] * q[0]
+            below = speed_below * (shift(mean[1], 0, -1) + unpack(pieces[1], -1))
+            transport = (rows - shift(rows, -1, 0)) + (speed[1] * q[1] - below)
             moved.append(
                 s[c]
                 - time_step * transport
                 + time_step * viscosity * (neighbours(s[c]) - 4.0 * s[c])
             )
-        source = 0.5 * (
-            (shift(moved[0], 1, 0) - shift(moved[0], -1, 0))
-            + (shift(moved[1], 0, 1) - shift(moved[1], 0, -1))
-        )
-        pressure = pressure_of(source)
-        after = [
-            moved[0] - 0.5 * (shift(pressure, 1, 0) - shift(pressure, -1, 0)),
-            moved[1] - 0.5 * (shift(pressure, 0, 1) - shift(pressure, 0, -1)),
-        ]
+        after = list(project(moved[0], moved[1]))
         for c in range(2):
             if step == 0:
                 column = lax.broadcasted_iota(jnp.int32, (2 * PACKED, LANES), 1)
@@ -288,14 +294,7 @@
     def backward(step, total):
         u = [up[c] for c in range(2)]
         s = [s_all[step, c] for c in range(2)]
-        p_bar = 0.5 * (
-            (shift(u[0], 1, 0) - shift(u[0], -1, 0)) + (shift(u[1], 0, 1) - shift(u[1], 0, -1))
-        )
-        half = 0.5 * pressure_of(p_bar)
-        m_bar = [
-            u[0] + (shift(half, -1, 0) - shift(half, 1, 0)),
-            u[1] + (shift(half, 0, -1) - shift(half, 0, 1)),
-        ]
+        m_bar = project(u[0], u[1])
         speed = [0.5 * (s[0] + shift(s[0], 1, 0)), 0.5 * (s[1] + shift(s[1], 0, 1))]
         box = []
         for c in range(2):
@@ -305,77 +304,87 @@
             box.append((1.0 / 16.0) * (shift(pair, -1, 0) + shift(pair, 1, 0)))
         speed_bar = [None, None]
         s_bar = []
-        mean = [None, None]
         parts = range(2) if step > 0 else range(1)
-        for c in range(2):
+        for part in parts:
+            weights = [pack(time_step * speed[f], part)[0] for f in range(2)]
+            boxes = [pack(box[c], part)[0] for c in range(2)]
+            mean = [None, None]
+            for c in range(2):
+                here = pack(m_bar[c], part)[0]
+                ahead = (
+                    pack(shift(m_bar[c], 1, 0), part)[0],
+                    pack(shift(m_bar[c], 0, 1), part, shift(m_bar[c], 0, 1 + HALF))[0],
+                )
+                for f in range(2):
+                    q_bar = weights[f] * (ahead[f] - here)
+                    bq[part, 2 * f + c] = q_bar
+                    term = q_bar * boxes[c]
+                    mean[f] = term if c == 0 else mean[f] + term
+            for f in range(2):
+                bq[part, 4 + f] = mean[f]
+        for c in range(2) if step > 0 else ():
             flux_bar = [
                 time_step * (shift(m_bar[c], 1, 0) - m_bar[c]),
                 time_step * (shift(m_bar[c], 0, 1) - m_bar[c]),
             ]
-            if step > 0:
-                kept = m_bar[c] + time_step * viscosity * (neighbours(m_bar[c]) - 4.0 * m_bar[c])
+            kept = m_bar[c] + time_step * viscosity * (neighbours(m_bar[c]) - 4.0 * m_bar[c])
             for f in range(2):
-                q_bar = speed[f] * flux_bar[f]
-                for part in parts:
-                    bq[part, 2 * f + c] = pack(q_bar, part)
-                term = q_bar * box[c]
-                mean[f] = term if c == 0 else mean[f] + term
-                if step > 0:
-                    term = qs[step, 2 * f + c] * flux_bar[f]
-                    speed_bar[f] = term if c == 0 else speed_bar[f] + term
-                    half = 0.5 * q_bar
-                    kept = kept + (half + (shift(half, -1, 0) if f == 0 else shift(half, 0, -1)))
-            if step > 0:
-                s_bar.append(kept)
+                term = qs[step, 2 * f + c] * flux_bar[f]
+                speed_bar[f] = term if c == 0 else speed_bar[f] + term
+                half = (0.5 * speed[f]) * flux_bar[f]
+                kept = kept + (half + (shift(half, -1, 0) if f == 0 else shift(half, 0, -1)))
+            s_bar.append(kept)
         if step > 0:
             half = 0.5 * speed_bar[0]
             s_bar[0] = s_bar[0] + (half + shift(half, -1, 0))
             half = 0.5 * speed_bar[1]
             s_bar[1] = s_bar[1] + (half + shift(half, 0, -1))
-        for f in range(2):
-            for part in parts:
-                bq[part, 4 + f] = pack(mean[f], part)
-
+
+        cells = PACKED * LANES
+
+        def spread_row(part, which, r):
+            return jnp.broadcast_to(bq[part, which, r : r + 1, :], (8, LANES))
+
+        third = []
         for part in parts:
-            slot = slot_of(step, part)
-
-            def spread_row(which, r):
-                return jnp.broadcast_to(bq[part, which, r : r + 1, :], (8, LANES))
-
-            third = []
             for r in range(PACKED):
                 pieces = []
                 for f in range(2):
-                    q0, q1, m = (spread_row(w, r) for w in (2 * f, 2 * f + 1, 4 + f))
+                    q0, q1, m = (spread_row(part, w, r) for w in (2 * f, 2 * f + 1, 4 + f))
                     for ah in range(2):
                         pieces.append(
                             (q0 * stencil(step, part, 0, ah, r) + q1 * stencil(step, part, 1, ah, r))
                             - m
                         )
                 third.append(jnp.concatenate(pieces, 0).astype(bf16))
-            third = jnp.concatenate(third, 1)
-            second = (dot(w3t[...], third) * g2_all[slot]).astype(bf16)
-            first = (dot(w2t[...], second) * g1_all[slot]).astype(bf16)
-            if part == 0:
-                terms = (
-                    dot_cells(first, x_all[slot]),
-                    dot_cells(second, a1_all[slot]),
-                    dot_cells(third, a2_all[slot]),
-                )
-                total = terms if total is None else tuple(a + b for a, b in zip(total, terms))
-            if step == 0:
-                return total
-            out = dot(w1t[...], first)
-
+        third = jnp.concatenate(third, 1)
+        first, first_up, second, second_up = saved[step]
+        second = (dot(w3t[...], third) * gelu_half_slope(second, second_up)).astype(bf16)
+        first = (dot(w2t[...], second) * gelu_half_slope(first, first_up)).astype(bf16)
+
+        def gradients():
+            terms = (
+                dot_cells(first[:, :cells], x_all[step]),
+                dot_cells(second[:, :cells], a1_all[step]),
+                dot_cells(third[:, :cells], a2_all[step]),
+            )
+            return terms if total is None else tuple(a + b for a, b in zip(total, terms))
+
+        if step == 0:
+            return gradients()
+        out = dot(w1t[...], first)
+
+        for part in parts:
             y = {}
             for r in range(PACKED):
-                lanes = slice(r * LANES, (r + 1) * LANES)
+                k = part * PACKED + r
+                lanes = slice(k * LANES, (k + 1) * LANES)
                 for c in range(2):
-                    q0, q1 = spread_row(c, r), spread_row(2 + c, r)
+                    q0, q1 = spread_row(part, c, r), spread_row(part, 2 + c, r)
                     for ah in range(2):
                         y[c, ah, r] = (
-                            cf[slot, 8 * ah : 8 * ah + 8, lanes] * q0
-                            + cf[slot, 16 + 8 * ah : 24 + 8 * ah, lanes] * q1
+                            cf[step, 8 * ah : 8 * ah + 8, lanes] * q0
+                            + cf[step, 16 + 8 * ah : 24 + 8 * ah, lanes] * q1
                         ) + out[16 * c + 8 * ah : 16 * c + 8 * ah + 8, lanes]
             for c in range(2):
                 rows = []
@@ -390,16 +399,16 @@
         for c in range(2):
             kept = s_bar[c]
             for b in range(4):
-                plane = unpack(
+                kept = kept + unpack(
                     [
                         ub[part, c, pl.ds(8 + b, PACKED, stride=8), :]
                         + ub[part, c, pl.ds(4 + b, PACKED, stride=8), :]
                         for part in parts
-                    ]
+                    ],
+                    1 - b,
                 )
-                kept = kept + shift(plane, 0, 1 - b)
             up[c] = kept
-        return total
+        return gradients()
 
     for step in range(STEPS):
         forward(step)
@@ -426,7 +435,6 @@
     cells = PACKED * LANES
     f32, bf16 = jnp.float32, jnp.bfloat16
     vmem = pl.BlockSpec(memory_space=pltpu.VMEM)
-    slots = 2 * STEPS - 1
     return pl.pallas_call(
         functools.partial(kernel, factor),
         out_shape=(
@@ -448,15 +456,13 @@
             pltpu.VMEM((STEPS, 32, cells), bf16),
             pltpu.VMEM((STEPS, CHANNELS, cells), bf16),
             pltpu.VMEM((STEPS, CHANNELS, cells), bf16),
-            pltpu.VMEM((slots, CHANNELS, cells), f32),
-            pltpu.VMEM((slots, CHANNELS, cells), f32),
-            pltpu.VMEM((slots, COEFS, cells), f32),
+            pltpu.VMEM((STEPS, COEFS, 2 * cells), f32),
         ],
         compiler_params=pltpu.CompilerParams(vmem_limit_bytes=48 * 1024 * 1024),
     )(*pieces, *weights)
 
 
-def finish(sent, got, mine, tile, first, second, third):
+def finish(sent, beyond, got, across, mine, tile, first, second, third):
     z = lax.axis_index("rows")
     lane = lax.broadcasted_iota(jnp.int32, (8, LANES), 1)
     odd = (lane * 0 + z) % 2 == 1
@@ -466,13 +472,13 @@
         low = jnp.where(odd, there, here)
         high = jnp.where(odd, here, there)
         tile[c] = jnp.where(lane < HALF, low, swap_halves(high))
-    grads = sent[0:64, :] + got[0:64, :]
+    grads = (sent[...] + beyond[...]) + (got[0:64, :] + across[...])
     first[...] = grads[0:TAPS, 64:]
     second[...] = grads[:, 0:64]
     third[...] = grads[32:, 64:]
 
 
-def finish_call(sent, got, mine):
+def finish_call(*pieces):
     vmem = pl.BlockSpec(memory_space=pltpu.VMEM)
     f32 = jnp.float32
     return pl.pallas_call(
@@ -483,10 +489,10 @@
             jax.ShapeDtypeStruct((CHANNELS, CHANNELS), f32),
             jax.ShapeDtypeStruct((COEFS, CHANNELS), f32),
         ),
-        in_specs=[vmem] * 3,
+        in_specs=[vmem] * len(pieces),
         out_specs=(vmem,) * 4,
         compiler_params=pltpu.CompilerParams(vmem_limit_bytes=8 * 1024 * 1024),
-    )(sent, got, mine)
+    )(*pieces)
 
 
 def swap(x, axis, bit):
@@ -518,9 +524,11 @@
     mine, theirs, grads = strip_call(factor, (near, far, other_near, other_far), weights)
 
     grads = grads + swap(grads, "section", 1)
-    grads = grads + swap(grads, "cols", 1)
-    sent = jnp.concatenate([grads, theirs], 0)
-    tile, first, second, third = finish_call(sent, swap(sent, "rows", 1), mine)
+    ring = ("rows", "cols")
+    across = lax.ppermute(grads, ring, [(i, i ^ 3) for i in range(2 * row_count)])
+    beyond = swap(grads, "cols", 1)
+    got = swap(jnp.concatenate([grads, theirs], 0), "rows", 1)
+    tile, first, second, third = finish_call(grads, beyond, got, across, mine)
     return tile, first.T, second, third
 
 

time: 38.3 us -> 34.8 us (0.909)
  Pallas kernels: 14.1 us -> 11.8 us
  waiting for transfers between devices: 12.4 us -> 10.3 us
  starting transfers between devices: 10.2 us -> 11.1 us
    ppermute x5, waiting for transfers between devices: 11.2 us -> 6 us  [swap(): lax.ppermute(x, axis, [(i, i ^ bit) for i in range(lax.axis_size(axis))])]
    ppermute x0 -> x1, waiting for transfers between devices: none -> 3.12 us  [strips(): lax.ppermute(grads, ring, [(i, i ^ 3) for i in range(2 * row_count)])]
    pallas_call x1, Pallas kernels: 13.1 us -> 10.8 us  [strip_call(): pl.pallas_call(functools.partial(kernel, factor), out_shape=(jax.ShapeDty...]
    ppermute x0 -> x1, starting transfers between devices: none -> 0.6 us  [strips(): lax.ppermute(grads, ring, [(i, i ^ 3) for i in range(2 * row_count)])]
  transfers between devices with their start and end apart: 7 -> 8, of which waited for: 7 -> 6; matrix products, arithmetic and copies ran while one was open for 0% -> 0% of each run, Pallas kernels for 1% -> 1%
where the time goes in v4:
time: 34.8 us; the launch traced here: 34.6 us
  Pallas kernels  11.8 us (34%)
  starting transfers between devices  11.1 us (32%)
  waiting for transfers between devices  10.3 us (30%)
  local copies, waits for them, and re-layouts  0.72 us (2%)
  between operations  0.67 us (2%)
    pallas_call x1, Pallas kernels, strip_call(): pl.pallas_call(functools.partial(kernel, factor), out_shape=(jax.ShapeDty...  10.8 us
    ppermute x5, starting transfers between devices, swap(): lax.ppermute(x, axis, [(i, i ^ bit) for i in range(lax.axis_size(axis))])  6.34 us
    ppermute x5, waiting for transfers between devices, swap(): lax.ppermute(x, axis, [(i, i ^ bit) for i in range(lax.axis_size(axis))])  6 us
    ppermute x1, waiting for transfers between devices, strips(): lax.ppermute(grads, ring, [(i, i ^ 3) for i in range(2 * row_count)])  3.12 us
    ppermute x1, starting transfers between devices, strips(): other_near = lax.ppermute(near, everyone, beside(0))  2.75 us
    ppermute x1, starting transfers between devices, strips(): other_far = lax.ppermute(near, everyone, beside(2))  1.38 us
    pallas_call x1, Pallas kernels, finish_call(): pl.pallas_call(finish, out_shape=(jax.ShapeDtypeStruct((2, 8, LANES), f32...  0.75 us
    unnamed x9, local copies, waits for them, and re-layouts  0.72 us
  transfers between devices with their start and end apart: 8, of which 6 were waited for; matrix products, arithmetic and copies ran while one was open for 0% of the time, Pallas kernels for 1%

profile of v4, /device:TPU:0, one launch (start us, length us, event | category | flops | bytes accessed | tf_op | source)
XLA Modules:
  0.0 34.6 jit_solution(10280695468894954804)
XLA Ops:
  0.6 0.0 copy-start.3
  0.6 0.7 %constant_dynamic-update-slice_fusion.1 = f32[4,8,128]{2,1,0:T(8,128)S(1)} fusion(f32[2,8,128]{2,1,0:T(8,128)} %param.5), kind=kLoop, calls=%fused_computation.3 | loop fusion | bytes 16384
  1.3 0.0 copy-done.3
  1.3 3.0 %collective-permute-start = (f32[4,8,128]{2,1,0:T(8,128)S(1)}, f32[4,8,128]{2,1,0:T(8,128)S(1)}, u32[]{:S(2)}, u32[]{:S(2)}) collective-permute-start(f32[4,8,128]{2,1,0:T(8,128)S(1)} %constant_dynamic-update-slice_fusion), channel_id=1, source_target_pairs={{0,4},{4,0},{8,12},{12,8},{1,5},{5,1},{9,13},{13,9},{2,6},{6,2},{1... | collective-permute-start | bytes 49160 | tf_op jit(solution)/shard_map/ppermute | solution.py:499
  4.4 1.7 %collective-permute-done = f32[4,8,128]{2,1,0:T(8,128)S(1)} collective-permute-done((f32[4,8,128]{2,1,0:T(8,128)S(1)}, f32[4,8,128]{2,1,0:T(8,128)S(1)}, u32[]{:S(2)}, u32[]{:S(2)}) %collective-permute-start) | collective-permute-done | bytes 16416 | tf_op jit(solution)/shard_map/ppermute | solution.py:499
  6.1 0.0 copy-start
  6.1 0.0 copy-start.1
  6.1 0.0 copy-start.2
  6.1 1.4 %collective-permute-start.3 = (f32[2,4,8,128]{3,2,1,0:T(8,128)S(1)}, f32[2,4,8,128]{3,2,1,0:T(8,128)S(1)}, u32[]{:S(2)}, u32[]{:S(2)}) collective-permute-start(f32[2,4,8,128]{3,2,1,0:T(8,128)S(1)} %pad_maximum_fusion.1.own_near), channel_id=1, source_target_pairs={{0,9},{1,10},{2,11},{3,8},{4,15},{5,12},{6,13},{7,14},{8,1},{9,2},... | collective-permute-start | bytes 98312 | tf_op jit(solution)/shard_map/ppermute | solution.py:520
  7.5 2.8 %collective-permute-start.2 = (f32[2,4,8,128]{3,2,1,0:T(8,128)S(1)}, f32[2,4,8,128]{3,2,1,0:T(8,128)S(1)}, u32[]{:S(2)}, u32[]{:S(2)}) collective-permute-start(f32[2,4,8,128]{3,2,1,0:T(8,128)S(1)} %pad_maximum_fusion.1.own_near), channel_id=1, source_target_pairs={{0,1},{1,2},{2,3},{3,0},{4,7},{5,4},{6,5},{7,6},{8,9},{9,10},{10,1... | collective-permute-start | bytes 98312 | tf_op jit(solution)/shard_map/ppermute | solution.py:519
  10.2 0.3 collective-permute-start.1
  10.6 0.0 copy-done
  10.6 0.0 copy-done.1
  10.6 0.0 copy-done.2
  10.6 0.2 shard_map.84
  10.8 0.5 %collective-permute-done.3.other_far = f32[2,4,8,128]{3,2,1,0:T(8,128)S(1)} collective-permute-done((f32[2,4,8,128]{3,2,1,0:T(8,128)S(1)}, f32[2,4,8,128]{3,2,1,0:T(8,128)S(1)}, u32[]{:S(2)}, u32[]{:S(2)}) %collective-permute-start.3) | collective-permute-done | bytes 32800 | tf_op jit(solution)/shard_map/ppermute | solution.py:520
  11.3 0.7 %collective-permute-done.2.other_near = f32[2,4,8,128]{3,2,1,0:T(8,128)S(1)} collective-permute-done((f32[2,4,8,128]{3,2,1,0:T(8,128)S(1)}, f32[2,4,8,128]{3,2,1,0:T(8,128)S(1)}, u32[]{:S(2)}, u32[]{:S(2)}) %collective-permute-start.2) | collective-permute-done | bytes 32800 | tf_op jit(solution)/shard_map/ppermute | solution.py:519
  12.0 3.1 %collective-permute-done.1.own_far = f32[2,4,8,128]{3,2,1,0:T(8,128)S(1)} collective-permute-done((f32[2,4,8,128]{3,2,1,0:T(8,128)S(1)}, f32[2,4,8,128]{3,2,1,0:T(8,128)S(1)}, u32[]{:S(2)}, u32[]{:S(2)}) %collective-permute-start.1) | collective-permute-done | bytes 32800 | tf_op jit(solution)/shard_map/ppermute | solution.py:499
  15.0 10.8 %shard_map.85 = (f32[8,128]{1,0:T(8,128)S(1)}, f32[8,128]{1,0:T(8,128)S(1)}, f32[64,128]{1,0:T(8,128)S(1)}) custom-call(f32[2,4,8,128]{3,2,1,0:T(8,128)S(1)} %pad_maximum_fusion.1.own_near, f32[2,4,8,128]{3,2,1,0:T(8,128)S(1)} %collective-permute-done.1.own_far, f32[2,4,8,128]{3,2,1,0:T(8,128)S(1)} %collective-permute-done.2.other_near, ...), custom_call_target="tpu_custom_call" | custom-call | tf_op jit(solution)/shard_map/pallas_call | solution.py:438
  25.9 0.0 collective-permute-start.4
  25.9 1.2 %collective-permute-done.4 = f32[64,128]{1,0:T(8,128)S(1)} collective-permute-done((f32[64,128]{1,0:T(8,128)S(1)}, f32[64,128]{1,0:T(8,128)S(1)}, u32[]{:S(2)}, u32[]{:S(2)}) %collective-permute-start.4) | collective-permute-done | bytes 32800 | tf_op jit(solution)/shard_map/ppermute | solution.py:499
  27.1 1.8 %collective-permute-start.6 = (f32[72,128]{1,0:T(8,128)S(1)}, f32[72,128]{1,0:T(8,128)S(1)}, u32[]{:S(2)}, u32[]{:S(2)}) collective-permute-start(f32[72,128]{1,0:T(8,128)S(1)} %pad_maximum_fusion), channel_id=1, source_target_pairs={{0,4},{4,0},{8,12},{12,8},{1,5},{5,1},{9,13},{13,9},{2,6},{6,2},{1... | collective-permute-start | bytes 110600 | tf_op jit(solution)/shard_map/ppermute | solution.py:499
  28.9 0.6 %collective-permute-start.7 = (f32[64,128]{1,0:T(8,128)S(1)}, f32[64,128]{1,0:T(8,128)S(1)}, u32[]{:S(2)}, u32[]{:S(2)}) collective-permute-start(f32[64,128]{1,0:T(8,128)S(1)} %add.3.sent), channel_id=1, source_target_pairs={{0,6},{2,4},{4,2},{6,0},{8,14},{10,12},{12,10},{14,8},{1,7},{3,5},... | collective-permute-start | bytes 98312 | tf_op jit(solution)/shard_map/ppermute | solution.py:528
  29.5 1.1 %collective-permute-start.5 = (f32[64,128]{1,0:T(8,128)S(1)}, f32[64,128]{1,0:T(8,128)S(1)}, u32[]{:S(2)}, u32[]{:S(2)}) collective-permute-start(f32[64,128]{1,0:T(8,128)S(1)} %add.3.sent), channel_id=1, source_target_pairs={{0,2},{2,0},{1,3},{3,1},{4,6},{6,4},{5,7},{7,5},{8,10},{10,8},{9,1... | collective-permute-start | bytes 98312 | tf_op jit(solution)/shard_map/ppermute | solution.py:499
  30.7 3.1 %collective-permute-done.7.across = f32[64,128]{1,0:T(8,128)S(1)} collective-permute-done((f32[64,128]{1,0:T(8,128)S(1)}, f32[64,128]{1,0:T(8,128)S(1)}, u32[]{:S(2)}, u32[]{:S(2)}) %collective-permute-start.7) | collective-permute-done | bytes 32800 | tf_op jit(solution)/shard_map/ppermute | solution.py:528
  33.8 0.0 collective-permute-done.5.beyond
  33.8 0.0 collective-permute-done.6.got
  33.8 0.8 %shard_map.86 = (f32[2,8,128]{2,1,0:T(8,128)}, f32[18,64]{1,0:T(8,128)}, f32[64,64]{1,0:T(8,128)}, f32[32,64]{1,0:T(8,128)}) custom-call(f32[64,128]{1,0:T(8,128)S(1)} %add.3.sent, f32[64,128]{1,0:T(8,128)S(1)} %collective-permute-done.5.beyond, f32[72,128]{1,0:T(8,128)S(1)} %collective-permute-done.6.got, f32[64,128]{1,0:T(8,128)S(1)} %collective-permute-done.7.across, ...), custom_call_target="tpu_custom_call" | custom-call | tf_op jit(solution)/shard_map/pallas_call | solution.py:484
  (4 shorter events, 0.0 us)
Async XLA Ops:
  0.6 0.7 %copy-start.3 = (f32[2,8,128]{2,1,0:T(8,128)S(1)}, f32[2,8,128]{2,1,0:T(8,128)}, u32[]{:S(2)}) copy-start(f32[2,8,128]{2,1,0:T(8,128)} %param.6) | copy-start | bytes 24580
  1.3 4.7 %collective-permute-start = (f32[4,8,128]{2,1,0:T(8,128)S(1)}, f32[4,8,128]{2,1,0:T(8,128)S(1)}, u32[]{:S(2)}, u32[]{:S(2)}) collective-permute-start(f32[4,8,128]{2,1,0:T(8,128)S(1)} %constant_dynamic-update-slice_fusion), channel_id=1, source_target_pairs={{0,4},{4,0},{8,12},{12,8},{1,5},{5,1},{9,13},{13,9},{2,6},{6,2},{1... | collective-permute-start | bytes 49160 | tf_op jit(solution)/shard_map/ppermute | solution.py:499
  6.1 4.5 %copy-start = (bf16[64,64]{1,0:T(8,128)(2,1)S(1)}, bf16[64,64]{1,0:T(8,128)(2,1)}, u32[]{:S(2)}) copy-start(bf16[64,64]{1,0:T(8,128)(2,1)} %w2_in.1) | copy-start | bytes 24580
  6.1 4.5 %copy-start.1 = (bf16[32,64]{1,0:T(8,128)(2,1)S(1)}, bf16[32,64]{1,0:T(8,128)(2,1)}, u32[]{:S(2)}) copy-start(bf16[32,64]{1,0:T(8,128)(2,1)} %w3_in.1) | copy-start | bytes 12292
  6.1 4.5 %copy-start.2 = (bf16[64,18]{0,1:T(8,128)(2,1)S(1)}, bf16[64,18]{0,1:T(8,128)(2,1)}, u32[]{:S(2)}) copy-start(bf16[64,18]{0,1:T(8,128)(2,1)} %param.7) | copy-start | bytes 6916
  6.1 5.2 %collective-permute-start.3 = (f32[2,4,8,128]{3,2,1,0:T(8,128)S(1)}, f32[2,4,8,128]{3,2,1,0:T(8,128)S(1)}, u32[]{:S(2)}, u32[]{:S(2)}) collective-permute-start(f32[2,4,8,128]{3,2,1,0:T(8,128)S(1)} %pad_maximum_fusion.1.own_near), channel_id=1, source_target_pairs={{0,9},{1,10},{2,11},{3,8},{4,15},{5,12},{6,13},{7,14},{8,1},{9,2},... | collective-permute-start | bytes 98312 | tf_op jit(solution)/shard_map/ppermute | solution.py:520
  7.5 4.5 %collective-permute-start.2 = (f32[2,4,8,128]{3,2,1,0:T(8,128)S(1)}, f32[2,4,8,128]{3,2,1,0:T(8,128)S(1)}, u32[]{:S(2)}, u32[]{:S(2)}) collective-permute-start(f32[2,4,8,128]{3,2,1,0:T(8,128)S(1)} %pad_maximum_fusion.1.own_near), channel_id=1, source_target_pairs={{0,1},{1,2},{2,3},{3,0},{4,7},{5,4},{6,5},{7,6},{8,9},{9,10},{10,1... | collective-permute-start | bytes 98312 | tf_op jit(solution)/shard_map/ppermute | solution.py:519
  10.2 4.8 %collective-permute-start.1 = (f32[2,4,8,128]{3,2,1,0:T(8,128)S(1)}, f32[2,4,8,128]{3,2,1,0:T(8,128)S(1)}, u32[]{:S(2)}, u32[]{:S(2)}) collective-permute-start(f32[2,4,8,128]{3,2,1,0:T(8,128)S(1)} %pad_maximum_fusion.1.own_near), channel_id=1, source_target_pairs={{0,8},{4,12},{8,0},{12,4},{1,9},{5,13},{9,1},{13,5},{2,10},{6,14},... | collective-permute-start | bytes 98312 | tf_op jit(solution)/shard_map/ppermute | solution.py:499
  25.9 1.2 %collective-permute-start.4 = (f32[64,128]{1,0:T(8,128)S(1)}, f32[64,128]{1,0:T(8,128)S(1)}, u32[]{:S(2)}, u32[]{:S(2)}) collective-permute-start(f32[64,128]{1,0:T(8,128)S(1)} %get-tuple-element.23), channel_id=1, source_target_pairs={{0,1},{1,0},{2,3},{3,2},{4,5},{5,4},{6,7},{7,6},{8,9},{9,8},{10,11... | collective-permute-start | bytes 98312 | tf_op jit(solution)/shard_map/ppermute | solution.py:499
  27.1 6.7 %collective-permute-start.6 = (f32[72,128]{1,0:T(8,128)S(1)}, f32[72,128]{1,0:T(8,128)S(1)}, u32[]{:S(2)}, u32[]{:S(2)}) collective-permute-start(f32[72,128]{1,0:T(8,128)S(1)} %pad_maximum_fusion), channel_id=1, source_target_pairs={{0,4},{4,0},{8,12},{12,8},{1,5},{5,1},{9,13},{13,9},{2,6},{6,2},{1... | collective-permute-start | bytes 110600 | tf_op jit(solution)/shard_map/ppermute | solution.py:499
  28.9 4.9 %collective-permute-start.7 = (f32[64,128]{1,0:T(8,128)S(1)}, f32[64,128]{1,0:T(8,128)S(1)}, u32[]{:S(2)}, u32[]{:S(2)}) collective-permute-start(f32[64,128]{1,0:T(8,128)S(1)} %add.3.sent), channel_id=1, source_target_pairs={{0,6},{2,4},{4,2},{6,0},{8,14},{10,12},{12,10},{14,8},{1,7},{3,5},... | collective-permute-start | bytes 98312 | tf_op jit(solution)/shard_map/ppermute | solution.py:528
  29.5 4.3 %collective-permute-start.5 = (f32[64,128]{1,0:T(8,128)S(1)}, f32[64,128]{1,0:T(8,128)S(1)}, u32[]{:S(2)}, u32[]{:S(2)}) collective-permute-start(f32[64,128]{1,0:T(8,128)S(1)} %add.3.sent), channel_id=1, source_target_pairs={{0,2},{2,0},{1,3},{3,1},{4,6},{6,4},{5,7},{7,5},{8,10},{10,8},{9,1... | collective-permute-start | bytes 98312 | tf_op jit(solution)/shard_map/ppermute | solution.py:499

commit v5 on v4

--- a/solution.py
+++ b/solution.py
@@ -164,9 +164,9 @@
         own, other = ((own_near, other_near), (own_far, other_far))[k // 2]
         for c in range(4):
             here = own[k % 2, c]
-            there = other[k % 2, c]
+            there = other[c] if k % 2 else swap_halves(other[c])
             turned = swap_halves(here)
-            upper = jnp.where(odd, jnp.where(lane < HALF, turned, swap_halves(there)), here)
+            upper = jnp.where(odd, jnp.where(lane < HALF, turned, there), here)
             lower = jnp.where(odd, turned, there)
             narrow = jnp.where(lane < LANES - SIDE, upper, lower)
             if c < 2:
@@ -507,18 +507,22 @@
     def beside(flip):
         pairs = []
         for row in range(row_count):
-            step = 1 if row % 2 == 0 else block_count - 1
+            step = 1 if (row ^ flip) % 2 == 0 else block_count - 1
             for block in range(block_count):
                 target = (row ^ flip) * block_count + (block + step) % block_count
                 pairs.append((row * block_count + block, target))
         return pairs
 
     tile = jnp.concatenate([state, cotangent], 0)
+    everyone = ("rows", "cols", "section")
+    across = lax.ppermute(tile, everyone, beside(1))
+    level = lax.ppermute(tile, everyone, beside(0))
     near = jnp.stack([tile, swap(tile, "rows", 1)])
-    everyone = ("rows", "cols", "section")
-    other_near = lax.ppermute(near, everyone, beside(0))
-    other_far = lax.ppermute(near, everyone, beside(2))
-    far = swap(near, "rows", 2)
+    odd = lax.axis_index("rows") % 2 == 1
+    half = [jnp.where(odd, x[..., :HALF], x[..., HALF:]) for x in (level, across)]
+    other_near = jnp.concatenate(half, -1)
+    both = swap(jnp.concatenate([near.reshape(8, 8, LANES), other_near]), "rows", 2)
+    far, other_far = both[:8].reshape(2, 4, 8, LANES), both[8:]
 
     factor = gradient_gain / math.sqrt(row_count * state.shape[1] * LANES * block_count)
     mine, theirs, grads = strip_call(factor, (near, far, other_near, other_far), weights)

time: 34.8 us -> 33.5 us (0.963)
  waiting for transfers between devices: 10.3 us -> 8.88 us
  starting transfers between devices: 11.1 us -> 10.2 us
  local copies, waits for them, and re-layouts: 0.72 us -> 1.42 us
    ppermute x5, starting transfers between devices: 6.34 us -> 5.02 us  [swap(): lax.ppermute(x, axis, [(i, i ^ bit) for i in range(lax.axis_size(axis))])]
    ppermute x1, waiting for transfers between devices: 3.12 us -> 1.84 us  [strips(): lax.ppermute(grads, ring, [(i, i ^ 3) for i in range(2 * row_count)])]
    ppermute x1, starting transfers between devices: 0.6 us -> 1.77 us  [strips(): lax.ppermute(grads, ring, [(i, i ^ 3) for i in range(2 * row_count)])]
    ppermute x2, waiting for transfers between devices: 1.16 us -> 0.01 us  [the longest x1 0.01 us: strips(): across = lax.ppermute(tile, everyone, beside(1))]
    ppermute x5, waiting for transfers between devices: 6 us -> 7.03 us  [swap(): lax.ppermute(x, axis, [(i, i ^ bit) for i in range(lax.axis_size(axis))])]
    ppermute x2, starting transfers between devices: 4.13 us -> 3.39 us  [the longest x1 3.39 us: strips(): across = lax.ppermute(tile, everyone, beside(1))]
    unnamed x9, local copies, waits for them, and re-layouts: 0.72 us -> 1.42 us
  transfers between devices with their start and end apart: 8 -> 8, of which waited for: 6 -> 5; matrix products, arithmetic and copies ran while one was open for 0% -> 0% of each run, Pallas kernels for 1% -> 1%
where the time goes in v5:
time: 33.5 us; the launch traced here: 33.3 us
  Pallas kernels  11.8 us (35%)
  starting transfers between devices  10.2 us (30%)
  waiting for transfers between devices  8.88 us (27%)
  local copies, waits for them, and re-layouts  1.42 us (4%)
  between operations  0.67 us (2%)
    pallas_call x1, Pallas kernels, strip_call(): pl.pallas_call(functools.partial(kernel, factor), out_shape=(jax.ShapeDty...  10.8 us
    ppermute x5, waiting for transfers between devices, swap(): lax.ppermute(x, axis, [(i, i ^ bit) for i in range(lax.axis_size(axis))])  7.03 us
    ppermute x5, starting transfers between devices, swap(): lax.ppermute(x, axis, [(i, i ^ bit) for i in range(lax.axis_size(axis))])  5.02 us
    ppermute x1, starting transfers between devices, strips(): across = lax.ppermute(tile, everyone, beside(1))  3.39 us
    ppermute x1, waiting for transfers between devices, strips(): lax.ppermute(grads, ring, [(i, i ^ 3) for i in range(2 * row_count)])  1.84 us
    ppermute x1, starting transfers between devices, strips(): lax.ppermute(grads, ring, [(i, i ^ 3) for i in range(2 * row_count)])  1.77 us
    unnamed x9, local copies, waits for them, and re-layouts  1.42 us
    pallas_call x1, Pallas kernels, finish_call(): pl.pallas_call(finish, out_shape=(jax.ShapeDtypeStruct((2, 8, LANES), f32...  0.75 us
  transfers between devices with their start and end apart: 8, of which 5 were waited for; matrix products, arithmetic and copies ran while one was open for 0% of the time, Pallas kernels for 1%

profile of v5, /device:TPU:0, one launch (start us, length us, event | category | flops | bytes accessed | tf_op | source)
XLA Modules:
  0.0 33.3 jit_solution(14652063296208332024)
XLA Ops:
  0.6 0.0 copy-start.3
  0.6 0.7 %constant_dynamic-update-slice_fusion.1 = f32[4,8,128]{2,1,0:T(8,128)S(1)} fusion(f32[2,8,128]{2,1,0:T(8,128)} %param.5), kind=kLoop, calls=%fused_computation.7 | loop fusion | bytes 16384
  1.3 0.0 copy-done.3
  1.3 0.0 copy-start
  1.4 3.4 %collective-permute-start.2 = (f32[4,8,128]{2,1,0:T(8,128)S(1)}, f32[4,8,128]{2,1,0:T(8,128)S(1)}, u32[]{:S(2)}, u32[]{:S(2)}) collective-permute-start(f32[4,8,128]{2,1,0:T(8,128)S(1)} %constant_dynamic-update-slice_fusion), channel_id=1, source_target_pairs={{0,7},{1,4},{2,5},{3,6},{4,1},{5,2},{6,3},{7,0},{8,15},{9,12},{10,... | collective-permute-start | bytes 49160 | tf_op jit(solution)/shard_map/ppermute | solution.py:518
  4.7 0.0 collective-permute-start.1
  4.7 0.6 %collective-permute-start = (f32[4,8,128]{2,1,0:T(8,128)S(1)}, f32[4,8,128]{2,1,0:T(8,128)S(1)}, u32[]{:S(2)}, u32[]{:S(2)}) collective-permute-start(f32[4,8,128]{2,1,0:T(8,128)S(1)} %constant_dynamic-update-slice_fusion), channel_id=1, source_target_pairs={{0,4},{4,0},{8,12},{12,8},{1,5},{5,1},{9,13},{13,9},{2,6},{6,2},{1... | collective-permute-start | bytes 49160 | tf_op jit(solution)/shard_map/ppermute | solution.py:499
  5.4 0.0 copy-start.1
  5.4 0.0 copy-start.2
  5.4 0.0 copy-done
  5.4 0.7 %copy-done.1 = bf16[32,64]{1,0:T(8,128)(2,1)S(1)} copy-done((bf16[32,64]{1,0:T(8,128)(2,1)S(1)}, bf16[32,64]{1,0:T(8,128)(2,1)}, u32[]{:S(2)}) %copy-start.1) | copy-done | bytes 4120
  6.1 0.0 copy-done.2
  6.1 0.2 shard_map.84
  6.3 0.0 collective-permute-done.2
  6.3 0.1 slice_select_fusion
  6.4 2.1 %collective-permute-done = f32[4,8,128]{2,1,0:T(8,128)S(1)} collective-permute-done((f32[4,8,128]{2,1,0:T(8,128)S(1)}, f32[4,8,128]{2,1,0:T(8,128)S(1)}, u32[]{:S(2)}, u32[]{:S(2)}) %collective-permute-start) | collective-permute-done | bytes 16416 | tf_op jit(solution)/shard_map/ppermute | solution.py:499
  8.5 0.0 collective-permute-done.1
  8.5 0.1 slice_select_fusion.1
  8.6 0.1 maximum_maximum_fusion
  8.6 2.6 %collective-permute-start.3 = (f32[12,8,128]{2,1,0:T(8,128)S(1)}, f32[12,8,128]{2,1,0:T(8,128)S(1)}, u32[]{:S(2)}, u32[]{:S(2)}) collective-permute-start(f32[12,8,128]{2,1,0:T(8,128)S(1)} %maximum_maximum_fusion), channel_id=1, source_target_pairs={{0,8},{4,12},{8,0},{12,4},{1,9},{5,13},{9,1},{13,5},{2,10},{6,14},... | collective-permute-start | bytes 147464 | tf_op jit(solution)/shard_map/ppermute | solution.py:499
  11.2 0.1 pad_maximum_fusion.2.other_near
  11.3 2.9 %collective-permute-done.3 = f32[12,8,128]{2,1,0:T(8,128)S(1)} collective-permute-done((f32[12,8,128]{2,1,0:T(8,128)S(1)}, f32[12,8,128]{2,1,0:T(8,128)S(1)}, u32[]{:S(2)}, u32[]{:S(2)}) %collective-permute-start.3) | collective-permute-done | bytes 49184 | tf_op jit(solution)/shard_map/ppermute | solution.py:499
  14.2 10.8 %shard_map.85 = (f32[8,128]{1,0:T(8,128)S(1)}, f32[8,128]{1,0:T(8,128)S(1)}, f32[64,128]{1,0:T(8,128)S(1)}) custom-call(f32[2,4,8,128]{3,2,1,0:T(8,128)S(1)} %pad_maximum_fusion.1.own_near, f32[2,4,8,128]{3,2,1,0:T(8,128)S(1)} %bitcast.7, f32[4,8,128]{2,1,0:T(8,128)S(1)} %pad_maximum_fusion.2.other_near, f32[4,8,128]{2,1,0:T(8,128)S(1)} %slice.29.other_far, ...), custom_call_target="tpu_custom_call" | custom-call | tf_op jit(solution)/shard_map/pallas_call | solution.py:438
  25.0 0.0 collective-permute-start.4
  25.0 1.2 %collective-permute-done.4 = f32[64,128]{1,0:T(8,128)S(1)} collective-permute-done((f32[64,128]{1,0:T(8,128)S(1)}, f32[64,128]{1,0:T(8,128)S(1)}, u32[]{:S(2)}, u32[]{:S(2)}) %collective-permute-start.4) | collective-permute-done | bytes 32800 | tf_op jit(solution)/shard_map/ppermute | solution.py:499
  26.2 0.6 %collective-permute-start.6 = (f32[72,128]{1,0:T(8,128)S(1)}, f32[72,128]{1,0:T(8,128)S(1)}, u32[]{:S(2)}, u32[]{:S(2)}) collective-permute-start(f32[72,128]{1,0:T(8,128)S(1)} %pad_maximum_fusion), channel_id=1, source_target_pairs={{0,4},{4,0},{8,12},{12,8},{1,5},{5,1},{9,13},{13,9},{2,6},{6,2},{1... | collective-permute-start | bytes 110600 | tf_op jit(solution)/shard_map/ppermute | solution.py:499
  26.8 1.8 %collective-permute-start.7 = (f32[64,128]{1,0:T(8,128)S(1)}, f32[64,128]{1,0:T(8,128)S(1)}, u32[]{:S(2)}, u32[]{:S(2)}) collective-permute-start(f32[64,128]{1,0:T(8,128)S(1)} %add.8.sent), channel_id=1, source_target_pairs={{0,6},{2,4},{4,2},{6,0},{8,14},{10,12},{12,10},{14,8},{1,7},{3,5},... | collective-permute-start | bytes 98312 | tf_op jit(solution)/shard_map/ppermute | solution.py:532
  28.6 1.2 %collective-permute-start.5 = (f32[64,128]{1,0:T(8,128)S(1)}, f32[64,128]{1,0:T(8,128)S(1)}, u32[]{:S(2)}, u32[]{:S(2)}) collective-permute-start(f32[64,128]{1,0:T(8,128)S(1)} %add.8.sent), channel_id=1, source_target_pairs={{0,2},{2,0},{1,3},{3,1},{4,6},{6,4},{5,7},{7,5},{8,10},{10,8},{9,1... | collective-permute-start | bytes 98312 | tf_op jit(solution)/shard_map/ppermute | solution.py:499
  29.8 1.8 %collective-permute-done.7.across = f32[64,128]{1,0:T(8,128)S(1)} collective-permute-done((f32[64,128]{1,0:T(8,128)S(1)}, f32[64,128]{1,0:T(8,128)S(1)}, u32[]{:S(2)}, u32[]{:S(2)}) %collective-permute-start.7) | collective-permute-done | bytes 32800 | tf_op jit(solution)/shard_map/ppermute | solution.py:532
  31.6 0.9 %collective-permute-done.5.beyond = f32[64,128]{1,0:T(8,128)S(1)} collective-permute-done((f32[64,128]{1,0:T(8,128)S(1)}, f32[64,128]{1,0:T(8,128)S(1)}, u32[]{:S(2)}, u32[]{:S(2)}) %collective-permute-start.5) | collective-permute-done | bytes 32800 | tf_op jit(solution)/shard_map/ppermute | solution.py:499
  32.5 0.0 collective-permute-done.6.got
  32.5 0.8 %shard_map.86 = (f32[2,8,128]{2,1,0:T(8,128)}, f32[18,64]{1,0:T(8,128)}, f32[64,64]{1,0:T(8,128)}, f32[32,64]{1,0:T(8,128)}) custom-call(f32[64,128]{1,0:T(8,128)S(1)} %add.8.sent, f32[64,128]{1,0:T(8,128)S(1)} %collective-permute-done.5.beyond, f32[72,128]{1,0:T(8,128)S(1)} %collective-permute-done.6.got, f32[64,128]{1,0:T(8,128)S(1)} %collective-permute-done.7.across, ...), custom_call_target="tpu_custom_call" | custom-call | tf_op jit(solution)/shard_map/pallas_call | solution.py:484
  (6 shorter events, 0.0 us)
Async XLA Ops:
  0.6 0.7 %copy-start.3 = (f32[2,8,128]{2,1,0:T(8,128)S(1)}, f32[2,8,128]{2,1,0:T(8,128)}, u32[]{:S(2)}) copy-start(f32[2,8,128]{2,1,0:T(8,128)} %param.6) | copy-start | bytes 24580
  1.3 4.0 %copy-start = (bf16[64,64]{1,0:T(8,128)(2,1)S(1)}, bf16[64,64]{1,0:T(8,128)(2,1)}, u32[]{:S(2)}) copy-start(bf16[64,64]{1,0:T(8,128)(2,1)} %w2_in.1) | copy-start | bytes 24580
  1.4 5.0 %collective-permute-start.2 = (f32[4,8,128]{2,1,0:T(8,128)S(1)}, f32[4,8,128]{2,1,0:T(8,128)S(1)}, u32[]{:S(2)}, u32[]{:S(2)}) collective-permute-start(f32[4,8,128]{2,1,0:T(8,128)S(1)} %constant_dynamic-update-slice_fusion), channel_id=1, source_target_pairs={{0,7},{1,4},{2,5},{3,6},{4,1},{5,2},{6,3},{7,0},{8,15},{9,12},{10,... | collective-permute-start | bytes 49160 | tf_op jit(solution)/shard_map/ppermute | solution.py:518
  4.7 3.7 %collective-permute-start.1 = (f32[4,8,128]{2,1,0:T(8,128)S(1)}, f32[4,8,128]{2,1,0:T(8,128)S(1)}, u32[]{:S(2)}, u32[]{:S(2)}) collective-permute-start(f32[4,8,128]{2,1,0:T(8,128)S(1)} %constant_dynamic-update-slice_fusion), channel_id=1, source_target_pairs={{0,1},{1,2},{2,3},{3,0},{4,7},{5,4},{6,5},{7,6},{8,9},{9,10},{10,1... | collective-permute-start | bytes 49160 | tf_op jit(solution)/shard_map/ppermute | solution.py:519
  4.7 3.7 %collective-permute-start = (f32[4,8,128]{2,1,0:T(8,128)S(1)}, f32[4,8,128]{2,1,0:T(8,128)S(1)}, u32[]{:S(2)}, u32[]{:S(2)}) collective-permute-start(f32[4,8,128]{2,1,0:T(8,128)S(1)} %constant_dynamic-update-slice_fusion), channel_id=1, source_target_pairs={{0,4},{4,0},{8,12},{12,8},{1,5},{5,1},{9,13},{13,9},{2,6},{6,2},{1... | collective-permute-start | bytes 49160 | tf_op jit(solution)/shard_map/ppermute | solution.py:499
  5.4 0.7 %copy-start.1 = (bf16[32,64]{1,0:T(8,128)(2,1)S(1)}, bf16[32,64]{1,0:T(8,128)(2,1)}, u32[]{:S(2)}) copy-start(bf16[32,64]{1,0:T(8,128)(2,1)} %w3_in.1) | copy-start | bytes 12292
  5.4 0.7 %copy-start.2 = (bf16[64,18]{0,1:T(8,128)(2,1)S(1)}, bf16[64,18]{0,1:T(8,128)(2,1)}, u32[]{:S(2)}) copy-start(bf16[64,18]{0,1:T(8,128)(2,1)} %param.7) | copy-start | bytes 6916
  8.6 5.5 %collective-permute-start.3 = (f32[12,8,128]{2,1,0:T(8,128)S(1)}, f32[12,8,128]{2,1,0:T(8,128)S(1)}, u32[]{:S(2)}, u32[]{:S(2)}) collective-permute-start(f32[12,8,128]{2,1,0:T(8,128)S(1)} %maximum_maximum_fusion), channel_id=1, source_target_pairs={{0,8},{4,12},{8,0},{12,4},{1,9},{5,13},{9,1},{13,5},{2,10},{6,14},... | collective-permute-start | bytes 147464 | tf_op jit(solution)/shard_map/ppermute | solution.py:499
  25.0 1.2 %collective-permute-start.4 = (f32[64,128]{1,0:T(8,128)S(1)}, f32[64,128]{1,0:T(8,128)S(1)}, u32[]{:S(2)}, u32[]{:S(2)}) collective-permute-start(f32[64,128]{1,0:T(8,128)S(1)} %get-tuple-element.23), channel_id=1, source_target_pairs={{0,1},{1,0},{2,3},{3,2},{4,5},{5,4},{6,7},{7,6},{8,9},{9,8},{10,11... | collective-permute-start | bytes 98312 | tf_op jit(solution)/shard_map/ppermute | solution.py:499
  26.2 6.3 %collective-permute-start.6 = (f32[72,128]{1,0:T(8,128)S(1)}, f32[72,128]{1,0:T(8,128)S(1)}, u32[]{:S(2)}, u32[]{:S(2)}) collective-permute-start(f32[72,128]{1,0:T(8,128)S(1)} %pad_maximum_fusion), channel_id=1, source_target_pairs={{0,4},{4,0},{8,12},{12,8},{1,5},{5,1},{9,13},{13,9},{2,6},{6,2},{1... | collective-permute-start | bytes 110600 | tf_op jit(solution)/shard_map/ppermute | solution.py:499
  26.8 4.8 %collective-permute-start.7 = (f32[64,128]{1,0:T(8,128)S(1)}, f32[64,128]{1,0:T(8,128)S(1)}, u32[]{:S(2)}, u32[]{:S(2)}) collective-permute-start(f32[64,128]{1,0:T(8,128)S(1)} %add.8.sent), channel_id=1, source_target_pairs={{0,6},{2,4},{4,2},{6,0},{8,14},{10,12},{12,10},{14,8},{1,7},{3,5},... | collective-permute-start | bytes 98312 | tf_op jit(solution)/shard_map/ppermute | solution.py:532
  28.6 3.9 %collective-permute-start.5 = (f32[64,128]{1,0:T(8,128)S(1)}, f32[64,128]{1,0:T(8,128)S(1)}, u32[]{:S(2)}, u32[]{:S(2)}) collective-permute-start(f32[64,128]{1,0:T(8,128)S(1)} %add.8.sent), channel_id=1, source_target_pairs={{0,2},{2,0},{1,3},{3,1},{4,6},{6,4},{5,7},{7,5},{8,10},{10,8},{9,1... | collective-permute-start | bytes 98312 | tf_op jit(solution)/shard_map/ppermute | solution.py:499

commit v6 on v5

--- a/solution.py
+++ b/solution.py
@@ -175,6 +175,10 @@
                 s_all[0, c, pl.ds(row, 8), :] = narrow
             else:
                 up[c - 2, pl.ds(row, 8), :] = narrow
+
+    def close(shape):
+        column = lax.broadcasted_iota(jnp.int32, shape, 1) % HALF
+        return (column < 16) | (column >= 48)
 
     def pack(plane, part, turned=None):
         if turned is None:
@@ -342,23 +346,43 @@
 
         cells = PACKED * LANES
 
+        dense = step in (1, 2)
+        lines = [(0, r) for r in range(PACKED)]
+        if step > 0:
+            lines += [(1, r) for r in range(PACKED // 2 if dense else PACKED)]
+
+        def joined(value, part, r):
+            if part == 1 and dense:
+                here, there = value(r), pltpu.roll(value(r + 8), 32, 1)
+                return jnp.where(close(here.shape), here, there)
+            return value(r)
+
         def spread_row(part, which, r):
-            return jnp.broadcast_to(bq[part, which, r : r + 1, :], (8, LANES))
+            row = joined(lambda k: bq[part, which, k : k + 1, :], part, r)
+            return jnp.broadcast_to(row, (8, LANES))
+
+        def taps(part, c, ah, r):
+            return joined(lambda k: stencil(step, part, c, ah, k), part, r)
+
+        def columns(array):
+            def block(part, k):
+                at = (part * PACKED + k) * LANES
+                return array[:, at : at + LANES]
+
+            return jnp.concatenate(
+                [joined(functools.partial(block, part), part, r) for part, r in lines], 1
+            )
 
         third = []
-        for part in parts:
-            for r in range(PACKED):
-                pieces = []
-                for f in range(2):
-                    q0, q1, m = (spread_row(part, w, r) for w in (2 * f, 2 * f + 1, 4 + f))
-                    for ah in range(2):
-                        pieces.append(
-                            (q0 * stencil(step, part, 0, ah, r) + q1 * stencil(step, part, 1, ah, r))
-                            - m
-                        )
-                third.append(jnp.concatenate(pieces, 0).astype(bf16))
+        for part, r in lines:
+            pieces = []
+            for f in range(2):
+                q0, q1, m = (spread_row(part, w, r) for w in (2 * f, 2 * f + 1, 4 + f))
+                for ah in range(2):
+                    pieces.append((q0 * taps(part, 0, ah, r) + q1 * taps(part, 1, ah, r)) - m)
+            third.append(jnp.concatenate(pieces, 0).astype(bf16))
         third = jnp.concatenate(third, 1)
-        first, first_up, second, second_up = saved[step]
+        first, first_up, second, second_up = (columns(value) for value in saved[step])
         second = (dot(w3t[...], third) * gelu_half_slope(second, second_up)).astype(bf16)
         first = (dot(w2t[...], second) * gelu_half_slope(first, first_up)).astype(bf16)
 
@@ -373,19 +397,30 @@
         if step == 0:
             return gradients()
         out = dot(w1t[...], first)
+        weights = columns(cf[step])
 
         for part in parts:
             y = {}
-            for r in range(PACKED):
-                k = part * PACKED + r
+            for k, (piece, r) in enumerate(lines):
+                if piece != part:
+                    continue
                 lanes = slice(k * LANES, (k + 1) * LANES)
                 for c in range(2):
                     q0, q1 = spread_row(part, c, r), spread_row(part, 2 + c, r)
                     for ah in range(2):
                         y[c, ah, r] = (
-                            cf[step, 8 * ah : 8 * ah + 8, lanes] * q0
-                            + cf[step, 16 + 8 * ah : 24 + 8 * ah, lanes] * q1
+                            weights[8 * ah : 8 * ah + 8, lanes] * q0
+                            + weights[16 + 8 * ah : 24 + 8 * ah, lanes] * q1
                         ) + out[16 * c + 8 * ah : 16 * c + 8 * ah + 8, lanes]
+            if part == 1 and dense:
+                for c in range(2):
+                    for ah in range(2):
+                        for r in range(PACKED // 2):
+                            value = y[c, ah, r]
+                            y[c, ah, r + 8] = jnp.where(
+                                close(value.shape), pltpu.roll(value, LANES - 32, 1), 0.0
+                            )
+                            y[c, ah, r] = jnp.where(close(value.shape), value, 0.0)
             for c in range(2):
                 rows = []
                 for m in range(PACKED):

time: 33.5 us -> 33.2 us (level)
  no operation moved by 1% of the time
where the time goes in v6:
time: 33.2 us; the launch traced here: 33 us
  Pallas kernels  11.5 us (35%)
  starting transfers between devices  10.2 us (31%)
  waiting for transfers between devices  8.88 us (27%)
  local copies, waits for them, and re-layouts  1.42 us (4%)
  between operations  0.67 us (2%)
    pallas_call x1, Pallas kernels, strip_call(): pl.pallas_call(functools.partial(kernel, factor), out_shape=(jax.ShapeDty...  10.5 us
    ppermute x5, waiting for transfers between devices, swap(): lax.ppermute(x, axis, [(i, i ^ bit) for i in range(lax.axis_size(axis))])  7.03 us
    ppermute x5, starting transfers between devices, swap(): lax.ppermute(x, axis, [(i, i ^ bit) for i in range(lax.axis_size(axis))])  5.02 us
    ppermute x1, starting transfers between devices, strips(): across = lax.ppermute(tile, everyone, beside(1))  3.39 us
    ppermute x1, waiting for transfers between devices, strips(): lax.ppermute(grads, ring, [(i, i ^ 3) for i in range(2 * row_count)])  1.84 us
    ppermute x1, starting transfers between devices, strips(): lax.ppermute(grads, ring, [(i, i ^ 3) for i in range(2 * row_count)])  1.77 us
    unnamed x9, local copies, waits for them, and re-layouts  1.42 us
    pallas_call x1, Pallas kernels, finish_call(): pl.pallas_call(finish, out_shape=(jax.ShapeDtypeStruct((2, 8, LANES), f32...  0.75 us
  transfers between devices with their start and end apart: 8, of which 5 were waited for; matrix products, arithmetic and copies ran while one was open for 0% of the time, Pallas kernels for 1%

profile of v6, /device:TPU:0, one launch (start us, length us, event | category | flops | bytes accessed | tf_op | source)
XLA Modules:
  0.0 33.0 jit_solution(2534622924555260047)
XLA Ops:
  0.6 0.0 copy-start.3
  0.6 0.7 %constant_dynamic-update-slice_fusion.1 = f32[4,8,128]{2,1,0:T(8,128)S(1)} fusion(f32[2,8,128]{2,1,0:T(8,128)} %param.5), kind=kLoop, calls=%fused_computation.7 | loop fusion | bytes 16384
  1.3 0.0 copy-done.3
  1.3 0.0 copy-start
  1.4 3.4 %collective-permute-start.2 = (f32[4,8,128]{2,1,0:T(8,128)S(1)}, f32[4,8,128]{2,1,0:T(8,128)S(1)}, u32[]{:S(2)}, u32[]{:S(2)}) collective-permute-start(f32[4,8,128]{2,1,0:T(8,128)S(1)} %constant_dynamic-update-slice_fusion), channel_id=1, source_target_pairs={{0,7},{1,4},{2,5},{3,6},{4,1},{5,2},{6,3},{7,0},{8,15},{9,12},{10,... | collective-permute-start | bytes 49160 | tf_op jit(solution)/shard_map/ppermute | solution.py:553
  4.7 0.0 collective-permute-start.1
  4.7 0.6 %collective-permute-start = (f32[4,8,128]{2,1,0:T(8,128)S(1)}, f32[4,8,128]{2,1,0:T(8,128)S(1)}, u32[]{:S(2)}, u32[]{:S(2)}) collective-permute-start(f32[4,8,128]{2,1,0:T(8,128)S(1)} %constant_dynamic-update-slice_fusion), channel_id=1, source_target_pairs={{0,4},{4,0},{8,12},{12,8},{1,5},{5,1},{9,13},{13,9},{2,6},{6,2},{1... | collective-permute-start | bytes 49160 | tf_op jit(solution)/shard_map/ppermute | solution.py:534
  5.4 0.0 copy-start.1
  5.4 0.0 copy-start.2
  5.4 0.0 copy-done
  5.4 0.7 %copy-done.1 = bf16[32,64]{1,0:T(8,128)(2,1)S(1)} copy-done((bf16[32,64]{1,0:T(8,128)(2,1)S(1)}, bf16[32,64]{1,0:T(8,128)(2,1)}, u32[]{:S(2)}) %copy-start.1) | copy-done | bytes 4120
  6.1 0.0 copy-done.2
  6.1 0.2 shard_map.84
  6.3 0.0 collective-permute-done.2
  6.3 0.1 slice_select_fusion
  6.4 2.1 %collective-permute-done = f32[4,8,128]{2,1,0:T(8,128)S(1)} collective-permute-done((f32[4,8,128]{2,1,0:T(8,128)S(1)}, f32[4,8,128]{2,1,0:T(8,128)S(1)}, u32[]{:S(2)}, u32[]{:S(2)}) %collective-permute-start) | collective-permute-done | bytes 16416 | tf_op jit(solution)/shard_map/ppermute | solution.py:534
  8.5 0.0 collective-permute-done.1
  8.5 0.1 slice_select_fusion.1
  8.6 0.1 maximum_maximum_fusion
  8.6 2.6 %collective-permute-start.3 = (f32[12,8,128]{2,1,0:T(8,128)S(1)}, f32[12,8,128]{2,1,0:T(8,128)S(1)}, u32[]{:S(2)}, u32[]{:S(2)}) collective-permute-start(f32[12,8,128]{2,1,0:T(8,128)S(1)} %maximum_maximum_fusion), channel_id=1, source_target_pairs={{0,8},{4,12},{8,0},{12,4},{1,9},{5,13},{9,1},{13,5},{2,10},{6,14},... | collective-permute-start | bytes 147464 | tf_op jit(solution)/shard_map/ppermute | solution.py:534
  11.2 0.1 pad_maximum_fusion.2.other_near
  11.3 2.9 %collective-permute-done.3 = f32[12,8,128]{2,1,0:T(8,128)S(1)} collective-permute-done((f32[12,8,128]{2,1,0:T(8,128)S(1)}, f32[12,8,128]{2,1,0:T(8,128)S(1)}, u32[]{:S(2)}, u32[]{:S(2)}) %collective-permute-start.3) | collective-permute-done | bytes 49184 | tf_op jit(solution)/shard_map/ppermute | solution.py:534
  14.2 10.5 %shard_map.85 = (f32[8,128]{1,0:T(8,128)S(1)}, f32[8,128]{1,0:T(8,128)S(1)}, f32[64,128]{1,0:T(8,128)S(1)}) custom-call(f32[2,4,8,128]{3,2,1,0:T(8,128)S(1)} %pad_maximum_fusion.1.own_near, f32[2,4,8,128]{3,2,1,0:T(8,128)S(1)} %bitcast.7, f32[4,8,128]{2,1,0:T(8,128)S(1)} %pad_maximum_fusion.2.other_near, f32[4,8,128]{2,1,0:T(8,128)S(1)} %slice.29.other_far, ...), custom_call_target="tpu_custom_call" | custom-call | tf_op jit(solution)/shard_map/pallas_call | solution.py:473
  24.7 0.0 collective-permute-start.4
  24.7 1.2 %collective-permute-done.4 = f32[64,128]{1,0:T(8,128)S(1)} collective-permute-done((f32[64,128]{1,0:T(8,128)S(1)}, f32[64,128]{1,0:T(8,128)S(1)}, u32[]{:S(2)}, u32[]{:S(2)}) %collective-permute-start.4) | collective-permute-done | bytes 32800 | tf_op jit(solution)/shard_map/ppermute | solution.py:534
  26.0 0.6 %collective-permute-start.6 = (f32[72,128]{1,0:T(8,128)S(1)}, f32[72,128]{1,0:T(8,128)S(1)}, u32[]{:S(2)}, u32[]{:S(2)}) collective-permute-start(f32[72,128]{1,0:T(8,128)S(1)} %pad_maximum_fusion), channel_id=1, source_target_pairs={{0,4},{4,0},{8,12},{12,8},{1,5},{5,1},{9,13},{13,9},{2,6},{6,2},{1... | collective-permute-start | bytes 110600 | tf_op jit(solution)/shard_map/ppermute | solution.py:534
  26.5 1.8 %collective-permute-start.7 = (f32[64,128]{1,0:T(8,128)S(1)}, f32[64,128]{1,0:T(8,128)S(1)}, u32[]{:S(2)}, u32[]{:S(2)}) collective-permute-start(f32[64,128]{1,0:T(8,128)S(1)} %add.8.sent), channel_id=1, source_target_pairs={{0,6},{2,4},{4,2},{6,0},{8,14},{10,12},{12,10},{14,8},{1,7},{3,5},... | collective-permute-start | bytes 98312 | tf_op jit(solution)/shard_map/ppermute | solution.py:567
  28.3 1.2 %collective-permute-start.5 = (f32[64,128]{1,0:T(8,128)S(1)}, f32[64,128]{1,0:T(8,128)S(1)}, u32[]{:S(2)}, u32[]{:S(2)}) collective-permute-start(f32[64,128]{1,0:T(8,128)S(1)} %add.8.sent), channel_id=1, source_target_pairs={{0,2},{2,0},{1,3},{3,1},{4,6},{6,4},{5,7},{7,5},{8,10},{10,8},{9,1... | collective-permute-start | bytes 98312 | tf_op jit(solution)/shard_map/ppermute | solution.py:534
  29.5 1.8 %collective-permute-done.7.across = f32[64,128]{1,0:T(8,128)S(1)} collective-permute-done((f32[64,128]{1,0:T(8,128)S(1)}, f32[64,128]{1,0:T(8,128)S(1)}, u32[]{:S(2)}, u32[]{:S(2)}) %collective-permute-start.7) | collective-permute-done | bytes 32800 | tf_op jit(solution)/shard_map/ppermute | solution.py:567
  31.3 0.9 %collective-permute-done.5.beyond = f32[64,128]{1,0:T(8,128)S(1)} collective-permute-done((f32[64,128]{1,0:T(8,128)S(1)}, f32[64,128]{1,0:T(8,128)S(1)}, u32[]{:S(2)}, u32[]{:S(2)}) %collective-permute-start.5) | collective-permute-done | bytes 32800 | tf_op jit(solution)/shard_map/ppermute | solution.py:534
  32.2 0.0 collective-permute-done.6.got
  32.2 0.8 %shard_map.86 = (f32[2,8,128]{2,1,0:T(8,128)}, f32[18,64]{1,0:T(8,128)}, f32[64,64]{1,0:T(8,128)}, f32[32,64]{1,0:T(8,128)}) custom-call(f32[64,128]{1,0:T(8,128)S(1)} %add.8.sent, f32[64,128]{1,0:T(8,128)S(1)} %collective-permute-done.5.beyond, f32[72,128]{1,0:T(8,128)S(1)} %collective-permute-done.6.got, f32[64,128]{1,0:T(8,128)S(1)} %collective-permute-done.7.across, ...), custom_call_target="tpu_custom_call" | custom-call | tf_op jit(solution)/shard_map/pallas_call | solution.py:519
  (6 shorter events, 0.0 us)
Async XLA Ops:
  0.6 0.7 %copy-start.3 = (f32[2,8,128]{2,1,0:T(8,128)S(1)}, f32[2,8,128]{2,1,0:T(8,128)}, u32[]{:S(2)}) copy-start(f32[2,8,128]{2,1,0:T(8,128)} %param.6) | copy-start | bytes 24580
  1.3 4.0 %copy-start = (bf16[64,64]{1,0:T(8,128)(2,1)S(1)}, bf16[64,64]{1,0:T(8,128)(2,1)}, u32[]{:S(2)}) copy-start(bf16[64,64]{1,0:T(8,128)(2,1)} %w2_in.1) | copy-start | bytes 24580
  1.4 5.0 %collective-permute-start.2 = (f32[4,8,128]{2,1,0:T(8,128)S(1)}, f32[4,8,128]{2,1,0:T(8,128)S(1)}, u32[]{:S(2)}, u32[]{:S(2)}) collective-permute-start(f32[4,8,128]{2,1,0:T(8,128)S(1)} %constant_dynamic-update-slice_fusion), channel_id=1, source_target_pairs={{0,7},{1,4},{2,5},{3,6},{4,1},{5,2},{6,3},{7,0},{8,15},{9,12},{10,... | collective-permute-start | bytes 49160 | tf_op jit(solution)/shard_map/ppermute | solution.py:553
  4.7 3.7 %collective-permute-start.1 = (f32[4,8,128]{2,1,0:T(8,128)S(1)}, f32[4,8,128]{2,1,0:T(8,128)S(1)}, u32[]{:S(2)}, u32[]{:S(2)}) collective-permute-start(f32[4,8,128]{2,1,0:T(8,128)S(1)} %constant_dynamic-update-slice_fusion), channel_id=1, source_target_pairs={{0,1},{1,2},{2,3},{3,0},{4,7},{5,4},{6,5},{7,6},{8,9},{9,10},{10,1... | collective-permute-start | bytes 49160 | tf_op jit(solution)/shard_map/ppermute | solution.py:554
  4.7 3.7 %collective-permute-start = (f32[4,8,128]{2,1,0:T(8,128)S(1)}, f32[4,8,128]{2,1,0:T(8,128)S(1)}, u32[]{:S(2)}, u32[]{:S(2)}) collective-permute-start(f32[4,8,128]{2,1,0:T(8,128)S(1)} %constant_dynamic-update-slice_fusion), channel_id=1, source_target_pairs={{0,4},{4,0},{8,12},{12,8},{1,5},{5,1},{9,13},{13,9},{2,6},{6,2},{1... | collective-permute-start | bytes 49160 | tf_op jit(solution)/shard_map/ppermute | solution.py:534
  5.4 0.7 %copy-start.1 = (bf16[32,64]{1,0:T(8,128)(2,1)S(1)}, bf16[32,64]{1,0:T(8,128)(2,1)}, u32[]{:S(2)}) copy-start(bf16[32,64]{1,0:T(8,128)(2,1)} %w3_in.1) | copy-start | bytes 12292
  5.4 0.7 %copy-start.2 = (bf16[64,18]{0,1:T(8,128)(2,1)S(1)}, bf16[64,18]{0,1:T(8,128)(2,1)}, u32[]{:S(2)}) copy-start(bf16[64,18]{0,1:T(8,128)(2,1)} %param.7) | copy-start | bytes 6916
  8.6 5.5 %collective-permute-start.3 = (f32[12,8,128]{2,1,0:T(8,128)S(1)}, f32[12,8,128]{2,1,0:T(8,128)S(1)}, u32[]{:S(2)}, u32[]{:S(2)}) collective-permute-start(f32[12,8,128]{2,1,0:T(8,128)S(1)} %maximum_maximum_fusion), channel_id=1, source_target_pairs={{0,8},{4,12},{8,0},{12,4},{1,9},{5,13},{9,1},{13,5},{2,10},{6,14},... | collective-permute-start | bytes 147464 | tf_op jit(solution)/shard_map/ppermute | solution.py:534
  24.7 1.2 %collective-permute-start.4 = (f32[64,128]{1,0:T(8,128)S(1)}, f32[64,128]{1,0:T(8,128)S(1)}, u32[]{:S(2)}, u32[]{:S(2)}) collective-permute-start(f32[64,128]{1,0:T(8,128)S(1)} %get-tuple-element.23), channel_id=1, source_target_pairs={{0,1},{1,0},{2,3},{3,2},{4,5},{5,4},{6,7},{7,6},{8,9},{9,8},{10,11... | collective-permute-start | bytes 98312 | tf_op jit(solution)/shard_map/ppermute | solution.py:534
  26.0 6.3 %collective-permute-start.6 = (f32[72,128]{1,0:T(8,128)S(1)}, f32[72,128]{1,0:T(8,128)S(1)}, u32[]{:S(2)}, u32[]{:S(2)}) collective-permute-start(f32[72,128]{1,0:T(8,128)S(1)} %pad_maximum_fusion), channel_id=1, source_target_pairs={{0,4},{4,0},{8,12},{12,8},{1,5},{5,1},{9,13},{13,9},{2,6},{6,2},{1... | collective-permute-start | bytes 110600 | tf_op jit(solution)/shard_map/ppermute | solution.py:534
  26.5 4.8 %collective-permute-start.7 = (f32[64,128]{1,0:T(8,128)S(1)}, f32[64,128]{1,0:T(8,128)S(1)}, u32[]{:S(2)}, u32[]{:S(2)}) collective-permute-start(f32[64,128]{1,0:T(8,128)S(1)} %add.8.sent), channel_id=1, source_target_pairs={{0,6},{2,4},{4,2},{6,0},{8,14},{10,12},{12,10},{14,8},{1,7},{3,5},... | collective-permute-start | bytes 98312 | tf_op jit(solution)/shard_map/ppermute | solution.py:567
  28.3 3.9 %collective-permute-start.5 = (f32[64,128]{1,0:T(8,128)S(1)}, f32[64,128]{1,0:T(8,128)S(1)}, u32[]{:S(2)}, u32[]{:S(2)}) collective-permute-start(f32[64,128]{1,0:T(8,128)S(1)} %add.8.sent), channel_id=1, source_target_pairs={{0,2},{2,0},{1,3},{3,1},{4,6},{6,4},{5,7},{7,5},{8,10},{10,8},{9,1... | collective-permute-start | bytes 98312 | tf_op jit(solution)/shard_map/ppermute | solution.py:534

commit v7 on v6

--- a/solution.py
+++ b/solution.py
@@ -388,7 +388,7 @@
 
         def gradients():
             terms = (
-                dot_cells(first[:, :cells], x_all[step]),
+                dot_cells(x_all[step], first[:, :cells]),
                 dot_cells(second[:, :cells], a1_all[step]),
                 dot_cells(third[:, :cells], a2_all[step]),
             )
@@ -454,14 +454,10 @@
     for step in reversed(range(STEPS)):
         total = backward(step, total)
     grads[:, 0:64] = factor * total[1]
-    first = lax.dot_general(
-        pick_taps((TAPS, 32), 0),
-        factor * total[0],
-        (((1,), (1,)), ((), ())),
-        precision=lax.Precision.HIGHEST,
-        preferred_element_type=f32,
-    )
-    grads[0:TAPS, 64:128] = first
+    first = factor * total[0]
+    for c in range(2):
+        for a in range(3):
+            grads[9 * c + 3 * a : 9 * c + 3 * a + 3, 64:128] = first[16 * c + 4 * a : 16 * c + 4 * a + 3]
     grads[TAPS:32, 64:128] = jnp.zeros((32 - TAPS, CHANNELS), f32)
     grads[32:64, 64:128] = (factor * correction_gain) * total[2]
 

time: 33.2 us -> 33.1 us (level)
  no operation moved by 1% of the time
where the time goes in v7:
time: 33.1 us; the launch traced here: 32.9 us
  Pallas kernels  11.4 us (34%)
  starting transfers between devices  10.2 us (31%)
  waiting for transfers between devices  8.86 us (27%)
  local copies, waits for them, and re-layouts  1.42 us (4%)
  between operations  0.67 us (2%)
    pallas_call x1, Pallas kernels, strip_call(): pl.pallas_call(functools.partial(kernel, factor), out_shape=(jax.ShapeDty...  10.4 us
    ppermute x5, waiting for transfers between devices, swap(): lax.ppermute(x, axis, [(i, i ^ bit) for i in range(lax.axis_size(axis))])  7.02 us
    ppermute x5, starting transfers between devices, swap(): lax.ppermute(x, axis, [(i, i ^ bit) for i in range(lax.axis_size(axis))])  5.02 us
    ppermute x1, starting transfers between devices, strips(): across = lax.ppermute(tile, everyone, beside(1))  3.39 us
    ppermute x1, waiting for transfers between devices, strips(): lax.ppermute(grads, ring, [(i, i ^ 3) for i in range(2 * row_count)])  1.83 us
    ppermute x1, starting transfers between devices, strips(): lax.ppermute(grads, ring, [(i, i ^ 3) for i in range(2 * row_count)])  1.77 us
    unnamed x9, local copies, waits for them, and re-layouts  1.42 us
    pallas_call x1, Pallas kernels, finish_call(): pl.pallas_call(finish, out_shape=(jax.ShapeDtypeStruct((2, 8, LANES), f32...  0.75 us
  transfers between devices with their start and end apart: 8, of which 5 were waited for; matrix products, arithmetic and copies ran while one was open for 0% of the time, Pallas kernels for 1%

profile of v7, /device:TPU:0, one launch (start us, length us, event | category | flops | bytes accessed | tf_op | source)
XLA Modules:
  0.0 32.9 jit_solution(4090658950867733836)
XLA Ops:
  0.6 0.0 copy-start.3
  0.6 0.7 %constant_dynamic-update-slice_fusion.1 = f32[4,8,128]{2,1,0:T(8,128)S(1)} fusion(f32[2,8,128]{2,1,0:T(8,128)} %param.5), kind=kLoop, calls=%fused_computation.7 | loop fusion | bytes 16384
  1.3 0.0 copy-done.3
  1.3 0.0 copy-start
  1.4 3.4 %collective-permute-start.2 = (f32[4,8,128]{2,1,0:T(8,128)S(1)}, f32[4,8,128]{2,1,0:T(8,128)S(1)}, u32[]{:S(2)}, u32[]{:S(2)}) collective-permute-start(f32[4,8,128]{2,1,0:T(8,128)S(1)} %constant_dynamic-update-slice_fusion), channel_id=1, source_target_pairs={{0,7},{1,4},{2,5},{3,6},{4,1},{5,2},{6,3},{7,0},{8,15},{9,12},{10,... | collective-permute-start | bytes 49160 | tf_op jit(solution)/shard_map/ppermute | solution.py:549
  4.7 0.0 collective-permute-start.1
  4.7 0.6 %collective-permute-start = (f32[4,8,128]{2,1,0:T(8,128)S(1)}, f32[4,8,128]{2,1,0:T(8,128)S(1)}, u32[]{:S(2)}, u32[]{:S(2)}) collective-permute-start(f32[4,8,128]{2,1,0:T(8,128)S(1)} %constant_dynamic-update-slice_fusion), channel_id=1, source_target_pairs={{0,4},{4,0},{8,12},{12,8},{1,5},{5,1},{9,13},{13,9},{2,6},{6,2},{1... | collective-permute-start | bytes 49160 | tf_op jit(solution)/shard_map/ppermute | solution.py:530
  5.4 0.0 copy-start.1
  5.4 0.0 copy-start.2
  5.4 0.0 copy-done
  5.4 0.7 %copy-done.1 = bf16[32,64]{1,0:T(8,128)(2,1)S(1)} copy-done((bf16[32,64]{1,0:T(8,128)(2,1)S(1)}, bf16[32,64]{1,0:T(8,128)(2,1)}, u32[]{:S(2)}) %copy-start.1) | copy-done | bytes 4120
  6.1 0.0 copy-done.2
  6.1 0.2 shard_map.84
  6.3 0.0 collective-permute-done.2
  6.3 0.1 slice_select_fusion
  6.4 2.1 %collective-permute-done = f32[4,8,128]{2,1,0:T(8,128)S(1)} collective-permute-done((f32[4,8,128]{2,1,0:T(8,128)S(1)}, f32[4,8,128]{2,1,0:T(8,128)S(1)}, u32[]{:S(2)}, u32[]{:S(2)}) %collective-permute-start) | collective-permute-done | bytes 16416 | tf_op jit(solution)/shard_map/ppermute | solution.py:530
  8.5 0.0 collective-permute-done.1
  8.5 0.1 slice_select_fusion.1
  8.6 0.1 maximum_maximum_fusion
  8.6 2.6 %collective-permute-start.3 = (f32[12,8,128]{2,1,0:T(8,128)S(1)}, f32[12,8,128]{2,1,0:T(8,128)S(1)}, u32[]{:S(2)}, u32[]{:S(2)}) collective-permute-start(f32[12,8,128]{2,1,0:T(8,128)S(1)} %maximum_maximum_fusion), channel_id=1, source_target_pairs={{0,8},{4,12},{8,0},{12,4},{1,9},{5,13},{9,1},{13,5},{2,10},{6,14},... | collective-permute-start | bytes 147464 | tf_op jit(solution)/shard_map/ppermute | solution.py:530
  11.2 0.1 pad_maximum_fusion.2.other_near
  11.3 2.9 %collective-permute-done.3 = f32[12,8,128]{2,1,0:T(8,128)S(1)} collective-permute-done((f32[12,8,128]{2,1,0:T(8,128)S(1)}, f32[12,8,128]{2,1,0:T(8,128)S(1)}, u32[]{:S(2)}, u32[]{:S(2)}) %collective-permute-start.3) | collective-permute-done | bytes 49184 | tf_op jit(solution)/shard_map/ppermute | solution.py:530
  14.2 10.4 %shard_map.85 = (f32[8,128]{1,0:T(8,128)S(1)}, f32[8,128]{1,0:T(8,128)S(1)}, f32[64,128]{1,0:T(8,128)S(1)}) custom-call(f32[2,4,8,128]{3,2,1,0:T(8,128)S(1)} %pad_maximum_fusion.1.own_near, f32[2,4,8,128]{3,2,1,0:T(8,128)S(1)} %bitcast.7, f32[4,8,128]{2,1,0:T(8,128)S(1)} %pad_maximum_fusion.2.other_near, f32[4,8,128]{2,1,0:T(8,128)S(1)} %slice.29.other_far, ...), custom_call_target="tpu_custom_call" | custom-call | tf_op jit(solution)/shard_map/pallas_call | solution.py:469
  24.6 0.0 collective-permute-start.4
  24.6 1.2 %collective-permute-done.4 = f32[64,128]{1,0:T(8,128)S(1)} collective-permute-done((f32[64,128]{1,0:T(8,128)S(1)}, f32[64,128]{1,0:T(8,128)S(1)}, u32[]{:S(2)}, u32[]{:S(2)}) %collective-permute-start.4) | collective-permute-done | bytes 32800 | tf_op jit(solution)/shard_map/ppermute | solution.py:530
  25.9 0.6 %collective-permute-start.6 = (f32[72,128]{1,0:T(8,128)S(1)}, f32[72,128]{1,0:T(8,128)S(1)}, u32[]{:S(2)}, u32[]{:S(2)}) collective-permute-start(f32[72,128]{1,0:T(8,128)S(1)} %pad_maximum_fusion), channel_id=1, source_target_pairs={{0,4},{4,0},{8,12},{12,8},{1,5},{5,1},{9,13},{13,9},{2,6},{6,2},{1... | collective-permute-start | bytes 110600 | tf_op jit(solution)/shard_map/ppermute | solution.py:530
  26.4 1.8 %collective-permute-start.7 = (f32[64,128]{1,0:T(8,128)S(1)}, f32[64,128]{1,0:T(8,128)S(1)}, u32[]{:S(2)}, u32[]{:S(2)}) collective-permute-start(f32[64,128]{1,0:T(8,128)S(1)} %add.8.sent), channel_id=1, source_target_pairs={{0,6},{2,4},{4,2},{6,0},{8,14},{10,12},{12,10},{14,8},{1,7},{3,5},... | collective-permute-start | bytes 98312 | tf_op jit(solution)/shard_map/ppermute | solution.py:563
  28.2 1.2 %collective-permute-start.5 = (f32[64,128]{1,0:T(8,128)S(1)}, f32[64,128]{1,0:T(8,128)S(1)}, u32[]{:S(2)}, u32[]{:S(2)}) collective-permute-start(f32[64,128]{1,0:T(8,128)S(1)} %add.8.sent), channel_id=1, source_target_pairs={{0,2},{2,0},{1,3},{3,1},{4,6},{6,4},{5,7},{7,5},{8,10},{10,8},{9,1... | collective-permute-start | bytes 98312 | tf_op jit(solution)/shard_map/ppermute | solution.py:530
  29.4 1.8 %collective-permute-done.7.across = f32[64,128]{1,0:T(8,128)S(1)} collective-permute-done((f32[64,128]{1,0:T(8,128)S(1)}, f32[64,128]{1,0:T(8,128)S(1)}, u32[]{:S(2)}, u32[]{:S(2)}) %collective-permute-start.7) | collective-permute-done | bytes 32800 | tf_op jit(solution)/shard_map/ppermute | solution.py:563
  31.2 0.9 %collective-permute-done.5.beyond = f32[64,128]{1,0:T(8,128)S(1)} collective-permute-done((f32[64,128]{1,0:T(8,128)S(1)}, f32[64,128]{1,0:T(8,128)S(1)}, u32[]{:S(2)}, u32[]{:S(2)}) %collective-permute-start.5) | collective-permute-done | bytes 32800 | tf_op jit(solution)/shard_map/ppermute | solution.py:530
  32.1 0.0 collective-permute-done.6.got
  32.1 0.8 %shard_map.86 = (f32[2,8,128]{2,1,0:T(8,128)}, f32[18,64]{1,0:T(8,128)}, f32[64,64]{1,0:T(8,128)}, f32[32,64]{1,0:T(8,128)}) custom-call(f32[64,128]{1,0:T(8,128)S(1)} %add.8.sent, f32[64,128]{1,0:T(8,128)S(1)} %collective-permute-done.5.beyond, f32[72,128]{1,0:T(8,128)S(1)} %collective-permute-done.6.got, f32[64,128]{1,0:T(8,128)S(1)} %collective-permute-done.7.across, ...), custom_call_target="tpu_custom_call" | custom-call | tf_op jit(solution)/shard_map/pallas_call | solution.py:515
  (6 shorter events, 0.0 us)
Async XLA Ops:
  0.6 0.7 %copy-start.3 = (f32[2,8,128]{2,1,0:T(8,128)S(1)}, f32[2,8,128]{2,1,0:T(8,128)}, u32[]{:S(2)}) copy-start(f32[2,8,128]{2,1,0:T(8,128)} %param.6) | copy-start | bytes 24580
  1.3 4.0 %copy-start = (bf16[64,64]{1,0:T(8,128)(2,1)S(1)}, bf16[64,64]{1,0:T(8,128)(2,1)}, u32[]{:S(2)}) copy-start(bf16[64,64]{1,0:T(8,128)(2,1)} %w2_in.1) | copy-start | bytes 24580
  1.4 5.0 %collective-permute-start.2 = (f32[4,8,128]{2,1,0:T(8,128)S(1)}, f32[4,8,128]{2,1,0:T(8,128)S(1)}, u32[]{:S(2)}, u32[]{:S(2)}) collective-permute-start(f32[4,8,128]{2,1,0:T(8,128)S(1)} %constant_dynamic-update-slice_fusion), channel_id=1, source_target_pairs={{0,7},{1,4},{2,5},{3,6},{4,1},{5,2},{6,3},{7,0},{8,15},{9,12},{10,... | collective-permute-start | bytes 49160 | tf_op jit(solution)/shard_map/ppermute | solution.py:549
  4.7 3.7 %collective-permute-start.1 = (f32[4,8,128]{2,1,0:T(8,128)S(1)}, f32[4,8,128]{2,1,0:T(8,128)S(1)}, u32[]{:S(2)}, u32[]{:S(2)}) collective-permute-start(f32[4,8,128]{2,1,0:T(8,128)S(1)} %constant_dynamic-update-slice_fusion), channel_id=1, source_target_pairs={{0,1},{1,2},{2,3},{3,0},{4,7},{5,4},{6,5},{7,6},{8,9},{9,10},{10,1... | collective-permute-start | bytes 49160 | tf_op jit(solution)/shard_map/ppermute | solution.py:550
  4.7 3.7 %collective-permute-start = (f32[4,8,128]{2,1,0:T(8,128)S(1)}, f32[4,8,128]{2,1,0:T(8,128)S(1)}, u32[]{:S(2)}, u32[]{:S(2)}) collective-permute-start(f32[4,8,128]{2,1,0:T(8,128)S(1)} %constant_dynamic-update-slice_fusion), channel_id=1, source_target_pairs={{0,4},{4,0},{8,12},{12,8},{1,5},{5,1},{9,13},{13,9},{2,6},{6,2},{1... | collective-permute-start | bytes 49160 | tf_op jit(solution)/shard_map/ppermute | solution.py:530
  5.4 0.7 %copy-start.1 = (bf16[32,64]{1,0:T(8,128)(2,1)S(1)}, bf16[32,64]{1,0:T(8,128)(2,1)}, u32[]{:S(2)}) copy-start(bf16[32,64]{1,0:T(8,128)(2,1)} %w3_in.1) | copy-start | bytes 12292
  5.4 0.7 %copy-start.2 = (bf16[64,18]{0,1:T(8,128)(2,1)S(1)}, bf16[64,18]{0,1:T(8,128)(2,1)}, u32[]{:S(2)}) copy-start(bf16[64,18]{0,1:T(8,128)(2,1)} %param.7) | copy-start | bytes 6916
  8.6 5.5 %collective-permute-start.3 = (f32[12,8,128]{2,1,0:T(8,128)S(1)}, f32[12,8,128]{2,1,0:T(8,128)S(1)}, u32[]{:S(2)}, u32[]{:S(2)}) collective-permute-start(f32[12,8,128]{2,1,0:T(8,128)S(1)} %maximum_maximum_fusion), channel_id=1, source_target_pairs={{0,8},{4,12},{8,0},{12,4},{1,9},{5,13},{9,1},{13,5},{2,10},{6,14},... | collective-permute-start | bytes 147464 | tf_op jit(solution)/shard_map/ppermute | solution.py:530
  24.6 1.2 %collective-permute-start.4 = (f32[64,128]{1,0:T(8,128)S(1)}, f32[64,128]{1,0:T(8,128)S(1)}, u32[]{:S(2)}, u32[]{:S(2)}) collective-permute-start(f32[64,128]{1,0:T(8,128)S(1)} %get-tuple-element.23), channel_id=1, source_target_pairs={{0,1},{1,0},{2,3},{3,2},{4,5},{5,4},{6,7},{7,6},{8,9},{9,8},{10,11... | collective-permute-start | bytes 98312 | tf_op jit(solution)/shard_map/ppermute | solution.py:530
  25.9 6.3 %collective-permute-start.6 = (f32[72,128]{1,0:T(8,128)S(1)}, f32[72,128]{1,0:T(8,128)S(1)}, u32[]{:S(2)}, u32[]{:S(2)}) collective-permute-start(f32[72,128]{1,0:T(8,128)S(1)} %pad_maximum_fusion), channel_id=1, source_target_pairs={{0,4},{4,0},{8,12},{12,8},{1,5},{5,1},{9,13},{13,9},{2,6},{6,2},{1... | collective-permute-start | bytes 110600 | tf_op jit(solution)/shard_map/ppermute | solution.py:530
  26.4 4.8 %collective-permute-start.7 = (f32[64,128]{1,0:T(8,128)S(1)}, f32[64,128]{1,0:T(8,128)S(1)}, u32[]{:S(2)}, u32[]{:S(2)}) collective-permute-start(f32[64,128]{1,0:T(8,128)S(1)} %add.8.sent), channel_id=1, source_target_pairs={{0,6},{2,4},{4,2},{6,0},{8,14},{10,12},{12,10},{14,8},{1,7},{3,5},... | collective-permute-start | bytes 98312 | tf_op jit(solution)/shard_map/ppermute | solution.py:563
  28.2 3.9 %collective-permute-start.5 = (f32[64,128]{1,0:T(8,128)S(1)}, f32[64,128]{1,0:T(8,128)S(1)}, u32[]{:S(2)}, u32[]{:S(2)}) collective-permute-start(f32[64,128]{1,0:T(8,128)S(1)} %add.8.sent), channel_id=1, source_target_pairs={{0,2},{2,0},{1,3},{3,1},{4,6},{6,4},{5,7},{7,5},{8,10},{10,8},{9,1... | collective-permute-start | bytes 98312 | tf_op jit(solution)/shard_map/ppermute | solution.py:530
